TPU v7x, 32 devices: a whole 2x2x4 slice. The times are simulated.
32 devices in a mesh: blk: 8 (over y, x, core), head: 4 (over z).
Axes of the slice: x: 2, y: 2, z: 4, core: 2. Of those that a mesh axis runs over, the one named last changes fastest.
Arguments:
- tokens: bfloat16 [4096, 1024], P(('blk', 'head')), may hold values from -6 to 6
- out_grad: bfloat16 [4096, 1024], P(('blk', 'head')), may hold values from -6 to 6
- ln_gain: bfloat16 [1024], P(('blk', 'head')), may hold values from 0.5 to 1.5
- w_query: bfloat16 [1024, 512], P(('blk', 'head')), may hold values from -0.25 to 0.25
- w_key: bfloat16 [1024, 512], P(('blk', 'head')), may hold values from -0.25 to 0.25
- w_value: bfloat16 [1024, 2560], P(('blk', 'head')), may hold values from -0.1875 to 0.1875
- w_output: bfloat16 [2560, 1024], P(('blk', 'head')), may hold values from -3 to 3
- route_value: bfloat16 [1024, 20], P(('blk', 'head')), may hold values from -0.1875 to 0.1875
- route_output: bfloat16 [1024, 20], P(('blk', 'head')), may hold values from -0.1875 to 0.1875
- route_expert: bfloat16 [1024, 256], P(None, ('blk', 'head')), may hold values from -0.09375 to 0.09375
- w_up: bfloat16 [1024, 32768], P(None, ('blk', 'head')), may hold values from -0.1875 to 0.1875
- w_down: bfloat16 [32768, 1024], P(('blk', 'head')), may hold values from -0.5 to 0.5
- value_ids: int32 [4096, 4, 2], P(('blk', 'head')), may hold values from 0 to 4, all different within a row
- output_ids: int32 [4096, 4, 2], P(('blk', 'head')), may hold values from 0 to 4, all different within a row
- expert_ids: int32 [4096, 16], P(('blk', 'head')), may hold values from 0 to 255, all different within a row; in each aligned block of 128 rows (0 to 127, 128 to 255, ...) at most 10 rows name the same one
Outputs:
- layer_out: float32 [4096, 1024], P(('blk', 'head'))
- grad_tokens: float32 [4096, 1024], P(('blk', 'head'))
- grad_ln_gain: float32 [1024], P(('blk', 'head'))
- grad_w_query: float32 [1024, 512], P(('blk', 'head'))
- grad_w_key: float32 [1024, 512], P(('blk', 'head'))
- grad_w_value: float32 [1024, 2560], P(('blk', 'head'))
- grad_w_output: float32 [2560, 1024], P(('blk', 'head'))
- grad_route_value: float32 [1024, 20], P(('blk', 'head'))
- grad_route_output: float32 [1024, 20], P(('blk', 'head'))
- grad_route_expert: float32 [1024, 256], P(None, ('blk', 'head'))
- grad_w_up: float32 [1024, 32768], P(None, ('blk', 'head'))
- grad_w_down: float32 [32768, 1024], P(('blk', 'head'))
Inputs may be any that keep to these rules, and one draw needn't show every extreme that they name: `expert_ids`: in the 128 tokens of each device no expert is named more than 10 times; each token names 16 different experts. `value_ids`: each token names 2 different value experts in each head. `output_ids`: each token names 2 different output experts in each head.
All inputs are finite; a program needn't handle non-finite values.
Results may differ from a plain program's by a relative error of at most 0.02.
Values may be sent and summed in bfloat16 or wider, within the bound.
No kernel may reach another device: no remote copies, remote signals or barrier semaphores. Data moves between devices by JAX's collectives and lax.ppermute only.
A program may use at most 192 MiB of HBM per device.

v0:
```python
import jax
import jax.numpy as jnp
from jax import lax
from jax.sharding import PartitionSpec as P

EXPERTS = 256
ATT_BLOCK = 256
CAPACITY = 10


ln_eps = 1e-05
rope_base = 10000.0


def rotate(values, places, sign_value):
    half_size = values.shape[-1] // 2
    frequency = rope_base ** (-jnp.arange(half_size, dtype=jnp.float32) / half_size)
    angles = places.astype(jnp.float32)[:, None] * frequency[None, :]
    cosine = jnp.cos(angles)[:, None, :]
    sine_part = sign_value * jnp.sin(angles)[:, None, :]
    first_half = values[..., :half_size]
    second_half = values[..., half_size:]
    return jnp.concatenate(
        [
            first_half * cosine - second_half * sine_part,
            second_half * cosine + first_half * sine_part,
        ],
        axis=-1,
    )


def unchanged(running):
    return running


def on_device(
    tokens,
    out_grad,
    ln_gain,
    w_query,
    w_key,
    w_value,
    w_output,
    route_value,
    route_output,
    route_expert,
    w_up,
    w_down,
    value_ids,
    output_ids,
    expert_ids,
):
    gain_full, query_full, key_full, value_full, output_full, value_router, output_router = (
        lax.all_gather(ln_gain, ("blk", "head"), axis=0, tiled=True),
        lax.all_gather(w_query, ("blk", "head"), axis=0, tiled=True),
        lax.all_gather(w_key, ("blk", "head"), axis=0, tiled=True),
        lax.all_gather(w_value, ("blk", "head"), axis=0, tiled=True),
        lax.all_gather(w_output, ("blk", "head"), axis=0, tiled=True),
        lax.all_gather(route_value, ("blk", "head"), axis=0, tiled=True),
        lax.all_gather(route_output, ("blk", "head"), axis=0, tiled=True),
    )
    tok_rows = tokens.shape[0]
    model_width = tokens.shape[1]
    head_count = value_ids.shape[1]
    local_experts = route_expert.shape[1]
    unit_count = w_up.shape[1] // local_experts
    att_count = value_router.shape[1] // head_count
    head_size = query_full.shape[1] // head_count
    top_count = expert_ids.shape[1]
    groups = lax.axis_size("head")
    all_devices = lax.axis_size(("blk", "head"))
    local_heads = head_count // groups
    span_rows = tok_rows * groups
    blk_index = lax.axis_index("blk")
    token_places = (blk_index * groups + lax.axis_index("head")) * tok_rows + jnp.arange(tok_rows)
    query_places = blk_index * span_rows + jnp.arange(span_rows)
    last_block = (blk_index * span_rows + span_rows - 1) // ATT_BLOCK
    score_scale = head_size ** (-0.5)
    inputs = tokens.astype(jnp.float32)
    centre = jnp.mean(inputs, -1, keepdims=True)
    shifted = inputs - centre
    inv_std = lax.rsqrt(jnp.mean(shifted * shifted, -1, keepdims=True) + ln_eps)
    normal = shifted * inv_std
    normed = (normal * gain_full).astype(jnp.bfloat16)
    query_pre = jnp.dot(normed, query_full, preferred_element_type=jnp.float32).reshape(
        tok_rows, head_count, head_size
    )
    key_pre = jnp.dot(normed, key_full, preferred_element_type=jnp.float32).reshape(
        tok_rows, head_count, head_size
    )
    query_low = rotate(query_pre, token_places, 1.0).astype(jnp.bfloat16)
    key_low = rotate(key_pre, token_places, 1.0).astype(jnp.bfloat16)
    value_gate = jax.nn.sigmoid(
        jnp.dot(tokens, value_router, preferred_element_type=jnp.float32)
    ).reshape(tok_rows, head_count, att_count)
    value_hot = jnp.sum((value_ids[..., None] == jnp.arange(att_count)).astype(jnp.float32), 2)
    value_weight = value_hot * value_gate
    expert_values = jnp.dot(tokens, value_full, preferred_element_type=jnp.float32).reshape(
        tok_rows, head_count, att_count, head_size
    )
    value_low = jnp.einsum("the,thed->thd", value_weight, expert_values).astype(jnp.bfloat16)
    head_q, head_k, head_v = (
        lax.all_to_all(query_low, "head", split_axis=1, concat_axis=0, tiled=True),
        lax.all_to_all(key_low, "head", split_axis=1, concat_axis=0, tiled=True),
        lax.all_to_all(value_low, "head", split_axis=1, concat_axis=0, tiled=True),
    )

    def sub_rows(length):
        factor = 4
        while length % (span_rows * factor) != 0:
            factor = factor // 2
        return span_rows * factor

    def masked_scores(key_rows, offset, step_rows):
        raw_scores = (
            jnp.einsum("qhd,khd->hqk", head_q, key_rows, preferred_element_type=jnp.float32)
            * score_scale
        )
        allowed = ((offset + jnp.arange(step_rows)) // ATT_BLOCK)[None, :] <= (
            query_places // ATT_BLOCK
        )[:, None]
        return jnp.where(allowed[None], raw_scores, -jnp.inf)

    init_top = jnp.full((local_heads, span_rows), -1e30, jnp.float32)
    init_total = jnp.zeros((local_heads, span_rows), jnp.float32)
    init_acc = jnp.zeros((span_rows, local_heads, head_size), jnp.float32)
    shard_piece = lax.all_gather(head_k, "blk", axis=0, tiled=True)
    stats_step_rows = sub_rows(shard_piece.shape[0])
    block_count = shard_piece.shape[0] // stats_step_rows
    key_blocks = shard_piece.reshape(block_count, stats_step_rows, local_heads, head_size)
    offsets = stats_step_rows * jnp.arange(block_count)

    def stats_advance(running, element):
        key_rows, offset = element

        def stats_compute(current):
            top_old, total_old = current
            masked = masked_scores(key_rows, offset, stats_step_rows)
            top_new = jnp.maximum(top_old, jnp.max(masked, -1))
            total_new = total_old * jnp.exp(top_old - top_new) + jnp.sum(
                jnp.exp(masked - top_new[..., None]), -1
            )
            return (top_new, total_new)

        return (
            lax.cond(offset // ATT_BLOCK <= last_block, stats_compute, unchanged, running),
            None,
        )

    result, unused = lax.scan(stats_advance, (init_top, init_total), (key_blocks, offsets))
    top_all, total_all = result
    log_total = top_all + jnp.log(total_all)
    key_part = lax.all_gather(head_k, "blk", axis=0, tiled=True)
    value_part = lax.all_gather(head_v, "blk", axis=0, tiled=True)
    values_step_rows = sub_rows(key_part.shape[0])
    block_count = key_part.shape[0] // values_step_rows
    key_blocks = key_part.reshape(block_count, values_step_rows, local_heads, head_size)
    value_blocks = value_part.reshape(block_count, values_step_rows, local_heads, head_size)
    offsets = values_step_rows * jnp.arange(block_count)

    def values_advance(running, element):
        key_rows, value_rows, offset = element

        def values_compute(current):
            masked = masked_scores(key_rows, offset, values_step_rows)
            weights = jnp.exp(masked - log_total[..., None]).astype(jnp.bfloat16)
            return current + jnp.einsum(
                "hqk,khd->qhd", weights, value_rows, preferred_element_type=jnp.float32
            )

        return (
            lax.cond(offset // ATT_BLOCK <= last_block, values_compute, unchanged, running),
            None,
        )

    result, unused = lax.scan(values_advance, init_acc, (key_blocks, value_blocks, offsets))
    attention_low = result.astype(jnp.bfloat16)
    head_out = lax.all_to_all(attention_low, "head", split_axis=0, concat_axis=1, tiled=True)
    output_gate = jax.nn.sigmoid(
        jnp.dot(tokens, output_router, preferred_element_type=jnp.float32)
    ).reshape(tok_rows, head_count, att_count)
    output_hot = jnp.sum((output_ids[..., None] == jnp.arange(att_count)).astype(jnp.float32), 2)
    output_weight = output_hot * output_gate
    mixed_heads = (
        (output_weight[..., None] * head_out[:, :, None, :].astype(jnp.float32))
        .reshape(tok_rows, head_count * att_count * head_size)
        .astype(jnp.bfloat16)
    )
    middle = inputs + jnp.dot(mixed_heads, output_full, preferred_element_type=jnp.float32)
    middle_low = middle.astype(jnp.bfloat16)
    pair_expert = expert_ids.reshape(-1)
    pair_token = jnp.arange(tok_rows * top_count) // top_count
    pair_hot = (pair_expert[:, None] == jnp.arange(EXPERTS)[None, :]).astype(jnp.int32)
    pair_rank = jnp.sum((jnp.cumsum(pair_hot, 0) - pair_hot) * pair_hot, 1)
    pair_slot = pair_expert * CAPACITY + pair_rank
    slot_total = all_devices * local_experts * CAPACITY
    send_rows = (
        jnp.zeros((slot_total, model_width), jnp.bfloat16)
        .at[pair_slot]
        .set(middle_low[pair_token])
        .reshape(all_devices, local_experts, CAPACITY, model_width)
    )
    send_grads = (
        jnp.zeros((slot_total, model_width), jnp.bfloat16)
        .at[pair_slot]
        .set(out_grad[pair_token])
        .reshape(all_devices, local_experts, CAPACITY, model_width)
    )
    got_rows, got_grads = (
        lax.all_to_all(send_rows, ("blk", "head"), split_axis=0, concat_axis=0, tiled=True),
        lax.all_to_all(send_grads, ("blk", "head"), split_axis=0, concat_axis=0, tiled=True),
    )
    up_table = w_up.reshape(model_width, local_experts, unit_count)
    down_table = w_down.reshape(local_experts, unit_count, model_width)
    slot_gate = jax.nn.sigmoid(
        jnp.einsum("secd,de->sec", got_rows, route_expert, preferred_element_type=jnp.float32)
    )
    hidden_pre = jnp.einsum(
        "secd,def->secf", got_rows, up_table, preferred_element_type=jnp.float32
    )
    pre_sigmoid = jax.nn.sigmoid(hidden_pre)
    hidden_act = hidden_pre * pre_sigmoid
    act_slope = pre_sigmoid * (1.0 + hidden_pre * (1.0 - pre_sigmoid))
    hidden = (hidden_act * slot_gate[..., None]).astype(jnp.bfloat16)
    slot_out = jnp.einsum("secf,efd->secd", hidden, down_table, preferred_element_type=jnp.float32)
    grad_down = jnp.einsum(
        "secf,secd->efd", hidden, got_grads, preferred_element_type=jnp.float32
    ).reshape(local_experts * unit_count, model_width)
    grad_hidden = jnp.einsum(
        "secd,efd->secf", got_grads, down_table, preferred_element_type=jnp.float32
    )
    slot_dgate = jnp.sum(grad_hidden * hidden_act, -1)
    grad_pre = (grad_hidden * slot_gate[..., None] * act_slope).astype(jnp.bfloat16)
    grad_up = jnp.einsum(
        "secd,secf->def", got_rows, grad_pre, preferred_element_type=jnp.float32
    ).reshape(model_width, local_experts * unit_count)
    router_grad = (slot_dgate * slot_gate * (1.0 - slot_gate)).astype(jnp.bfloat16)
    grad_expert_router = jnp.einsum(
        "secd,sec->de", got_rows, router_grad, preferred_element_type=jnp.float32
    )
    slot_dinput = jnp.einsum(
        "secf,def->secd", grad_pre, up_table, preferred_element_type=jnp.float32
    ) + jnp.einsum("sec,de->secd", router_grad, route_expert, preferred_element_type=jnp.float32)
    back_out, back_dinput = (
        lax.all_to_all(
            slot_out.astype(jnp.bfloat16), ("blk", "head"), split_axis=0, concat_axis=0, tiled=True
        ).astype(slot_out.dtype),
        lax.all_to_all(
            slot_dinput.astype(jnp.bfloat16),
            ("blk", "head"),
            split_axis=0,
            concat_axis=0,
            tiled=True,
        ).astype(slot_dinput.dtype),
    )
    layer_out = middle + jnp.sum(
        back_out.reshape(slot_total, model_width)[pair_slot].reshape(
            tok_rows, top_count, model_width
        ),
        1,
    )
    grad_middle = out_grad.astype(jnp.float32) + jnp.sum(
        back_dinput.reshape(slot_total, model_width)[pair_slot].reshape(
            tok_rows, top_count, model_width
        ),
        1,
    )
    gain_full, query_full, key_full, value_full, output_full, value_router, output_router = (
        lax.all_gather(ln_gain, ("blk", "head"), axis=0, tiled=True),
        lax.all_gather(w_query, ("blk", "head"), axis=0, tiled=True),
        lax.all_gather(w_key, ("blk", "head"), axis=0, tiled=True),
        lax.all_gather(w_value, ("blk", "head"), axis=0, tiled=True),
        lax.all_gather(w_output, ("blk", "head"), axis=0, tiled=True),
        lax.all_gather(route_value, ("blk", "head"), axis=0, tiled=True),
        lax.all_gather(route_output, ("blk", "head"), axis=0, tiled=True),
    )
    branch_grad = grad_middle.astype(jnp.bfloat16)
    grad_output = jnp.einsum(
        "tk,td->kd", mixed_heads, branch_grad, preferred_element_type=jnp.float32
    )
    grad_mixed = jnp.einsum(
        "td,kd->tk", branch_grad, output_full, preferred_element_type=jnp.float32
    ).reshape(tok_rows, head_count, att_count, head_size)
    grad_head_out = jnp.einsum("thed,the->thd", grad_mixed, output_weight).astype(jnp.bfloat16)
    grad_oweight = jnp.einsum("thed,thd->the", grad_mixed, head_out.astype(jnp.float32))
    output_lgrad = (
        (grad_oweight * output_hot * output_gate * (1.0 - output_gate))
        .reshape(tok_rows, head_count * att_count)
        .astype(jnp.bfloat16)
    )
    grad_output_router = jnp.einsum(
        "td,tk->dk", tokens, output_lgrad, preferred_element_type=jnp.float32
    )
    grad_input = grad_middle + jnp.einsum(
        "tk,dk->td", output_lgrad, output_router, preferred_element_type=jnp.float32
    )
    head_grad = lax.all_to_all(grad_head_out, "head", split_axis=1, concat_axis=0, tiled=True)
    row_delta = jnp.einsum("qhd,qhd->hq", head_grad.astype(jnp.float32), result)
    whole_keys, whole_values = (
        lax.all_gather(head_k, "blk", axis=0, tiled=True),
        lax.all_gather(head_v, "blk", axis=0, tiled=True),
    )
    whole_rows = whole_keys.shape[0]
    step_rows = sub_rows(whole_rows)
    block_total = whole_rows // step_rows
    key_blocks = whole_keys.reshape(block_total, step_rows, local_heads, head_size)
    value_blocks = whole_values.reshape(block_total, step_rows, local_heads, head_size)
    offsets = step_rows * jnp.arange(block_total)
    zero_rows = jnp.zeros((span_rows, local_heads, head_size), jnp.float32)

    def backward_step(query_grad, element):
        key_rows, value_rows, offset = element

        def backward_compute(dummy_arg):
            masked = masked_scores(key_rows, offset, step_rows)
            prob_full = jnp.exp(masked - log_total[..., None])
            prob_low = prob_full.astype(jnp.bfloat16)
            value_term = jnp.einsum(
                "hqk,qhd->khd", prob_low, head_grad, preferred_element_type=jnp.float32
            )
            prob_grad = jnp.einsum(
                "qhd,khd->hqk", head_grad, value_rows, preferred_element_type=jnp.float32
            )
            score_grad = (prob_full * (prob_grad - row_delta[..., None]) * score_scale).astype(
                jnp.bfloat16
            )
            key_term = jnp.einsum(
                "hqk,qhd->khd", score_grad, head_q, preferred_element_type=jnp.float32
            )
            query_term = jnp.einsum(
                "hqk,khd->qhd", score_grad, key_rows, preferred_element_type=jnp.float32
            )
            return (query_term, jnp.stack([key_term, value_term], 1))

        def skipped(dummy_arg):
            return (
                jnp.zeros((span_rows, local_heads, head_size), jnp.float32),
                jnp.zeros((step_rows, 2, local_heads, head_size), jnp.float32),
            )

        query_term, pair_terms = lax.cond(
            offset // ATT_BLOCK <= last_block, backward_compute, skipped, 0
        )
        return (query_grad + query_term, pair_terms)

    query_grad, kv_terms = lax.scan(backward_step, zero_rows, (key_blocks, value_blocks, offsets))
    own_terms = lax.psum_scatter(
        kv_terms.reshape(whole_rows, 2, local_heads, head_size).astype(jnp.bfloat16),
        "blk",
        scatter_dimension=0,
        tiled=True,
    ).astype(jnp.float32)
    key_total = own_terms[:, 0]
    value_total = own_terms[:, 1]
    query_back = rotate(query_grad, query_places, -1.0).astype(jnp.bfloat16)
    key_back = rotate(key_total, query_places, -1.0).astype(jnp.bfloat16)
    value_back = value_total.astype(jnp.bfloat16)
    token_q, token_k, token_v = (
        lax.all_to_all(query_back, "head", split_axis=0, concat_axis=1, tiled=True),
        lax.all_to_all(key_back, "head", split_axis=0, concat_axis=1, tiled=True),
        lax.all_to_all(value_back, "head", split_axis=0, concat_axis=1, tiled=True),
    )
    query_flat = token_q.reshape(tok_rows, head_count * head_size)
    key_flat = token_k.reshape(tok_rows, head_count * head_size)
    grad_query = jnp.einsum("td,tk->dk", normed, query_flat, preferred_element_type=jnp.float32)
    grad_key = jnp.einsum("td,tk->dk", normed, key_flat, preferred_element_type=jnp.float32)
    grad_normed = jnp.einsum(
        "tk,dk->td", query_flat, query_full, preferred_element_type=jnp.float32
    ) + jnp.einsum("tk,dk->td", key_flat, key_full, preferred_element_type=jnp.float32)
    grad_expert_values = (
        (value_weight[..., None] * token_v[:, :, None, :].astype(jnp.float32))
        .reshape(tok_rows, head_count * att_count * head_size)
        .astype(jnp.bfloat16)
    )
    grad_value = jnp.einsum(
        "td,tk->dk", tokens, grad_expert_values, preferred_element_type=jnp.float32
    )
    grad_input = grad_input + jnp.einsum(
        "tk,dk->td", grad_expert_values, value_full, preferred_element_type=jnp.float32
    )
    grad_vweight = jnp.einsum("thd,thed->the", token_v.astype(jnp.float32), expert_values)
    value_lgrad = (
        (grad_vweight * value_hot * value_gate * (1.0 - value_gate))
        .reshape(tok_rows, head_count * att_count)
        .astype(jnp.bfloat16)
    )
    grad_value_router = jnp.einsum(
        "td,tk->dk", tokens, value_lgrad, preferred_element_type=jnp.float32
    )
    grad_input = grad_input + jnp.einsum(
        "tk,dk->td", value_lgrad, value_router, preferred_element_type=jnp.float32
    )
    grad_gain = jnp.sum(grad_normed * normal, 0)
    grad_normal = grad_normed * gain_full
    grad_input = grad_input + inv_std * (
        grad_normal
        - jnp.mean(grad_normal, -1, keepdims=True)
        - normal * jnp.mean(grad_normal * normal, -1, keepdims=True)
    )
    summed = (
        lax.psum_scatter(grad_gain, ("blk", "head"), scatter_dimension=0, tiled=True),
        lax.psum_scatter(grad_query, ("blk", "head"), scatter_dimension=0, tiled=True),
        lax.psum_scatter(grad_key, ("blk", "head"), scatter_dimension=0, tiled=True),
        lax.psum_scatter(grad_value, ("blk", "head"), scatter_dimension=0, tiled=True),
        lax.psum_scatter(grad_output, ("blk", "head"), scatter_dimension=0, tiled=True),
        lax.psum_scatter(grad_value_router, ("blk", "head"), scatter_dimension=0, tiled=True),
        lax.psum_scatter(grad_output_router, ("blk", "head"), scatter_dimension=0, tiled=True),
    )
    return (
        layer_out,
        grad_input,
        summed[0],
        summed[1],
        summed[2],
        summed[3],
        summed[4],
        summed[5],
        summed[6],
        grad_expert_router,
        grad_up,
        grad_down,
    )


def solution(mesh):
    return jax.shard_map(
        on_device,
        mesh=mesh,
        in_specs=(
            P(("blk", "head"), None),
            P(("blk", "head"), None),
            P(("blk", "head")),
            P(("blk", "head"), None),
            P(("blk", "head"), None),
            P(("blk", "head"), None),
            P(("blk", "head"), None),
            P(("blk", "head"), None),
            P(("blk", "head"), None),
            P(None, ("blk", "head")),
            P(None, ("blk", "head")),
            P(("blk", "head"), None),
            P(("blk", "head"), None, None),
            P(("blk", "head"), None, None),
            P(("blk", "head"), None),
        ),
        out_specs=(
            P(("blk", "head"), None),
            P(("blk", "head"), None),
            P(("blk", "head")),
            P(("blk", "head"), None),
            P(("blk", "head"), None),
            P(("blk", "head"), None),
            P(("blk", "head"), None),
            P(("blk", "head"), None),
            P(("blk", "head"), None),
            P(None, ("blk", "head")),
            P(None, ("blk", "head")),
            P(("blk", "head"), None),
        ),
        check_vma=False,
    )
```

profile of v0, /device:TPU:0, one launch (start us, length us, event | category | flops | bytes accessed | tf_op | source)
XLA Modules:
  0.0 2052.4 jit_solution(1988802702905318208)
XLA Ops:
  10.3 42.0 %all-reduce = bf16[1024]{0:T(1024)(128)(2,1)S(1)} all-reduce(bf16[1024]{0:T(1024)(128)(2,1)S(1)} %dynamic-update-slice), channel_id=1, replica_groups=mesh['blk'=8,'head'=4] {'blk','head'}, use_global_device_ids=true, to_apply=%add | all-reduce | flops 1024 | bytes 4096
  55.0 12.6 all-gather.13.cloned.1.call-done
  69.4 53.9 %all-gather.17.cloned.1.call-done = bf16[1024,512]{1,0:T(8,128)(2,1)} async-done(((bf16[32,512]{1,0:T(8,128)(2,1)}), bf16[1024,512]{1,0:T(8,128)(2,1)}) %all-gather.17.cloned.1.call-update) | async-done | bytes 1048592 | tf_op jit(solution)/shard_map/all_gather | solution.py:55
  125.7 9.8 all_to_all.152
  135.6 67.4 %all-gather.1 = bf16[32,32,20]{1,2,0:T(8,128)(2,1)S(1)} all-gather(bf16[1,32,20]{1,2,0:T(8,128)(2,1)S(1)} %bitcast.364), channel_id=1, replica_groups=mesh['blk'=8,'head'=4] {'blk','head'}, dimensions={0}, use_global_device_ids=true | all-gather | bytes 42240 | tf_op jit(solution)/shard_map/all_gather | solution.py:59
  209.5 9.0 all_to_all.153
  232.4 5.9 all-to-all-done.2
  238.2 11.4 while.46
  249.8 11.1 while.47
  266.7 27.8 %scatter_custom_fusion.1 = bf16[2560,1024]{1,0:T(8,128)(2,1)} fusion(s32[2048]{0:T(1024)S(1)} %bitcast.358, bf16[128,1024]{1,0:T(8,128)(2,1)S(1)} %copy-done.15, s32[2048]{0:T(1024)S(1)} %broadcast_clamp_fusion.1, bf16[]{:T(256)} %constant.337.clone.1), kind=kCustom, calls=%fused_computation.117 | custom fusion | bytes 5242882 | tf_op jit(solution)/shard_map/scatter | solution.py:206
  294.5 10.5 reshape.675
  305.0 11.7 copy.280
  316.7 11.8 all-to-all-start.6
  328.5 177.3 %all-gather = bf16[32,32,20]{1,2,0:T(8,128)(2,1)S(1)} all-gather(bf16[1,32,20]{1,2,0:T(8,128)(2,1)S(1)} %bitcast.365), channel_id=1, replica_groups=mesh['blk'=8,'head'=4] {'blk','head'}, dimensions={0}, use_global_device_ids=true | all-gather | bytes 42240 | tf_op jit(solution)/shard_map/all_gather | solution.py:60
  513.5 34.3 %scatter_custom_fusion = bf16[2560,1024]{1,0:T(8,128)(2,1)} fusion(s32[2048]{0:T(1024)S(1)} %bitcast.359, bf16[128,1024]{1,0:T(8,128)(2,1)} %get-tuple-element.1026, s32[2048]{0:T(1024)S(1)} %broadcast_clamp_fusion.1, bf16[]{:T(256)} %constant.337.clone.1), kind=kCustom, calls=%fused_computation.119 | custom fusion | bytes 5243392 | tf_op jit(solution)/shard_map/scatter | solution.py:200
  547.8 10.5 reshape.669
  558.3 11.5 copy.275
  577.4 6.7 fusion.93
  584.1 104.2 %all-to-all-done.4 = bf16[32,8,10,1024]{3,1,2,0:T(8,128)(2,1)} async-done(((bf16[32,8,10,1024]{3,1,2,0:T(8,128)(2,1)}), bf16[32,8,10,1024]{3,1,2,0:T(8,128)(2,1)}, u32[]{:S(2)}, u32[]{:S(2)}) %all-to-all-start.4) | async-done | bytes 5242912 | tf_op jit(solution)/shard_map/all_to_all | solution.py:210
  688.3 6.4 fusion.76
  697.0 8.2 multiply_convert_fusion.1
  713.2 6.4 all-to-all-start.7
  719.7 114.5 %all-to-all-done.7 = bf16[32,8,10,1024]{3,1,2,0:T(8,128)(2,1)} async-done(((bf16[32,8,10,1024]{3,1,2,0:T(8,128)(2,1)}), bf16[32,8,10,1024]{3,1,2,0:T(8,128)(2,1)}, u32[]{:S(2)}, u32[]{:S(2)}) %all-to-all-start.7) | async-done | bytes 5242912 | tf_op jit(solution)/shard_map/all_to_all | solution.py:248
  834.1 17.5 copy.284
  851.7 14.8 reshape.689
  866.5 15.9 gather_fusion.1
  899.0 6.5 all-to-all-done.8
  906.3 19.3 while.48
  910.1 6.0 conditional.11
  931.3 44.5 %reduce-scatter.14.cloned.1.call-done = bf16[512,2,1,128]{0,3,2,1:T(8,128)(2,1)} async-done(((bf16[4096,2,1,128]{0,3,2,1:T(8,128)(2,1)}), bf16[512,2,1,128]{0,3,2,1:T(8,128)(2,1)}) %reduce-scatter.14.cloned.1.call-update) | async-done | bytes 262160 | tf_op jit(solution)/shard_map/reduce_scatter | solution.py:347
  1011.7 10.0 all_to_all.154
  1030.0 6.6 fusion.150
  1038.4 5.5 convolution_bitcast_fusion.3
  1044.0 11.5 copy.350
  1068.4 8.2 fusion.74
  1077.2 10.7 fusion.72
  1088.0 5.5 copy.306
  1093.5 11.3 fusion.64
  1104.8 83.0 %all-to-all-done.5 = bf16[32,8,10,1024]{3,1,2,0:T(8,128)(2,1)} async-done(((bf16[32,8,10,1024]{3,1,2,0:T(8,128)(2,1)}), bf16[32,8,10,1024]{3,1,2,0:T(8,128)(2,1)}, u32[]{:S(2)}, u32[]{:S(2)}) %all-to-all-start.5) | async-done | bytes 5242912 | tf_op jit(solution)/shard_map/all_to_all | solution.py:245
  1187.8 17.8 copy.279
  1205.6 14.9 reshape.687
  1220.5 15.7 gather_fusion
  1248.2 43.1 %all-reduce.1 = f32[1024]{0:T(1024)S(1)} all-reduce(f32[1024]{0:T(1024)S(1)} %get-tuple-element.939), channel_id=3, replica_groups=mesh['blk'=8,'head'=4] {'blk','head'}, use_global_device_ids=true, to_apply=%region_30.31.clone | all-reduce | flops 1024 | bytes 8192
  1297.9 11.6 reduce-scatter.24.cloned.1.call-done
  1310.9 136.0 %reduce-scatter.18.cloned.1.call-done = f32[32,512]{1,0:T(8,128)} async-done(((f32[1024,512]{1,0:T(8,128)}), f32[32,512]{1,0:T(8,128)}) %reduce-scatter.18.cloned.1.call-update) | async-done | bytes 65552 | tf_op jit(solution)/shard_map/reduce_scatter | solution.py:403
  1446.9 139.0 %reduce-scatter.16.cloned.1.call-done = f32[32,512]{1,0:T(8,128)} async-done(((f32[1024,512]{1,0:T(8,128)}), f32[32,512]{1,0:T(8,128)}) %reduce-scatter.16.cloned.1.call-update) | async-done | bytes 65552 | tf_op jit(solution)/shard_map/reduce_scatter | solution.py:402
  1585.8 229.9 %reduce-scatter.20.cloned.1.call-done = f32[80,1024]{1,0:T(8,128)} async-done(((f32[2560,1024]{1,0:T(8,128)}), f32[80,1024]{1,0:T(8,128)}) %reduce-scatter.20.cloned.1.call-update) | async-done | bytes 327696 | tf_op jit(solution)/shard_map/reduce_scatter | solution.py:405
  1815.8 229.7 %reduce-scatter.22.cloned.1.call-done = f32[32,2560]{1,0:T(8,128)} async-done(((f32[1024,2560]{1,0:T(8,128)}), f32[32,2560]{1,0:T(8,128)}) %reduce-scatter.22.cloned.1.call-update) | async-done | bytes 327696
  (343 shorter events, 196.4 us)
Async XLA Ops:
  7.2 570.2 %copy-start = (bf16[1024,1024]{1,0:T(8,128)(2,1)S(1)}, bf16[1024,1024]{1,0:T(8,128)(2,1)}, u32[]{:S(2)}) copy-start(bf16[1024,1024]{1,0:T(8,128)(2,1)} %param.38) | copy-start | bytes 6291460
  7.2 60.4 %all-gather.13.cloned.1.call-start = ((), (), s32[]{:S(2)}) async-start(), calls=%async_computation.21 | async-start | bytes 1081344 | tf_op jit(solution)/shard_map/all_gather | solution.py:56
  7.9 115.3 %all-gather.17.cloned.1.call-start = ((), (), s32[]{:S(2)}) async-start(), calls=%async_computation.23 | async-start | bytes 1081344 | tf_op jit(solution)/shard_map/all_gather | solution.py:55
  8.7 194.8 %all-gather.9.cloned.1.call-start = ((), (), s32[]{:S(2)}) async-start(), calls=%async_computation.19 | async-start | bytes 5406720 | tf_op jit(solution)/shard_map/all_gather | solution.py:57
  9.4 228.8 %all-gather.15.cloned.1.call-start = ((), (), s32[]{:S(2)}) async-start(), calls=%async_computation.22 | async-start | bytes 1179648 | tf_op jit(solution)/shard_map/all_gather | solution.py:153
  52.3 72.6 %copy-start.30 = (f32[1024]{0:T(1024)}, f32[1024]{0:T(1024)S(1)}, u32[]{:S(2)}) copy-start(f32[1024]{0:T(1024)S(1)} %convert_element_type.200) | copy-start | bytes 12292
  52.4 72.6 %copy-start.57 = (f32[64]{0:T(128)}, f32[64]{0:T(128)S(1)}, u32[]{:S(2)}) copy-start(f32[64]{0:T(128)S(1)} %multiply_power_fusion) | copy-start | bytes 772
  53.5 71.5 %copy-start.47 = (f32[128]{0:T(128)}, f32[128]{0:T(128)S(1)}, u32[]{:S(2)}) copy-start(f32[128]{0:T(128)S(1)} %broadcast_multiply_fusion.3) | copy-start | bytes 1540
  54.7 70.3 %copy-start.49 = (f32[128]{0:T(128)}, f32[128]{0:T(128)S(1)}, u32[]{:S(2)}) copy-start(f32[128]{0:T(128)S(1)} %add_rsqrt_fusion) | copy-start | bytes 1540
  55.0 80.5 %copy-start.52 = (bf16[32,20]{0,1:T(8,128)(2,1)S(1)}, bf16[32,20]{0,1:T(8,128)(2,1)}, u32[]{:S(2)}) copy-start(bf16[32,20]{0,1:T(8,128)(2,1)} %param.34) | copy-start | bytes 3844
  69.3 133.9 %copy-start.1 = (bf16[128,1024]{1,0:T(8,128)(2,1)S(1)}, bf16[128,1024]{1,0:T(8,128)(2,1)}, u32[]{:S(2)}) copy-start(bf16[128,1024]{1,0:T(8,128)(2,1)} %param.27) | copy-start | bytes 786436
  69.3 134.1 %copy-start.54 = (s32[128,4,2]{0,2,1:T(2,128)S(1)}, s32[128,4,2]{0,2,1:T(2,128)}, u32[]{:S(2)}) copy-start(s32[128,4,2]{0,2,1:T(2,128)} %param.39) | copy-start | bytes 12292
  135.5 114.2 %all-gather.11.cloned.1.call-start = ((), (), s32[]{:S(2)}) async-start(), calls=%async_computation.20 | async-start | bytes 1179648 | tf_op jit(solution)/shard_map/all_gather | solution.py:154
  218.5 290.5 %all-gather.19.cloned.1.call-start = ((), (), s32[]{:S(2)}) async-start(), calls=%async_computation.24 | async-start | bytes 5406720 | tf_op jit(solution)/shard_map/all_gather | solution.py:58
  229.0 9.2 all-to-all-start.2
  260.9 44.1 %copy-start.13 = (bf16[512,1,128]{2,0,1:T(8,128)(2,1)}, bf16[512,1,128]{2,0,1:T(8,128)(2,1)S(1)}, u32[]{:S(2)}) copy-start(bf16[512,1,128]{2,0,1:T(8,128)(2,1)S(1)} %get-tuple-element.1400) | copy-start | bytes 393220
  260.9 44.1 %copy-start.18 = (f32[512,1,128]{0,2,1:T(8,128)}, f32[512,1,128]{0,2,1:T(8,128)S(1)}, u32[]{:S(2)}) copy-start(f32[512,1,128]{0,2,1:T(8,128)S(1)} %get-tuple-element.583) | copy-start | bytes 786436
  260.9 44.1 %copy-start.56 = (f32[1,512]{1,0:T(1,128)}, f32[1,512]{1,0:T(1,128)S(1)}, u32[]{:S(2)}) copy-start(f32[1,512]{1,0:T(1,128)S(1)} %get-tuple-element.1427) | copy-start | bytes 6148
  263.0 53.7 %all-to-all-start.3 = ((bf16[4,2,8192]{2,1,0:T(2,128)(2,1)}), bf16[4,2,8192]{2,1,0:T(2,128)(2,1)S(1)}, u32[]{:S(2)}, u32[]{:S(2)}) async-start(bf16[4,2,8192]{2,1,0:T(2,128)(2,1)} %reshape.783), calls=%async_computation.3 | async-start | bytes 262144 | tf_op jit(solution)/shard_map/all_to_all | solution.py:178
  316.7 189.6 %copy-start.55 = (s32[128,4,2]{0,2,1:T(2,128)S(1)}, s32[128,4,2]{0,2,1:T(2,128)}, u32[]{:S(2)}) copy-start(s32[128,4,2]{0,2,1:T(2,128)} %param.40) | copy-start | bytes 12292
  316.7 253.1 %all-to-all-start.6 = ((bf16[32,8,10,1024]{3,1,2,0:T(8,128)(2,1)}), bf16[32,8,10,1024]{3,1,2,0:T(8,128)(2,1)}, u32[]{:S(2)}, u32[]{:S(2)}) async-start(bf16[32,8,10,1024]{3,1,2,0:T(8,128)(2,1)} %copy.280), calls=%async_computation.6 | async-start | bytes 10485760 | tf_op jit(solution)/shard_map/all_to_all | solution.py:211
  509.0 38.8 %copy-start.10 = (bf16[128,4,5,128]{0,3,2,1:T(8,128)(2,1)}, bf16[128,4,5,128]{0,3,2,1:T(8,128)(2,1)S(1)}, u32[]{:S(2)}) copy-start(bf16[128,4,5,128]{0,3,2,1:T(8,128)(2,1)S(1)} %multiply_convert_fusion.3) | copy-start | bytes 1966084
  569.8 118.5 %all-to-all-start.4 = ((bf16[32,8,10,1024]{3,1,2,0:T(8,128)(2,1)}), bf16[32,8,10,1024]{3,1,2,0:T(8,128)(2,1)}, u32[]{:S(2)}, u32[]{:S(2)}) async-start(bf16[32,8,10,1024]{3,1,2,0:T(8,128)(2,1)} %copy.275), calls=%async_computation.4 | async-start | bytes 10485760 | tf_op jit(solution)/shard_map/all_to_all | solution.py:210
  713.2 120.9 %all-to-all-start.7 = ((bf16[32,8,10,1024]{3,1,2,0:T(8,128)(2,1)}), bf16[32,8,10,1024]{3,1,2,0:T(8,128)(2,1)}, u32[]{:S(2)}, u32[]{:S(2)}) async-start(bf16[32,8,10,1024]{3,1,2,0:T(8,128)(2,1)} %copy.283), calls=%async_computation.7 | async-start | bytes 10485760 | tf_op jit(solution)/shard_map/all_to_all | solution.py:248
  719.6 146.9 %copy-start.39 = (s32[2048]{0:T(1024)}, s32[2048]{0:T(1024)S(1)}, u32[]{:S(2)}) copy-start(s32[2048]{0:T(1024)S(1)} %broadcast_clamp_fusion) | copy-start | bytes 24580
  887.7 17.9 copy-start.19
  894.0 11.5 all-to-all-start.8
  899.0 76.8 %reduce-scatter.14.cloned.1.call-start = ((), (), s32[]{:S(2)}) async-start(), calls=%async_computation.25 | async-start | bytes 2359296 | tf_op jit(solution)/shard_map/reduce_scatter | solution.py:347
  925.6 57.3 %copy-start.7 = (f32[512,1,128]{0,2,1:T(8,128)S(1)}, f32[512,1,128]{0,2,1:T(8,128)}, u32[]{:S(2)}) copy-start(f32[512,1,128]{0,2,1:T(8,128)} %get-tuple-element.585) | copy-start | bytes 786436
  925.6 57.3 %copy-start.58 = (f32[64]{0:T(128)S(1)}, f32[64]{0:T(128)}, u32[]{:S(2)}) copy-start(f32[64]{0:T(128)} %copy-done.57) | copy-start | bytes 772
  931.2 62.5 %copy-start.43 = (bf16[128,20]{0,1:T(8,128)(2,1)}, bf16[128,20]{0,1:T(8,128)(2,1)S(1)}, u32[]{:S(2)}) copy-start(bf16[128,20]{0,1:T(8,128)(2,1)S(1)} %convert_element_type.219) | copy-start | bytes 15364
  976.8 23.1 %copy-start.37 = (f32[128,4,5]{0,1,2:T(4,128)S(1)}, f32[128,4,5]{0,1,2:T(4,128)}, u32[]{:S(2)}) copy-start(f32[128,4,5]{0,1,2:T(4,128)} %copy-done.36) | copy-start | bytes 30724
  978.3 10.7 all-to-all-start.9
  984.1 17.8 copy-start.31
  989.0 9.2 all-to-all-start.11
  992.3 250.2 %reduce-scatter.26.cloned.1.call-start = ((), (), s32[]{:S(2)}) async-start(), calls=%async_computation.31 | async-start | bytes 540672
  993.6 316.0 %reduce-scatter.24.cloned.1.call-start = ((), (), s32[]{:S(2)}) async-start(), calls=%async_computation.30 | async-start | bytes 540672
  1000.7 26.1 %copy-start.48 = (f32[128]{0:T(128)S(1)}, f32[128]{0:T(128)}, u32[]{:S(2)}) copy-start(f32[128]{0:T(128)} %copy-done.47) | copy-start | bytes 1540
  1001.9 445.0 %reduce-scatter.18.cloned.1.call-start = ((), (), s32[]{:S(2)}) async-start(), calls=%async_computation.27 | async-start | bytes 2162688 | tf_op jit(solution)/shard_map/reduce_scatter | solution.py:403
  1004.6 25.5 %copy-start.6 = (f32[128,1024]{1,0:T(8,128)S(1)}, f32[128,1024]{1,0:T(8,128)}, u32[]{:S(2)}) copy-start(f32[128,1024]{1,0:T(8,128)} %copy-done.5) | copy-start | bytes 1572868
  1004.6 25.5 %copy-start.16 = (bf16[128,1024]{1,0:T(8,128)(2,1)S(1)}, bf16[128,1024]{1,0:T(8,128)(2,1)}, u32[]{:S(2)}) copy-start(bf16[128,1024]{1,0:T(8,128)(2,1)} %param.28) | copy-start | bytes 786436
  1004.6 581.3 %reduce-scatter.16.cloned.1.call-start = ((), (), s32[]{:S(2)}) async-start(), calls=%async_computation.26 | async-start | bytes 2162688 | tf_op jit(solution)/shard_map/reduce_scatter | solution.py:402
  1029.6 786.2 %reduce-scatter.20.cloned.1.call-start = ((), (), s32[]{:S(2)}) async-start(), calls=%async_computation.28 | async-start | bytes 10813440 | tf_op jit(solution)/shard_map/reduce_scatter | solution.py:405
  1036.7 1008.8 %reduce-scatter.22.cloned.1.call-start = ((), (), s32[]{:S(2)}) async-start(), calls=%async_computation.29 | async-start | bytes 10813440
  1064.5 123.4 %all-to-all-start.5 = ((bf16[32,8,10,1024]{3,1,2,0:T(8,128)(2,1)}), bf16[32,8,10,1024]{3,1,2,0:T(8,128)(2,1)}, u32[]{:S(2)}, u32[]{:S(2)}) async-start(bf16[32,8,10,1024]{3,1,2,0:T(8,128)(2,1)} %copy.278), calls=%async_computation.5 | async-start | bytes 10485760 | tf_op jit(solution)/shard_map/all_to_all | solution.py:245
  1245.6 50.9 %copy-start.27 = (bf16[1024,20]{0,1:T(8,128)(2,1)S(1)}, bf16[1024,20]{0,1:T(8,128)(2,1)}, u32[]{:S(2)}) copy-start(bf16[1024,20]{0,1:T(8,128)(2,1)} %copy-done.26) | copy-start | bytes 122884
  1245.6 50.9 %copy-start.44 = (bf16[128,20]{0,1:T(8,128)(2,1)S(1)}, bf16[128,20]{0,1:T(8,128)(2,1)}, u32[]{:S(2)}) copy-start(bf16[128,20]{0,1:T(8,128)(2,1)} %copy-done.43) | copy-start | bytes 15364
  1248.2 48.6 %copy-start.29 = (bf16[1024,20]{0,1:T(8,128)(2,1)S(1)}, bf16[1024,20]{0,1:T(8,128)(2,1)}, u32[]{:S(2)}) copy-start(bf16[1024,20]{0,1:T(8,128)(2,1)} %copy-done.28) | copy-start | bytes 122884
  (34 other events, 172.6 us)
Sparse Core Ops, SparseCore 0:
  11.0 56.5 all-gather.12
  70.6 52.6 all-gather.16
  126.1 64.9 all-gather.8
  192.8 22.5 all-gather.14
  218.6 22.0 all-gather.10
  243.4 66.1 all-gather.18
  929.9 45.8 reduce-scatter.13
  995.5 176.0 reduce-scatter.25
  1173.8 135.6 reduce-scatter.23
  1312.3 134.5 reduce-scatter.17
  1449.7 136.0 reduce-scatter.15
  1588.7 227.0 reduce-scatter.19
  1818.7 226.6 reduce-scatter.21
where the time goes:
time: 2070 us; the launch traced here: 2050 us
  waiting for transfers between devices  1180 us (57%)
  blocking collectives  359 us (17%)
  local copies, waits for them, and re-layouts  281 us (14%)
  matrix products  111 us (5%)
  starting transfers between devices  46.9 us (2%)
  other arithmetic  42.3 us (2%)
    unnamed x16, waiting for transfers between devices  244 us
    reduce_scatter x1, waiting for transfers between devices, on_device(): lax.psum_scatter(grad_output, ('blk', 'head'), scatter_dimension=0, tiled...  230 us
    all_gather x1, blocking collectives, on_device(): lax.all_gather(route_output, ('blk', 'head'), axis=0, tiled=True)  177 us
    reduce_scatter x1, waiting for transfers between devices, on_device(): lax.psum_scatter(grad_query, ('blk', 'head'), scatter_dimension=0, tiled=...  139 us
    reduce_scatter x1, waiting for transfers between devices, on_device(): lax.psum_scatter(grad_key, ('blk', 'head'), scatter_dimension=0, tiled=True)  136 us
    all_to_all x1, waiting for transfers between devices, on_device(): lax.all_to_all(slot_dinput.astype(jnp.bfloat16), ('blk', 'head'), split_a...  114 us
    all_to_all x1, waiting for transfers between devices, on_device(): lax.all_to_all(send_rows, ('blk', 'head'), split_axis=0, concat_axis=0, t...  104 us
    unnamed x2, blocking collectives  85.1 us
  transfers between devices with their start and end apart: 22, of which 15 were waited for; matrix products, arithmetic and copies ran while one was open for 16% of the time, Pallas kernels for 0%

commit v1 on v0

v1 whole, which is shorter than its diff:
```python
import functools

import jax
import jax.numpy as jnp
from jax import lax
from jax.experimental import pallas as pl
from jax.experimental.pallas import tpu as pltpu
from jax.sharding import PartitionSpec as P

ATT_BLOCK = 256
ln_eps = 1e-05
rope_base = 10000.0
MIB = 1 << 20
BF = jnp.bfloat16
F32 = jnp.float32


def swap(value, axis, mask):
    size = lax.axis_size(axis)
    return lax.ppermute(value, axis, [(i, i ^ mask) for i in range(size)])


def gather_blk(value, size=None):
    size = size or lax.axis_size("blk")
    pieces = []
    for mask in range(0, size, 2):
        mine = value if mask == 0 else swap(value, "blk", mask)
        pieces += [mine, swap(mine, "blk", 1)]
    return pieces


def reduce_blk(parts):
    size = len(parts)
    total = None
    for mask in [*range(2, size, 2), 0]:
        pair = parts[mask].astype(F32) + swap(parts[mask + 1], "blk", 1).astype(F32)
        if mask:
            pair = swap(pair.astype(BF), "blk", mask).astype(F32)
        total = pair if total is None else total + pair
    return total


def gather_head(value):
    size = lax.axis_size("head")
    return [value] + [swap(value, "head", mask) for mask in range(1, size)]


def rotate(values, cosine, sine):
    half = values.shape[-1] // 2
    first, second = values[..., :half], values[..., half:]
    return jnp.concatenate(
        [first * cosine - second * sine, second * cosine + first * sine], axis=-1
    )


def nt(left, right):
    return lax.dot_general(left, right, (((1,), (1,)), ((), ())), preferred_element_type=F32)


def tn(left, right):
    return lax.dot_general(left, right, (((0,), (0,)), ((), ())), preferred_element_type=F32)


def nn(left, right):
    return jnp.dot(left, right, preferred_element_type=F32)


def block_of(place, blk, head, tok_rows, span):
    return (blk * span + (head ^ (place // tok_rows)) * tok_rows + place % tok_rows) // ATT_BLOCK


def own_allowed(blk, head, tok_rows, span):
    keys = lax.broadcasted_iota(jnp.int32, (span, span), 0)
    queries = lax.broadcasted_iota(jnp.int32, (span, span), 1)
    return block_of(keys, blk, head, tok_rows, span) <= block_of(
        queries, blk, head, tok_rows, span
    )


def attend_kernel(groups, tok_rows, scale, at_ref, q_ref, *refs):
    kv_refs = refs[:groups]
    o_ref, lse_ref, top_ref, total_ref, acc_ref = refs[groups:]
    span, size = q_ref.shape
    blk, head = at_ref[0], at_ref[1]
    queries = q_ref[...]

    def advance(kv_ref, first):
        scores = nt(kv_ref[:, :size], queries) * scale
        if first:
            scores = jnp.where(own_allowed(blk, head, tok_rows, span), scores, -jnp.inf)
            top = jnp.max(scores, 0, keepdims=True)
        else:
            top = jnp.maximum(top_ref[...], jnp.max(scores, 0, keepdims=True))
        weights = jnp.exp(scores - top)
        mass = jnp.sum(weights, 0, keepdims=True)
        term = tn(kv_ref[:, size:], weights.astype(BF))
        if first:
            total_ref[...] = mass
            acc_ref[...] = term
        else:
            fade = jnp.exp(top_ref[...] - top)
            total_ref[...] = total_ref[...] * fade + mass
            acc_ref[...] = acc_ref[...] * fade + term
        top_ref[...] = top

    advance(kv_refs[0], True)
    for mask in range(1, groups):
        pl.when((blk ^ mask) < blk)(functools.partial(advance, kv_refs[mask], False))
    lse_ref[...] = top_ref[...] + jnp.log(total_ref[...])
    o_ref[...] = (acc_ref[...] / total_ref[...]).T.astype(BF)


def attend(at, queries, pieces, tok_rows, scale):
    span, size = queries.shape
    groups = len(pieces)
    vmem = pl.BlockSpec(memory_space=pltpu.VMEM)
    return pl.pallas_call(
        functools.partial(attend_kernel, groups, tok_rows, scale),
        out_shape=(
            jax.ShapeDtypeStruct((span, size), BF),
            jax.ShapeDtypeStruct((1, span), F32),
        ),
        in_specs=[pl.BlockSpec(memory_space=pltpu.SMEM)] + [vmem] * (1 + groups),
        out_specs=(vmem, vmem),
        scratch_shapes=[
            pltpu.VMEM((1, span), F32),
            pltpu.VMEM((1, span), F32),
            pltpu.VMEM((size, span), F32),
        ],
        compiler_params=pltpu.CompilerParams(vmem_limit_bytes=32 * MIB),
        cost_estimate=pl.CostEstimate(
            flops=4 * groups * span * span * size,
            bytes_accessed=(2 * groups + 2) * span * size * 2,
            transcendentals=groups * span * span,
        ),
        name="attend",
    )(at, queries, *pieces)


def attend_back_kernel(groups, tok_rows, scale, at_ref, *refs):
    kv_refs = refs[:groups]
    q_refs = refs[groups : 2 * groups]
    dout_refs = refs[2 * groups : 3 * groups]
    stat_refs = refs[3 * groups : 4 * groups]
    dq_ref, dk_ref, dv_ref, dq_acc = refs[4 * groups :]
    span, size = q_refs[0].shape
    blk, head = at_ref[0], at_ref[1]

    def terms(kv_ref, q_ref, dout_ref, stat_ref, own):
        scores = nt(kv_ref[:, :size], q_ref[...]) * scale
        if own:
            scores = jnp.where(own_allowed(blk, head, tok_rows, span), scores, -jnp.inf)
        prob = jnp.exp(scores - stat_ref[0:1, :])
        prob_grad = nt(kv_ref[:, size:], dout_ref[...])
        score_grad = prob * (prob_grad - stat_ref[1:2, :]) * scale
        return prob.astype(BF), score_grad.astype(BF)

    prob, grad = terms(kv_refs[0], q_refs[0], dout_refs[0], stat_refs[0], True)
    dq_acc[...] = tn(kv_refs[0][:, :size], grad)
    dk_ref[...] = nn(grad, q_refs[0][...])
    dv_ref[...] = nn(prob, dout_refs[0][...])

    def earlier(mask):
        prob, grad = terms(kv_refs[mask], q_refs[0], dout_refs[0], stat_refs[0], False)
        dq_acc[...] += tn(kv_refs[mask][:, :size], grad)

    def later(mask):
        prob, grad = terms(kv_refs[0], q_refs[mask], dout_refs[mask], stat_refs[mask], False)
        dk_ref[...] += nn(grad, q_refs[mask][...])
        dv_ref[...] += nn(prob, dout_refs[mask][...])

    for mask in range(1, groups):
        pl.when((blk ^ mask) < blk)(functools.partial(earlier, mask))
        pl.when((blk ^ mask) > blk)(functools.partial(later, mask))
    dq_ref[...] = dq_acc[...].T


def attend_back(at, kv, queries, douts, stats, tok_rows, scale):
    span, size = queries[0].shape
    groups = len(kv)
    vmem = pl.BlockSpec(memory_space=pltpu.VMEM)
    shape = jax.ShapeDtypeStruct((span, size), F32)
    return pl.pallas_call(
        functools.partial(attend_back_kernel, groups, tok_rows, scale),
        out_shape=(shape, shape, shape),
        in_specs=[pl.BlockSpec(memory_space=pltpu.SMEM)] + [vmem] * (4 * groups),
        out_specs=(vmem, vmem, vmem),
        scratch_shapes=[pltpu.VMEM((size, span), F32)],
        compiler_params=pltpu.CompilerParams(vmem_limit_bytes=40 * MIB),
        cost_estimate=pl.CostEstimate(
            flops=8 * groups * span * span * size,
            bytes_accessed=(4 * groups + 6) * span * size * 2,
            transcendentals=groups * span * span,
        ),
        name="attend_back",
    )(at, *kv, *queries, *douts, *stats)


def experts_kernel(
    experts,
    x_ref,
    g_ref,
    hot_ref,
    up_ref,
    down_ref,
    route_ref,
    out_ref,
    dx_ref,
    hidden_ref,
    da_ref,
    dsm_ref,
):
    rows = x_ref.shape[0]
    units = up_ref.shape[1]
    width = units // experts
    step = min(units, 256)
    x, g = x_ref[...], g_ref[...]
    gate = jax.nn.sigmoid(nn(x, route_ref[...]))
    hot = hot_ref[...]
    named = hot * gate
    dgate = jnp.zeros((rows, experts), F32)
    lane = lax.broadcasted_iota(jnp.int32, (rows, experts), 1)
    for at in range(0, units, step):
        pre_all = nn(x, up_ref[:, at : at + step])
        dh_all = nt(g, down_ref[at : at + step, :])
        for inner in range(0, step, width):
            pre, dh = pre_all[:, inner : inner + width], dh_all[:, inner : inner + width]
            expert = (at + inner) // width
            scale = named[:, expert : expert + 1]
            sig = jax.nn.sigmoid(pre)
            act = pre * sig
            slope = sig * (1.0 + pre * (1.0 - sig))
            hidden_ref[:, at + inner : at + inner + width] = (act * scale).astype(BF)
            da_ref[:, at + inner : at + inner + width] = (dh * scale * slope).astype(BF)
            dgate = jnp.where(lane == expert, jnp.sum(dh * act, -1, keepdims=True), dgate)
    dsm = (dgate * hot * gate * (1.0 - gate)).astype(BF)
    dsm_ref[...] = dsm
    out_ref[...] = nn(hidden_ref[...], down_ref[...]).astype(BF)
    dx_ref[...] = (nt(da_ref[...], up_ref[...]) + nt(dsm, route_ref[...])).astype(BF)


def run_experts(x, g, hot, up, down, route):
    rows, width = x.shape
    units = up.shape[1]
    experts = hot.shape[1]
    tile = 256

    def moving(columns):
        return pl.BlockSpec((tile, columns), lambda i: (i, 0))

    def fixed(array):
        return pl.BlockSpec(array.shape, lambda i: (0, 0))

    return pl.pallas_call(
        functools.partial(experts_kernel, experts),
        grid=(rows // tile,),
        out_shape=(
            jax.ShapeDtypeStruct((rows, width), BF),
            jax.ShapeDtypeStruct((rows, width), BF),
            jax.ShapeDtypeStruct((rows, units), BF),
            jax.ShapeDtypeStruct((rows, units), BF),
            jax.ShapeDtypeStruct((rows, experts), BF),
        ),
        in_specs=[moving(width), moving(width), moving(experts), fixed(up), fixed(down), fixed(route)],
        out_specs=(moving(width), moving(width), moving(units), moving(units), moving(experts)),
        compiler_params=pltpu.CompilerParams(vmem_limit_bytes=40 * MIB),
        cost_estimate=pl.CostEstimate(
            flops=8 * rows * width * units,
            bytes_accessed=2 * (4 * rows * width + 2 * rows * units + 2 * width * units),
            transcendentals=rows * units,
        ),
        name="experts",
    )(x, g, hot, up, down, route)


def expert_grads_kernel(groups, *refs):
    x_refs, g_refs, hidden_refs, da_refs, dsm_refs = (
        refs[i * groups : (i + 1) * groups] for i in range(5)
    )
    up_ref, down_ref, route_ref, wide, narrow, small, sems = refs[5 * groups :]

    def copies(mask):
        slot = mask % 2
        places = (
            (x_refs, wide.at[slot, 0]),
            (g_refs, wide.at[slot, 1]),
            (hidden_refs, narrow.at[slot, 0]),
            (da_refs, narrow.at[slot, 1]),
            (dsm_refs, small.at[slot]),
        )
        return [
            pltpu.make_async_copy(sources[mask], place, sems.at[slot, i])
            for i, (sources, place) in enumerate(places)
        ]

    for move in copies(0):
        move.start()
    for mask in range(groups):
        slot = mask % 2
        if mask + 1 < groups:
            for move in copies(mask + 1):
                move.start()
        for move in copies(mask):
            move.wait()
        up = tn(wide[slot, 0], narrow[slot, 1])
        down = tn(narrow[slot, 0], wide[slot, 1])
        route = tn(wide[slot, 0], small[slot])
        if mask == 0:
            up_ref[...], down_ref[...], route_ref[...] = up, down, route
        else:
            up_ref[...] += up
            down_ref[...] += down
            route_ref[...] += route


def expert_grads(rows, grads, hidden, das, dsms):
    groups = len(rows)
    span, width = rows[0].shape
    units, experts = das[0].shape[1], dsms[0].shape[1]
    any_spec = pl.BlockSpec(memory_space=pl.ANY)
    vmem = pl.BlockSpec(memory_space=pltpu.VMEM)
    return pl.pallas_call(
        functools.partial(expert_grads_kernel, groups),
        out_shape=(
            jax.ShapeDtypeStruct((width, units), F32),
            jax.ShapeDtypeStruct((units, width), F32),
            jax.ShapeDtypeStruct((width, experts), F32),
        ),
        in_specs=[any_spec] * (5 * groups),
        out_specs=(vmem, vmem, vmem),
        scratch_shapes=[
            pltpu.VMEM((2, 2, span, width), BF),
            pltpu.VMEM((2, 2, span, units), BF),
            pltpu.VMEM((2, span, experts), BF),
            pltpu.SemaphoreType.DMA((2, 5)),
        ],
        compiler_params=pltpu.CompilerParams(vmem_limit_bytes=48 * MIB),
        cost_estimate=pl.CostEstimate(
            flops=4 * groups * span * width * units,
            bytes_accessed=4 * groups * span * (width + units) + 8 * width * units,
            transcendentals=0,
        ),
        name="expert_grads",
    )(*rows, *grads, *hidden, *das, *dsms)


def on_device(
    tokens,
    out_grad,
    ln_gain,
    w_query,
    w_key,
    w_value,
    w_output,
    route_value,
    route_output,
    route_expert,
    w_up,
    w_down,
    value_ids,
    output_ids,
    expert_ids,
):
    groups, heads = lax.axis_size("blk"), lax.axis_size("head")
    blk, head = lax.axis_index("blk"), lax.axis_index("head")
    tok_rows, width = tokens.shape
    head_count = value_ids.shape[1]
    att_count = route_value.shape[1] // head_count
    head_size = w_query.shape[1] // head_count
    experts = route_expert.shape[1]
    span = tok_rows * heads
    own_rows = w_query.shape[0]
    mixed = att_count * head_size
    scale = head_size ** (-0.5)
    device = blk * heads + head
    at = jnp.stack([blk, head]).astype(jnp.int32)

    used = 2 * head_size + mixed + att_count + head_count * att_count + 1
    packed_width = -(-used // 128) * 128
    per_head = []
    for h in range(head_count):
        per_head.append(
            jnp.concatenate(
                [
                    w_query[:, h * head_size : (h + 1) * head_size],
                    w_key[:, h * head_size : (h + 1) * head_size],
                    w_value[:, h * mixed : (h + 1) * mixed],
                    route_value[:, h * att_count : (h + 1) * att_count],
                    route_output,
                    ln_gain[:, None],
                    jnp.zeros((own_rows, packed_width - used), BF),
                ],
                axis=1,
            )
        )
    by_head = lax.all_to_all(jnp.stack(per_head), "head", 0, 0, tiled=True)
    by_head = by_head.reshape(heads * own_rows, packed_width)
    order = blk ^ jnp.arange(groups)
    weights = jnp.stack(gather_blk(by_head))[order].reshape(width, packed_width)

    wide = jnp.concatenate(gather_head(tokens))
    ids_all = jnp.concatenate(
        [value_ids.reshape(tok_rows, -1), output_ids.reshape(tok_rows, -1)], axis=1
    ).T
    ids_group = jnp.concatenate(gather_head(ids_all), axis=1).T
    value_hot = jnp.sum(
        (
            ids_group[:, : 2 * head_count].reshape(span, head_count, 2)[..., None]
            == jnp.arange(att_count)
        ).astype(F32),
        2,
    )
    output_hot = jnp.sum(
        (
            ids_group[:, 2 * head_count :].reshape(span, head_count, 2)[..., None]
            == jnp.arange(att_count)
        ).astype(F32),
        2,
    )
    output_full = lax.all_gather(w_output, ("blk", "head"), axis=0, tiled=True)

    places = jnp.arange(span)
    places = blk * span + (head ^ (places // tok_rows)) * tok_rows + places % tok_rows
    half = head_size // 2
    frequency = rope_base ** (-jnp.arange(half, dtype=F32) / half)
    angles = places.astype(F32)[:, None] * frequency[None, :]
    cosine, sine = jnp.cos(angles), jnp.sin(angles)

    inputs = wide.astype(F32)
    centre = jnp.mean(inputs, -1, keepdims=True)
    shifted = inputs - centre
    inv_std = lax.rsqrt(jnp.mean(shifted * shifted, -1, keepdims=True) + ln_eps)
    normal = shifted * inv_std
    gain = weights[:, used - 1].astype(F32)
    normed = (normal * gain).astype(BF)
    qk_weight = weights[:, : 2 * head_size]
    v_weight = weights[:, 2 * head_size :]
    qk_pre = nn(normed, qk_weight)
    from_tokens = nn(wide, v_weight)
    query = rotate(qk_pre[:, :head_size], cosine, sine).astype(BF)
    key = rotate(qk_pre[:, head_size:], cosine, sine).astype(BF)
    value_gate = jax.nn.sigmoid(from_tokens[:, mixed : mixed + att_count])
    my_value_hot = lax.dynamic_index_in_dim(value_hot, head, 1, keepdims=False)
    value_weight = my_value_hot * value_gate
    expert_values = from_tokens[:, :mixed].reshape(span, att_count, head_size)
    value = jnp.sum(value_weight[..., None] * expert_values, 1).astype(BF)
    output_gate = jax.nn.sigmoid(
        from_tokens[:, mixed + att_count : mixed + att_count + head_count * att_count]
    ).reshape(span, head_count, att_count)
    output_weight = output_hot * output_gate

    kv = gather_blk(jnp.concatenate([key, value], axis=1))
    mine, log_total = attend(at, query, kv, tok_rows, scale)

    def reorder(piece, mask):
        return jnp.concatenate(
            [piece[(s ^ mask) * tok_rows : ((s ^ mask) + 1) * tok_rows] for s in range(heads)]
        )

    got = [reorder(piece, mask) for mask, piece in enumerate(gather_head(mine))]
    head_order = head ^ jnp.arange(heads)
    head_out = jnp.stack(got)[head_order]
    weight_by_head = output_weight.transpose(1, 0, 2)
    mixed_heads = (weight_by_head[..., None] * head_out[:, :, None, :].astype(F32)).astype(BF)
    mixed_flat = mixed_heads.transpose(1, 0, 2, 3).reshape(span, head_count * mixed)
    middle = inputs + nn(mixed_flat, output_full)
    middle_low = middle.astype(BF)

    grad_group = jnp.concatenate(gather_head(out_grad))
    ids_expert = jnp.concatenate(gather_head(expert_ids.T), axis=1)
    first = device * experts + jnp.arange(experts)
    branch = group_grad = weight_grads = None
    near = min(groups, 8)
    for far in range(0, groups, near):
        base = (middle_low, grad_group, ids_expert)
        if far:
            base, branch, group_grad, weight_grads = lax.optimization_barrier(
                (base, branch, group_grad, weight_grads)
            )
            base = [swap(value, "blk", far) for value in base]
        rows, grads, ids_pieces = (gather_blk(value, near) for value in base)
        hots = [
            jnp.any(ids[:, :, None] == first, axis=0).astype(F32) for ids in ids_pieces
        ]
        done = [
            run_experts(x, g, hot, w_up, w_down, route_expert)
            for x, g, hot in zip(rows, grads, hots)
        ]
        outs, dxs, hidden, das, dsms = zip(*done)
        terms = expert_grads(rows, grads, hidden, das, dsms)
        dx_sum = reduce_blk(dxs)
        out_sum = reduce_blk(outs)
        if far:
            branch = branch + swap(out_sum.astype(BF), "blk", far).astype(F32)
            group_grad = group_grad + swap(dx_sum.astype(BF), "blk", far).astype(F32)
            weight_grads = [old + new for old, new in zip(weight_grads, terms)]
        else:
            branch, group_grad, weight_grads = out_sum, dx_sum, terms
    grad_up, grad_down, grad_route_expert = weight_grads

    group_grad = group_grad + jnp.concatenate(
        [out_grad.astype(F32), jnp.zeros((span - tok_rows, width), F32)]
    )
    group_low = group_grad.astype(BF)
    du = nt(group_low, output_full).reshape(span, head_count, att_count, head_size)
    dout_part = jnp.einsum("thed,the->htd", du, output_weight)
    dso_part = jnp.einsum("thed,htd->het", du, head_out.astype(F32))
    pad = -att_count % 8
    dso_part = jnp.concatenate([dso_part, jnp.zeros((head_count, pad, span), F32)], axis=1)
    dout = lax.dynamic_index_in_dim(dout_part, head, 0, keepdims=False)
    dso = lax.dynamic_index_in_dim(dso_part, head, 0, keepdims=False)
    for mask in range(1, heads):
        there = head ^ mask
        part = lax.dynamic_index_in_dim(dout_part, there, 0, keepdims=False).astype(BF)
        dout = dout + reorder(swap(part, "head", mask), mask).astype(F32)
        small = swap(lax.dynamic_index_in_dim(dso_part, there, 0, keepdims=False), "head", mask)
        dso = dso + reorder(small.T, mask).T
    dout_low = dout.astype(BF)
    my_gate = lax.dynamic_index_in_dim(output_gate, head, 1, keepdims=False)
    my_hot = lax.dynamic_index_in_dim(output_hot, head, 1, keepdims=False)
    output_lgrad = (dso.T[:, :att_count] * my_hot * my_gate * (1.0 - my_gate)).astype(BF)

    delta = jnp.sum(dout_low.astype(F32) * mine.astype(F32), -1)
    stats = jnp.concatenate([log_total, delta[None, :], jnp.zeros((6, span), F32)])
    douts = gather_blk(dout_low)
    stat_pieces = gather_blk(stats)
    queries = gather_blk(query)
    dq, dk, dv = attend_back(at, kv, queries, douts, stat_pieces, tok_rows, scale)

    flat_grad = tn(mixed_flat, group_low).astype(BF)
    out_rows = w_output.shape[0]
    by_group = flat_grad.reshape(groups, heads * out_rows, width)
    mine_rows = reduce_blk(
        [lax.dynamic_index_in_dim(by_group, blk ^ m, 0, keepdims=False) for m in range(groups)]
    ).reshape(heads, out_rows, width)
    grad_output = lax.dynamic_index_in_dim(mine_rows, head, 0, keepdims=False)
    for mask in range(1, heads):
        part = lax.dynamic_index_in_dim(mine_rows, head ^ mask, 0, keepdims=False).astype(BF)
        grad_output = grad_output + swap(part, "head", mask).astype(F32)

    query_back = rotate(dq, cosine, -sine).astype(BF)
    key_back = rotate(dk, cosine, -sine).astype(BF)
    value_back = dv.astype(BF).astype(F32)
    qk_back = jnp.concatenate([query_back, key_back], axis=1)
    dexpert = (value_weight[..., None] * value_back[:, None, :]).astype(BF).reshape(span, mixed)
    dvweight = jnp.sum(value_back[:, None, :] * expert_values, -1)
    value_lgrad = (dvweight * my_value_hot * value_gate * (1.0 - value_gate)).astype(BF)
    spread = jnp.where(
        (jnp.arange(head_count) == head)[None, :, None], output_lgrad[:, None, :], 0
    ).astype(BF)
    tail = packed_width - used + 1
    v_back = jnp.concatenate(
        [
            dexpert,
            value_lgrad,
            spread.reshape(span, head_count * att_count),
            jnp.zeros((span, tail), BF),
        ],
        axis=1,
    )
    grad_normed = nt(qk_back, qk_weight)
    grad_gain = jnp.sum(grad_normed * normal, 0)
    grad_normal = grad_normed * gain
    part = (
        group_grad
        + nt(v_back, v_weight)
        + inv_std
        * (
            grad_normal
            - jnp.mean(grad_normal, -1, keepdims=True)
            - normal * jnp.mean(grad_normal * normal, -1, keepdims=True)
        )
    )
    grad_input = part[:tok_rows]
    for mask in range(1, heads):
        piece = part[mask * tok_rows : (mask + 1) * tok_rows].astype(BF)
        grad_input = grad_input + swap(piece, "head", mask).astype(F32)

    grad_tok = tn(wide, v_back)
    lane = jnp.arange(grad_tok.shape[1])
    grad_tok = jnp.where(lane[None, :] == used - 1 - 2 * head_size, grad_gain[:, None], grad_tok)
    packed = jnp.concatenate([tn(normed, qk_back), grad_tok], axis=1).astype(BF)
    packed = packed.reshape(groups, heads * own_rows, packed_width)
    summed = reduce_blk(
        [lax.dynamic_index_in_dim(packed, blk ^ m, 0, keepdims=False) for m in range(groups)]
    )
    summed = lax.all_to_all(
        summed.astype(BF).reshape(heads, own_rows, packed_width), "head", 0, 0, tiled=True
    ).astype(F32)

    def columns(first, count):
        return summed[:, :, first : first + count].transpose(1, 0, 2).reshape(own_rows, -1)

    grad_query = columns(0, head_size)
    grad_key = columns(head_size, head_size)
    grad_value = columns(2 * head_size, mixed)
    grad_value_router = columns(2 * head_size + mixed, att_count)
    routed = summed[:, :, 2 * head_size + mixed + att_count : used]
    grad_output_router = jnp.sum(routed[:, :, :-1], 0)
    grad_gain_out = jnp.sum(routed[:, :, -1], 0)

    layer_out = middle[:tok_rows] + branch[:tok_rows]
    for mask in range(1, heads):
        piece = branch[mask * tok_rows : (mask + 1) * tok_rows].astype(BF)
        layer_out = layer_out + swap(piece, "head", mask).astype(F32)

    return (
        layer_out,
        grad_input,
        grad_gain_out,
        grad_query,
        grad_key,
        grad_value,
        grad_output,
        grad_value_router,
        grad_output_router,
        grad_route_expert,
        grad_up,
        grad_down,
    )


def solution(mesh):
    both = P(("blk", "head"), None)
    columns = P(None, ("blk", "head"))
    vector = P(("blk", "head"))
    return jax.shard_map(
        on_device,
        mesh=mesh,
        in_specs=(
            both, both, vector, both, both, both, both, both, both, columns, columns, both,
            P(("blk", "head"), None, None), P(("blk", "head"), None, None), both,
        ),
        out_specs=(
            both, both, vector, both, both, both, both, both, both, columns, columns, both,
        ),
        check_vma=False,
    )
```

time: 2070 us -> 628 us (0.30)
  waiting for transfers between devices: 1180 us -> 206 us
  blocking collectives: 359 us -> 0 us
  local copies, waits for them, and re-layouts: 281 us -> 92.5 us
  Pallas kernels: 0 us -> 92.6 us
  matrix products: 111 us -> 24.6 us
  starting transfers between devices: 46.9 us -> 131 us
    reduce_scatter x4 -> x0, waiting for transfers between devices: 549 us -> none  [the longest x1 230 us: on_device(): lax.psum_scatter(grad_output, ('blk', 'head'), scatter_dimension=0, tiled...]
    all_to_all x9 -> x2, waiting for transfers between devices: 322 us -> 0.01 us  [the longest x1 0.01 us: on_device(): lax.all_to_all(summed.astype(BF).reshape(heads, own_rows, packed_width),...]
    all_gather x2 -> x0, blocking collectives: 245 us -> none  [the longest x1 177 us: on_device(): lax.all_gather(route_output, ('blk', 'head'), axis=0, tiled=True)]
    unnamed x16 -> x1, waiting for transfers between devices: 244 us -> 0.68 us
    ppermute x0 -> x114, waiting for transfers between devices: none -> 206 us  [swap(): return lax.ppermute(value, axis, [(i, i ^ mask) for i in range(size)])]
    ppermute x0 -> x114, starting transfers between devices: none -> 124 us  [swap(): return lax.ppermute(value, axis, [(i, i ^ mask) for i in range(size)])]
    reshape x12 -> x5, local copies, waits for them, and re-layouts: 109 us -> 3.48 us  [the longest x4 2.62 us: columns(): summed[:, :, first:first + count].transpose(1, 0, 2).reshape(own_rows, -1)]
    pallas_call x0 -> x11, Pallas kernels: none -> 92.6 us  [the longest x8 55.5 us: run_experts(): pl.pallas_call(functools.partial(experts_kernel, experts), grid=(rows //...]
  transfers between devices with their start and end apart: 22 -> 117, of which waited for: 15 -> 33; matrix products, arithmetic and copies ran while one was open for 16% -> 21% of each run, Pallas kernels for 0% -> 15%
where the time goes in v1:
time: 628 us; the launch traced here: 617 us
  waiting for transfers between devices  206 us (33%)
  starting transfers between devices  131 us (21%)
  Pallas kernels  92.6 us (15%)
  local copies, waits for them, and re-layouts  92.5 us (15%)
  other arithmetic  54.3 us (9%)
  matrix products  24.6 us (4%)
  between operations  16.1 us (3%)
    ppermute x114, waiting for transfers between devices, swap(): return lax.ppermute(value, axis, [(i, i ^ mask) for i in range(size)])  206 us
    ppermute x114, starting transfers between devices, swap(): return lax.ppermute(value, axis, [(i, i ^ mask) for i in range(size)])  124 us
    unnamed x302, local copies, waits for them, and re-layouts  56.9 us
    pallas_call x8, Pallas kernels, run_experts(): pl.pallas_call(functools.partial(experts_kernel, experts), grid=(rows //...  55.5 us
    pallas_call x1, Pallas kernels, expert_grads(): pl.pallas_call(functools.partial(expert_grads_kernel, groups), out_shape=...  27.6 us
    convert_element_type x8, other arithmetic, reduce_blk(): pair = swap(pair.astype(BF), 'blk', mask).astype(F32)  16.1 us
  transfers between devices with their start and end apart: 117, of which 33 were waited for; matrix products, arithmetic and copies ran while one was open for 21% of the time, Pallas kernels for 15%

profile of v1, /device:TPU:0, one launch (start us, length us, event | category | flops | bytes accessed | tf_op | source)
XLA Modules:
  0.0 617.5 jit_solution(3108191139603419127)
XLA Ops:
  7.9 3.1 collective-permute-start
  24.3 3.4 all-to-all-start
  28.0 3.8 collective-permute-start.30
  33.2 3.9 collective-permute-done.30
  43.2 7.6 %collective-permute-done.2 = bf16[128,1024]{1,0:T(8,128)(2,1)S(1)} collective-permute-done((bf16[128,1024]{1,0:T(8,128)(2,1)S(1)}, bf16[128,1024]{1,0:T(8,128)(2,1)S(1)}, u32[]{:S(2)}, u32[]{:S(2)}) %collective-permute-start.2) | collective-permute-done | bytes 262176 | tf_op jit(solution)/shard_map/ppermute | solution.py:20
  55.9 4.9 collective-permute-done.7
  62.2 5.2 collective-permute-done.9
  72.0 3.7 gather_fusion
  98.8 3.8 collective-permute-done.31
  112.3 3.5 collective-permute-start.22
  116.6 3.8 collective-permute-done.22
  120.4 19.3 %collective-permute-start.21 = (bf16[512,128]{1,0:T(8,128)(2,1)S(1)}, bf16[512,128]{1,0:T(8,128)(2,1)S(1)}, u32[]{:S(2)}, u32[]{:S(2)}) collective-permute-start(bf16[512,128]{1,0:T(8,128)(2,1)S(1)} %get-tuple-element.60), channel_id=1, source_target_pairs={{0,2},{1,3},{2,0},{3,1},{4,6},{5,7},{6,4},{7,5},{8,10},{9,11},{10,... | collective-permute-start | bytes 393224 | tf_op jit(solution)/shard_map/ppermute | solution.py:20
  139.7 6.4 %collective-permute-done.21 = bf16[512,128]{1,0:T(8,128)(2,1)S(1)} collective-permute-done((bf16[512,128]{1,0:T(8,128)(2,1)S(1)}, bf16[512,128]{1,0:T(8,128)(2,1)S(1)}, u32[]{:S(2)}, u32[]{:S(2)}) %collective-permute-start.21) | collective-permute-done | bytes 131104 | tf_op jit(solution)/shard_map/ppermute | solution.py:20
  146.2 4.9 collective-permute-done.20
  156.6 5.4 collective-permute-start.46
  162.7 7.7 %fusion.142 = (bf16[512,1024]{1,0:T(8,128)(2,1)S(1)}, f32[512,1024]{1,0:T(8,128)}) fusion(bf16[512,2560]{0,1:T(8,128)(2,1)} %bitcast.219, bf16[2560,1024]{1,0:T(8,128)(2,1)} %all-gather.2.cloned.1.call-done, bf16[512,1024]{1,0:T(8,128)(2,1)} %copy-done.90), kind=kOutput, calls=%fused_computation.291 | convolution fusion | flops 2685927424 | bytes 12058624 | tf_op jit(solution)/shard_map/dot_general | solution.py:65
  173.3 12.9 %collective-permute-done.46.g_ref.refs_14_ = bf16[512,1024]{1,0:T(8,128)(2,1)} collective-permute-done((bf16[512,1024]{1,0:T(8,128)(2,1)S(1)}, bf16[512,1024]{1,0:T(8,128)(2,1)}, u32[]{:S(2)}, u32[]{:S(2)}) %collective-permute-start.46) | collective-permute-done | bytes 1048608 | tf_op jit(solution)/shard_map/ppermute | solution.py:20
  189.9 18.8 %collective-permute-done.38.g_ref.refs_12_ = bf16[512,1024]{1,0:T(8,128)(2,1)} collective-permute-done((bf16[512,1024]{1,0:T(8,128)(2,1)S(1)}, bf16[512,1024]{1,0:T(8,128)(2,1)}, u32[]{:S(2)}, u32[]{:S(2)}) %collective-permute-start.38) | collective-permute-done | bytes 1048608 | tf_op jit(solution)/shard_map/ppermute | solution.py:20
  221.8 9.4 %collective-permute-done.45.x_ref.refs_6_ = bf16[512,1024]{1,0:T(8,128)(2,1)} collective-permute-done((bf16[512,1024]{1,0:T(8,128)(2,1)S(1)}, bf16[512,1024]{1,0:T(8,128)(2,1)}, u32[]{:S(2)}, u32[]{:S(2)}) %collective-permute-start.45) | collective-permute-done | bytes 1048608 | tf_op jit(solution)/shard_map/ppermute | solution.py:20
  237.5 6.2 %experts.14 = (bf16[512,1024]{1,0:T(8,128)(2,1)S(1)}, bf16[512,1024]{1,0:T(8,128)(2,1)S(1)}, bf16[512,1024]{1,0:T(8,128)(2,1)S(1)}, bf16[512,1024]{1,0:T(8,128)(2,1)S(1)}, bf16[512,8]{1,0:T(8,128)(2,1)S(1)}) custom-call(bf16[512,1024]{1,0:T(8,128)(2,1)S(1)} %get-tuple-element.298.x_ref.refs_0_, bf16[512,1024]{1,0:T(8,128)(2,1)S(1)} %copy-done.16, ...), custom_call_target="tpu_custom_call" | custom-call | flops 4294967296 | bytes 10485760 | tf_op jit(solution)/shard_map/experts/pallas_call | solution.py:254
  245.2 8.2 %collective-permute-done.37.x_ref.refs_4_ = bf16[512,1024]{1,0:T(8,128)(2,1)} collective-permute-done((bf16[512,1024]{1,0:T(8,128)(2,1)S(1)}, bf16[512,1024]{1,0:T(8,128)(2,1)}, u32[]{:S(2)}, u32[]{:S(2)}) %collective-permute-start.37) | collective-permute-done | bytes 1048608 | tf_op jit(solution)/shard_map/ppermute | solution.py:20
  253.4 6.9 %experts.12 = (bf16[512,1024]{1,0:T(8,128)(2,1)S(1)}, bf16[512,1024]{1,0:T(8,128)(2,1)S(1)}, bf16[512,1024]{1,0:T(8,128)(2,1)S(1)}, bf16[512,1024]{1,0:T(8,128)(2,1)S(1)}, bf16[512,8]{1,0:T(8,128)(2,1)S(1)}) custom-call(bf16[512,1024]{1,0:T(8,128)(2,1)} %collective-permute-done.45.x_ref.refs_6_, bf16[512,1024]{1,0:T(8,128)(2,1)} %collective-permute-done.46.g_ref.refs_14_, ...), custom_call_target="tpu_custom_call" | custom-call | flops 4294967296 | bytes 10485760 | tf_op jit(solution)/shard_map/experts/pallas_call | solution.py:254
  262.9 7.7 %experts.15 = (bf16[512,1024]{1,0:T(8,128)(2,1)}, bf16[512,1024]{1,0:T(8,128)(2,1)}, bf16[512,1024]{1,0:T(8,128)(2,1)S(1)}, bf16[512,1024]{1,0:T(8,128)(2,1)S(1)}, bf16[512,8]{1,0:T(8,128)(2,1)S(1)}) custom-call(bf16[512,1024]{1,0:T(8,128)(2,1)} %collective-permute-done.53.x_ref.refs_1_, bf16[512,1024]{1,0:T(8,128)(2,1)} %collective-permute-done.54.g_ref.refs_9_, ...), custom_call_target="tpu_custom_call" | custom-call | flops 4294967296 | bytes 10485760 | tf_op jit(solution)/shard_map/experts/pallas_call | solution.py:254
  273.0 7.1 %experts.13 = (bf16[512,1024]{1,0:T(8,128)(2,1)}, bf16[512,1024]{1,0:T(8,128)(2,1)S(1)}, bf16[512,1024]{1,0:T(8,128)(2,1)S(1)}, bf16[512,1024]{1,0:T(8,128)(2,1)S(1)}, bf16[512,8]{1,0:T(8,128)(2,1)S(1)}) custom-call(bf16[512,1024]{1,0:T(8,128)(2,1)S(1)} %collective-permute-done.48.x_ref.refs_7_, bf16[512,1024]{1,0:T(8,128)(2,1)} %collective-permute-done.49.g_ref.refs_15_, ...), custom_call_target="tpu_custom_call" | custom-call | flops 4294967296 | bytes 10485760 | tf_op jit(solution)/shard_map/experts/pallas_call | solution.py:254
  281.6 6.3 %experts.11 = (bf16[512,1024]{1,0:T(8,128)(2,1)}, bf16[512,1024]{1,0:T(8,128)(2,1)S(1)}, bf16[512,1024]{1,0:T(8,128)(2,1)S(1)}, bf16[512,1024]{1,0:T(8,128)(2,1)S(1)}, bf16[512,8]{1,0:T(8,128)(2,1)S(1)}) custom-call(bf16[512,1024]{1,0:T(8,128)(2,1)S(1)} %collective-permute-done.40.x_ref.refs_5_, ...), custom_call_target="tpu_custom_call" | custom-call | flops 4294967296 | bytes 10485760 | tf_op jit(solution)/shard_map/experts/pallas_call | solution.py:254
  290.0 7.2 %experts.9 = (bf16[512,1024]{1,0:T(8,128)(2,1)S(1)}, bf16[512,1024]{1,0:T(8,128)(2,1)S(1)}, bf16[512,1024]{1,0:T(8,128)(2,1)S(1)}, bf16[512,1024]{1,0:T(8,128)(2,1)S(1)}, bf16[512,8]{1,0:T(8,128)(2,1)S(1)}) custom-call(bf16[512,1024]{1,0:T(8,128)(2,1)} %collective-permute-done.32.x_ref.refs_3_, bf16[512,1024]{1,0:T(8,128)(2,1)S(1)} %collective-permute-done.33.g_ref.refs_11_, ...), custom_call_target="tpu_custom_call" | custom-call | flops 4294967296 | bytes 10485760 | tf_op jit(solution)/shard_map/experts/pallas_call | solution.py:254
  300.8 6.9 %experts.10 = (bf16[512,1024]{1,0:T(8,128)(2,1)S(1)}, bf16[512,1024]{1,0:T(8,128)(2,1)S(1)}, bf16[512,1024]{1,0:T(8,128)(2,1)S(1)}, bf16[512,1024]{1,0:T(8,128)(2,1)S(1)}, bf16[512,8]{1,0:T(8,128)(2,1)S(1)}) custom-call(bf16[512,1024]{1,0:T(8,128)(2,1)} %collective-permute-done.37.x_ref.refs_4_, bf16[512,1024]{1,0:T(8,128)(2,1)} %collective-permute-done.38.g_ref.refs_12_, ...), custom_call_target="tpu_custom_call" | custom-call | flops 4294967296 | bytes 10485760 | tf_op jit(solution)/shard_map/experts/pallas_call | solution.py:254
  309.7 7.1 %experts.8 = (bf16[512,1024]{1,0:T(8,128)(2,1)S(1)}, bf16[512,1024]{1,0:T(8,128)(2,1)S(1)}, bf16[512,1024]{1,0:T(8,128)(2,1)S(1)}, bf16[512,1024]{1,0:T(8,128)(2,1)S(1)}, bf16[512,8]{1,0:T(8,128)(2,1)S(1)}) custom-call(bf16[512,1024]{1,0:T(8,128)(2,1)} %collective-permute-done.23.x_ref.refs_2_, bf16[512,1024]{1,0:T(8,128)(2,1)} %collective-permute-done.27.g_ref.refs_10_, ...), custom_call_target="tpu_custom_call" | custom-call | flops 4294967296 | bytes 10485760 | tf_op jit(solution)/shard_map/experts/pallas_call | solution.py:254
  333.3 16.6 %collective-permute-done.68.refs_10_ = bf16[512,128]{1,0:T(8,128)(2,1)S(1)} collective-permute-done((bf16[512,128]{1,0:T(8,128)(2,1)S(1)}, bf16[512,128]{1,0:T(8,128)(2,1)S(1)}, u32[]{:S(2)}, u32[]{:S(2)}) %collective-permute-start.68) | collective-permute-done | bytes 131104 | tf_op jit(solution)/shard_map/ppermute | solution.py:20
  353.4 17.0 %collective-permute-done.44 = bf16[512,1024]{1,0:T(8,128)(2,1)S(1)} collective-permute-done((bf16[512,1024]{1,0:T(8,128)(2,1)S(1)}, bf16[512,1024]{1,0:T(8,128)(2,1)S(1)}, u32[]{:S(2)}, u32[]{:S(2)}) %collective-permute-start.44) | collective-permute-done | bytes 1048608 | tf_op jit(solution)/shard_map/ppermute | solution.py:20
  371.4 27.6 %expert_grads.1 = (f32[1024,1024]{1,0:T(8,128)}, f32[1024,1024]{1,0:T(8,128)}, f32[1024,8]{1,0:T(8,128)S(1)}) custom-call(bf16[512,1024]{1,0:T(8,128)(2,1)S(1)} %get-tuple-element.298.x_ref.refs_0_, bf16[512,1024]{1,0:T(8,128)(2,1)} %collective-permute-done.53.x_ref.refs_1_, bf16[512,1024]{1,0:T(8,128)(2,1)} %collective-permute-done.23.x_ref.refs_2_, ...), custom_call_target="tpu_custom_call" | custom-call | flops 17179869184 | bytes 41943040 | tf_op jit(solution)/shard_map/expert_grads/pallas_call | solution.py:322
  403.1 4.7 fusion.125
  407.8 10.3 %collective-permute-done.70.refs_12_ = bf16[512,128]{1,0:T(8,128)(2,1)S(1)} collective-permute-done((bf16[512,128]{1,0:T(8,128)(2,1)}, bf16[512,128]{1,0:T(8,128)(2,1)S(1)}, u32[]{:S(2)}, u32[]{:S(2)}) %collective-permute-start.70) | collective-permute-done | bytes 131104 | tf_op jit(solution)/shard_map/ppermute | solution.py:20
  420.7 3.8 collective-permute-done.72.refs_14_
  425.6 3.6 convert_add_fusion.1
  429.2 3.3 convolution_convert_fusion
  452.8 3.4 collective-permute-done.93
  456.9 9.0 %collective-permute-done.75 = bf16[512,128]{1,0:T(8,128)(2,1)S(1)} collective-permute-done((bf16[512,128]{1,0:T(8,128)(2,1)}, bf16[512,128]{1,0:T(8,128)(2,1)S(1)}, u32[]{:S(2)}, u32[]{:S(2)}) %collective-permute-start.75) | collective-permute-done | bytes 131104 | tf_op jit(solution)/shard_map/ppermute | solution.py:20
  468.1 4.8 collective-permute-done.76
  472.9 5.2 collective-permute-done.74
  510.5 7.7 %attend_back.1 = (f32[512,128]{1,0:T(8,128)S(1)}, f32[512,128]{1,0:T(8,128)S(1)}, f32[512,128]{1,0:T(8,128)S(1)}) custom-call(s32[2]{0:T(128)S(1)} %copy-done.71, bf16[512,256]{1,0:T(8,128)(2,1)S(1)} %pad_maximum_fusion.2.refs_0_, bf16[512,256]{1,0:T(8,128)(2,1)S(1)} %copy-done.36, bf16[512,256]{1,0:T(8,128)(2,1)S(1)} %copy-done.30, ...), custom_call_target="tpu_custom_call" | custom-call | flops 2147483648 | bytes 4980736 | tf_op jit(solution)/shard_map/attend_back/pallas_call | solution.py:183
  531.7 6.8 %collective-permute-done.102 = bf16[128,1024]{1,0:T(8,128)(2,1)S(1)} collective-permute-done((bf16[128,1024]{1,0:T(8,128)(2,1)S(1)}, bf16[128,1024]{1,0:T(8,128)(2,1)S(1)}, u32[]{:S(2)}, u32[]{:S(2)}) %collective-permute-start.102) | collective-permute-done | bytes 262176 | tf_op jit(solution)/shard_map/ppermute | solution.py:20
  539.8 3.2 fusion.143
  549.3 3.6 all-to-all-start.1
  557.4 4.1 fusion.22
  564.0 11.3 %collective-permute-done.95 = bf16[128,1024]{1,0:T(8,128)(2,1)S(1)} collective-permute-done((bf16[128,1024]{1,0:T(8,128)(2,1)S(1)}, bf16[128,1024]{1,0:T(8,128)(2,1)S(1)}, u32[]{:S(2)}, u32[]{:S(2)}) %collective-permute-start.95) | collective-permute-done | bytes 262176 | tf_op jit(solution)/shard_map/ppermute | solution.py:20
  578.8 12.0 %collective-permute-done.107 = bf16[320,1024]{1,0:T(8,128)(2,1)} collective-permute-done((bf16[320,1024]{1,0:T(8,128)(2,1)}, bf16[320,1024]{1,0:T(8,128)(2,1)}, u32[]{:S(2)}, u32[]{:S(2)}) %collective-permute-start.107) | collective-permute-done | bytes 655392 | tf_op jit(solution)/shard_map/ppermute | solution.py:20
  602.1 7.5 %collective-permute-done.112 = bf16[80,1024]{1,0:T(8,128)(2,1)S(1)} collective-permute-done((bf16[80,1024]{1,0:T(8,128)(2,1)S(1)}, bf16[80,1024]{1,0:T(8,128)(2,1)S(1)}, u32[]{:S(2)}, u32[]{:S(2)}) %collective-permute-start.112) | collective-permute-done | bytes 163872 | tf_op jit(solution)/shard_map/ppermute | solution.py:20
  (658 shorter events, 240.5 us)
Async XLA Ops:
  7.2 155.5 %all-gather.2.cloned.1.call-start = ((), (), s32[]{:S(2)}) async-start(), calls=%async_computation.2 | async-start | bytes 5406720 | tf_op jit(solution)/shard_map/all_gather | solution.py:420
  7.9 34.2 %collective-permute-start = (bf16[128,1024]{1,0:T(8,128)(2,1)}, bf16[128,1024]{1,0:T(8,128)(2,1)}, u32[]{:S(2)}, u32[]{:S(2)}) collective-permute-start(bf16[128,1024]{1,0:T(8,128)(2,1)} %param.15), channel_id=1, source_target_pairs={{0,1},{1,0},{2,3},{3,2},{4,5},{5,4},{6,7},{7,6},{8,9},{9,8},{10,11... | collective-permute-start | bytes 786440 | tf_op jit(solution)/shard_map/ppermute | solution.py:20
  11.0 32.1 %collective-permute-start.1 = (bf16[128,1024]{1,0:T(8,128)(2,1)}, bf16[128,1024]{1,0:T(8,128)(2,1)S(1)}, u32[]{:S(2)}, u32[]{:S(2)}) collective-permute-start(bf16[128,1024]{1,0:T(8,128)(2,1)} %param.15), channel_id=1, source_target_pairs={{0,2},{1,3},{2,0},{3,1},{4,6},{5,7},{6,4},{7,5},{8,10},{9,11},{10,... | collective-permute-start | bytes 786440 | tf_op jit(solution)/shard_map/ppermute | solution.py:20
  24.3 27.2 %all-to-all-start = ((bf16[4,32,1024]{2,1,0:T(8,128)(2,1)}), bf16[4,32,1024]{2,1,0:T(8,128)(2,1)S(1)}, u32[]{:S(2)}, u32[]{:S(2)}) async-start(bf16[4,32,1024]{2,1,0:T(8,128)(2,1)} %pad_maximum_fusion.1), calls=%async_computation | async-start | bytes 524288 | tf_op jit(solution)/shard_map/all_to_all | solution.py:396
  38.2 52.7 %collective-permute-start.24 = (bf16[128,1024]{1,0:T(8,128)(2,1)S(1)}, bf16[128,1024]{1,0:T(8,128)(2,1)}, u32[]{:S(2)}, u32[]{:S(2)}) collective-permute-start(bf16[128,1024]{1,0:T(8,128)(2,1)S(1)} %copy-done.100), channel_id=1, source_target_pairs={{0,1},{1,0},{2,3},{3,2},{4,5},{5,4},{6,7},{7,6},{8,9},{9,8},{10,11... | collective-permute-start | bytes 786440 | tf_op jit(solution)/shard_map/ppermute | solution.py:20
  39.2 53.3 %collective-permute-start.25 = (bf16[128,1024]{1,0:T(8,128)(2,1)S(1)}, bf16[128,1024]{1,0:T(8,128)(2,1)}, u32[]{:S(2)}, u32[]{:S(2)}) collective-permute-start(bf16[128,1024]{1,0:T(8,128)(2,1)S(1)} %copy-done.100), channel_id=1, source_target_pairs={{0,2},{1,3},{2,0},{3,1},{4,6},{5,7},{6,4},{7,5},{8,10},{9,11},{10,... | collective-permute-start | bytes 786440 | tf_op jit(solution)/shard_map/ppermute | solution.py:20
  67.4 26.9 %collective-permute-start.26 = (bf16[128,1024]{1,0:T(8,128)(2,1)S(1)}, bf16[128,1024]{1,0:T(8,128)(2,1)}, u32[]{:S(2)}, u32[]{:S(2)}) collective-permute-start(bf16[128,1024]{1,0:T(8,128)(2,1)S(1)} %copy-done.100), channel_id=1, source_target_pairs={{0,3},{1,2},{2,1},{3,0},{4,7},{5,6},{6,5},{7,4},{8,11},{9,10},{10,... | collective-permute-start | bytes 786440 | tf_op jit(solution)/shard_map/ppermute | solution.py:20
  109.5 47.1 %collective-permute-start.55 = (s32[16,512]{1,0:T(8,128)}, s32[16,512]{1,0:T(8,128)}, u32[]{:S(2)}, u32[]{:S(2)}) collective-permute-start(s32[16,512]{1,0:T(8,128)} %pad_add_fusion), channel_id=1, source_target_pairs={{0,4},{4,0},{8,12},{12,8},{16,20},{20,16},{24,28},{28,24},{1,5},{5... | collective-permute-start | bytes 98312 | tf_op jit(solution)/shard_map/ppermute | solution.py:20
  109.5 52.6 %collective-permute-start.34 = (s32[16,512]{1,0:T(8,128)}, s32[16,512]{1,0:T(8,128)}, u32[]{:S(2)}, u32[]{:S(2)}) collective-permute-start(s32[16,512]{1,0:T(8,128)} %copy-done.115), channel_id=1, source_target_pairs={{0,4},{4,0},{8,12},{12,8},{16,20},{20,16},{24,28},{28,24},{1,5},{5... | collective-permute-start | bytes 98312 | tf_op jit(solution)/shard_map/ppermute | solution.py:20
  110.0 52.1 %collective-permute-start.42 = (s32[16,512]{1,0:T(8,128)}, s32[16,512]{1,0:T(8,128)}, u32[]{:S(2)}, u32[]{:S(2)}) collective-permute-start(s32[16,512]{1,0:T(8,128)} %copy-done.117), channel_id=1, source_target_pairs={{0,4},{4,0},{8,12},{12,8},{16,20},{20,16},{24,28},{28,24},{1,5},{5... | collective-permute-start | bytes 98312 | tf_op jit(solution)/shard_map/ppermute | solution.py:20
  110.1 60.4 %collective-permute-start.50 = (s32[16,512]{1,0:T(8,128)}, s32[16,512]{1,0:T(8,128)}, u32[]{:S(2)}, u32[]{:S(2)}) collective-permute-start(s32[16,512]{1,0:T(8,128)} %collective-permute-done.47), channel_id=1, source_target_pairs={{0,4},{4,0},{8,12},{12,8},{16,20},{20,16},{24,28},{28,24},{1,5},{5... | collective-permute-start | bytes 98312 | tf_op jit(solution)/shard_map/ppermute | solution.py:20
  151.1 35.1 %collective-permute-start.54 = (bf16[512,1024]{1,0:T(8,128)(2,1)S(1)}, bf16[512,1024]{1,0:T(8,128)(2,1)}, u32[]{:S(2)}, u32[]{:S(2)}) collective-permute-start(bf16[512,1024]{1,0:T(8,128)(2,1)S(1)} %constant_dynamic-update-slice_fusion.4.g_ref.refs_8_), channel_id=1, source_target_pairs={{0,4},{4,0},{8,12},{12,8},{16,20},{20,16},{24,28},{28,24},{1,5},{5... | collective-permute-start | bytes 3145736 | tf_op jit(solution)/shard_map/ppermute | solution.py:20
  156.6 29.6 %collective-permute-start.46 = (bf16[512,1024]{1,0:T(8,128)(2,1)S(1)}, bf16[512,1024]{1,0:T(8,128)(2,1)}, u32[]{:S(2)}, u32[]{:S(2)}) collective-permute-start(bf16[512,1024]{1,0:T(8,128)(2,1)S(1)} %constant_dynamic-update-slice_fusion.4.g_ref.refs_8_), channel_id=1, source_target_pairs={{0,24},{4,28},{8,16},{12,20},{16,8},{20,12},{24,0},{28,4},{1,25},{... | collective-permute-start | bytes 3145736 | tf_op jit(solution)/shard_map/ppermute | solution.py:20
  162.0 46.7 %collective-permute-start.38 = (bf16[512,1024]{1,0:T(8,128)(2,1)S(1)}, bf16[512,1024]{1,0:T(8,128)(2,1)}, u32[]{:S(2)}, u32[]{:S(2)}) collective-permute-start(bf16[512,1024]{1,0:T(8,128)(2,1)S(1)} %constant_dynamic-update-slice_fusion.4.g_ref.refs_8_), channel_id=1, source_target_pairs={{0,16},{4,20},{8,24},{12,28},{16,0},{20,4},{24,8},{28,12},{1,17},{... | collective-permute-start | bytes 3145736 | tf_op jit(solution)/shard_map/ppermute | solution.py:20
  162.0 46.6 %collective-permute-start.27 = (bf16[512,1024]{1,0:T(8,128)(2,1)S(1)}, bf16[512,1024]{1,0:T(8,128)(2,1)}, u32[]{:S(2)}, u32[]{:S(2)}) collective-permute-start(bf16[512,1024]{1,0:T(8,128)(2,1)S(1)} %constant_dynamic-update-slice_fusion.4.g_ref.refs_8_), channel_id=1, source_target_pairs={{0,8},{4,12},{8,0},{12,4},{16,24},{20,28},{24,16},{28,20},{1,9},{5... | collective-permute-start | bytes 3145736 | tf_op jit(solution)/shard_map/ppermute | solution.py:20
  170.4 60.7 %collective-permute-start.45 = (bf16[512,1024]{1,0:T(8,128)(2,1)S(1)}, bf16[512,1024]{1,0:T(8,128)(2,1)}, u32[]{:S(2)}, u32[]{:S(2)}) collective-permute-start(bf16[512,1024]{1,0:T(8,128)(2,1)S(1)} %get-tuple-element.298.x_ref.refs_0_), channel_id=1, source_target_pairs={{0,24},{4,28},{8,16},{12,20},{16,8},{20,12},{24,0},{28,4},{1,25},{... | collective-permute-start | bytes 3145736 | tf_op jit(solution)/shard_map/ppermute | solution.py:20
  186.2 58.5 %collective-permute-start.49 = (bf16[512,1024]{1,0:T(8,128)(2,1)}, bf16[512,1024]{1,0:T(8,128)(2,1)}, u32[]{:S(2)}, u32[]{:S(2)}) collective-permute-start(bf16[512,1024]{1,0:T(8,128)(2,1)} %collective-permute-done.46.g_ref.refs_14_), channel_id=1, source_target_pairs={{0,4},{4,0},{8,12},{12,8},{16,20},{20,16},{24,28},{28,24},{1,5},{5... | collective-permute-start | bytes 3145736 | tf_op jit(solution)/shard_map/ppermute | solution.py:20
  186.2 67.2 %collective-permute-start.37 = (bf16[512,1024]{1,0:T(8,128)(2,1)S(1)}, bf16[512,1024]{1,0:T(8,128)(2,1)}, u32[]{:S(2)}, u32[]{:S(2)}) collective-permute-start(bf16[512,1024]{1,0:T(8,128)(2,1)S(1)} %get-tuple-element.298.x_ref.refs_0_), channel_id=1, source_target_pairs={{0,16},{4,20},{8,24},{12,28},{16,0},{20,4},{24,8},{28,12},{1,17},{... | collective-permute-start | bytes 3145736 | tf_op jit(solution)/shard_map/ppermute | solution.py:20
  208.7 53.6 %collective-permute-start.53 = (bf16[512,1024]{1,0:T(8,128)(2,1)S(1)}, bf16[512,1024]{1,0:T(8,128)(2,1)}, u32[]{:S(2)}, u32[]{:S(2)}) collective-permute-start(bf16[512,1024]{1,0:T(8,128)(2,1)S(1)} %get-tuple-element.298.x_ref.refs_0_), channel_id=1, source_target_pairs={{0,4},{4,0},{8,12},{12,8},{16,20},{20,16},{24,28},{28,24},{1,5},{5... | collective-permute-start | bytes 3145736 | tf_op jit(solution)/shard_map/ppermute | solution.py:20
  208.7 54.1 %collective-permute-start.23 = (bf16[512,1024]{1,0:T(8,128)(2,1)S(1)}, bf16[512,1024]{1,0:T(8,128)(2,1)}, u32[]{:S(2)}, u32[]{:S(2)}) collective-permute-start(bf16[512,1024]{1,0:T(8,128)(2,1)S(1)} %get-tuple-element.298.x_ref.refs_0_), channel_id=1, source_target_pairs={{0,8},{4,12},{8,0},{12,4},{16,24},{20,28},{24,16},{28,20},{1,9},{5... | collective-permute-start | bytes 3145736 | tf_op jit(solution)/shard_map/ppermute | solution.py:20
  231.2 41.4 %collective-permute-start.48 = (bf16[512,1024]{1,0:T(8,128)(2,1)}, bf16[512,1024]{1,0:T(8,128)(2,1)S(1)}, u32[]{:S(2)}, u32[]{:S(2)}) collective-permute-start(bf16[512,1024]{1,0:T(8,128)(2,1)} %collective-permute-done.45.x_ref.refs_6_), channel_id=1, source_target_pairs={{0,4},{4,0},{8,12},{12,8},{16,20},{20,16},{24,28},{28,24},{1,5},{5... | collective-permute-start | bytes 3145736 | tf_op jit(solution)/shard_map/ppermute | solution.py:20
  244.7 36.4 %collective-permute-start.41 = (bf16[512,1024]{1,0:T(8,128)(2,1)}, bf16[512,1024]{1,0:T(8,128)(2,1)S(1)}, u32[]{:S(2)}, u32[]{:S(2)}) collective-permute-start(bf16[512,1024]{1,0:T(8,128)(2,1)} %collective-permute-done.38.g_ref.refs_12_), channel_id=1, source_target_pairs={{0,4},{4,0},{8,12},{12,8},{16,20},{20,16},{24,28},{28,24},{1,5},{5... | collective-permute-start | bytes 3145736 | tf_op jit(solution)/shard_map/ppermute | solution.py:20
  253.4 28.3 %collective-permute-start.40 = (bf16[512,1024]{1,0:T(8,128)(2,1)}, bf16[512,1024]{1,0:T(8,128)(2,1)S(1)}, u32[]{:S(2)}, u32[]{:S(2)}) collective-permute-start(bf16[512,1024]{1,0:T(8,128)(2,1)} %collective-permute-done.37.x_ref.refs_4_), channel_id=1, source_target_pairs={{0,4},{4,0},{8,12},{12,8},{16,20},{20,16},{24,28},{28,24},{1,5},{5... | collective-permute-start | bytes 3145736 | tf_op jit(solution)/shard_map/ppermute | solution.py:20
  262.3 27.6 %collective-permute-start.33 = (bf16[512,1024]{1,0:T(8,128)(2,1)}, bf16[512,1024]{1,0:T(8,128)(2,1)S(1)}, u32[]{:S(2)}, u32[]{:S(2)}) collective-permute-start(bf16[512,1024]{1,0:T(8,128)(2,1)} %collective-permute-done.27.g_ref.refs_10_), channel_id=1, source_target_pairs={{0,4},{4,0},{8,12},{12,8},{16,20},{20,16},{24,28},{28,24},{1,5},{5... | collective-permute-start | bytes 3145736 | tf_op jit(solution)/shard_map/ppermute | solution.py:20
  262.8 27.2 %collective-permute-start.32 = (bf16[512,1024]{1,0:T(8,128)(2,1)}, bf16[512,1024]{1,0:T(8,128)(2,1)}, u32[]{:S(2)}, u32[]{:S(2)}) collective-permute-start(bf16[512,1024]{1,0:T(8,128)(2,1)} %collective-permute-done.23.x_ref.refs_2_), channel_id=1, source_target_pairs={{0,4},{4,0},{8,12},{12,8},{16,20},{20,16},{24,28},{28,24},{1,5},{5... | collective-permute-start | bytes 3145736 | tf_op jit(solution)/shard_map/ppermute | solution.py:20
  272.6 79.1 %collective-permute-start.56 = (bf16[512,1024]{1,0:T(8,128)(2,1)}, bf16[512,1024]{1,0:T(8,128)(2,1)}, u32[]{:S(2)}, u32[]{:S(2)}) collective-permute-start(bf16[512,1024]{1,0:T(8,128)(2,1)} %get-tuple-element.68), channel_id=1, source_target_pairs={{0,4},{4,0},{8,12},{12,8},{16,20},{20,16},{24,28},{28,24},{1,5},{5... | collective-permute-start | bytes 3145736 | tf_op jit(solution)/shard_map/ppermute | solution.py:20
  281.1 35.8 %collective-permute-start.51 = (bf16[512,1024]{1,0:T(8,128)(2,1)}, bf16[512,1024]{1,0:T(8,128)(2,1)}, u32[]{:S(2)}, u32[]{:S(2)}) collective-permute-start(bf16[512,1024]{1,0:T(8,128)(2,1)} %get-tuple-element.66), channel_id=1, source_target_pairs={{0,4},{4,0},{8,12},{12,8},{16,20},{20,16},{24,28},{28,24},{1,5},{5... | collective-permute-start | bytes 3145736 | tf_op jit(solution)/shard_map/ppermute | solution.py:20
  289.9 29.7 %collective-permute-start.43 = (bf16[512,1024]{1,0:T(8,128)(2,1)}, bf16[512,1024]{1,0:T(8,128)(2,1)}, u32[]{:S(2)}, u32[]{:S(2)}) collective-permute-start(bf16[512,1024]{1,0:T(8,128)(2,1)} %get-tuple-element.64), channel_id=1, source_target_pairs={{0,4},{4,0},{8,12},{12,8},{16,20},{20,16},{24,28},{28,24},{1,5},{5... | collective-permute-start | bytes 3145736 | tf_op jit(solution)/shard_map/ppermute | solution.py:20
  321.7 31.1 %collective-permute-start.52 = (bf16[512,1024]{1,0:T(8,128)(2,1)S(1)}, bf16[512,1024]{1,0:T(8,128)(2,1)S(1)}, u32[]{:S(2)}, u32[]{:S(2)}) collective-permute-start(bf16[512,1024]{1,0:T(8,128)(2,1)S(1)} %add_convert_fusion.3), channel_id=1, source_target_pairs={{0,24},{4,28},{8,16},{12,20},{16,8},{20,12},{24,0},{28,4},{1,25},{... | collective-permute-start | bytes 3145736 | tf_op jit(solution)/shard_map/ppermute | solution.py:20
  323.6 46.9 %collective-permute-start.44 = (bf16[512,1024]{1,0:T(8,128)(2,1)S(1)}, bf16[512,1024]{1,0:T(8,128)(2,1)S(1)}, u32[]{:S(2)}, u32[]{:S(2)}) collective-permute-start(bf16[512,1024]{1,0:T(8,128)(2,1)S(1)} %add_convert_fusion.4), channel_id=1, source_target_pairs={{0,16},{4,20},{8,24},{12,28},{16,0},{20,4},{24,8},{28,12},{1,17},{... | collective-permute-start | bytes 3145736 | tf_op jit(solution)/shard_map/ppermute | solution.py:20
  331.9 92.6 %collective-permute-start.66 = (bf16[512,1024]{1,0:T(8,128)(2,1)}, bf16[512,1024]{1,0:T(8,128)(2,1)}, u32[]{:S(2)}, u32[]{:S(2)}) collective-permute-start(bf16[512,1024]{1,0:T(8,128)(2,1)} %get-tuple-element.76), channel_id=1, source_target_pairs={{0,4},{4,0},{8,12},{12,8},{16,20},{20,16},{24,28},{28,24},{1,5},{5... | collective-permute-start | bytes 3145736 | tf_op jit(solution)/shard_map/ppermute | solution.py:20
  349.9 51.7 %collective-permute-start.36 = (bf16[512,1024]{1,0:T(8,128)(2,1)}, bf16[512,1024]{1,0:T(8,128)(2,1)}, u32[]{:S(2)}, u32[]{:S(2)}) collective-permute-start(bf16[512,1024]{1,0:T(8,128)(2,1)} %add_convert_fusion.5), channel_id=1, source_target_pairs={{0,8},{4,12},{8,0},{12,4},{16,24},{20,28},{24,16},{28,20},{1,9},{5... | collective-permute-start | bytes 3145736 | tf_op jit(solution)/shard_map/ppermute | solution.py:20
  351.6 73.4 %collective-permute-start.65 = (bf16[512,1024]{1,0:T(8,128)(2,1)}, bf16[512,1024]{1,0:T(8,128)(2,1)}, u32[]{:S(2)}, u32[]{:S(2)}) collective-permute-start(bf16[512,1024]{1,0:T(8,128)(2,1)} %add_convert_fusion), channel_id=1, source_target_pairs={{0,24},{4,28},{8,16},{12,20},{16,8},{20,12},{24,0},{28,4},{1,25},{... | collective-permute-start | bytes 3145736 | tf_op jit(solution)/shard_map/ppermute | solution.py:20
  352.8 72.4 %collective-permute-start.63 = (bf16[512,1024]{1,0:T(8,128)(2,1)}, bf16[512,1024]{1,0:T(8,128)(2,1)}, u32[]{:S(2)}, u32[]{:S(2)}) collective-permute-start(bf16[512,1024]{1,0:T(8,128)(2,1)} %add_convert_fusion.1), channel_id=1, source_target_pairs={{0,16},{4,20},{8,24},{12,28},{16,0},{20,4},{24,8},{28,12},{1,17},{... | collective-permute-start | bytes 3145736 | tf_op jit(solution)/shard_map/ppermute | solution.py:20
  370.4 55.1 %collective-permute-start.61 = (bf16[512,1024]{1,0:T(8,128)(2,1)}, bf16[512,1024]{1,0:T(8,128)(2,1)}, u32[]{:S(2)}, u32[]{:S(2)}) collective-permute-start(bf16[512,1024]{1,0:T(8,128)(2,1)} %add_convert_fusion.2), channel_id=1, source_target_pairs={{0,8},{4,12},{8,0},{12,4},{16,24},{20,28},{24,16},{28,20},{1,9},{5... | collective-permute-start | bytes 3145736 | tf_op jit(solution)/shard_map/ppermute | solution.py:20
  424.5 54.8 %collective-permute-start.67 = (bf16[512,128]{1,0:T(8,128)(2,1)S(1)}, bf16[512,128]{1,0:T(8,128)(2,1)S(1)}, u32[]{:S(2)}, u32[]{:S(2)}) collective-permute-start(bf16[512,128]{1,0:T(8,128)(2,1)S(1)} %copy-done.13), channel_id=1, source_target_pairs={{0,4},{4,0},{8,12},{12,8},{16,20},{20,16},{24,28},{28,24},{1,5},{5... | collective-permute-start | bytes 393224 | tf_op jit(solution)/shard_map/ppermute | solution.py:20
  424.5 54.9 %collective-permute-start.69 = (bf16[512,128]{1,0:T(8,128)(2,1)S(1)}, bf16[512,128]{1,0:T(8,128)(2,1)S(1)}, u32[]{:S(2)}, u32[]{:S(2)}) collective-permute-start(bf16[512,128]{1,0:T(8,128)(2,1)S(1)} %copy-done.44), channel_id=1, source_target_pairs={{0,4},{4,0},{8,12},{12,8},{16,20},{20,16},{24,28},{28,24},{1,5},{5... | collective-permute-start | bytes 393224 | tf_op jit(solution)/shard_map/ppermute | solution.py:20
  425.0 56.6 %collective-permute-start.71 = (bf16[512,128]{1,0:T(8,128)(2,1)S(1)}, bf16[512,128]{1,0:T(8,128)(2,1)}, u32[]{:S(2)}, u32[]{:S(2)}) collective-permute-start(bf16[512,128]{1,0:T(8,128)(2,1)S(1)} %collective-permute-done.70.refs_12_), channel_id=1, source_target_pairs={{0,4},{4,0},{8,12},{12,8},{16,20},{20,16},{24,28},{28,24},{1,5},{5... | collective-permute-start | bytes 393224 | tf_op jit(solution)/shard_map/ppermute | solution.py:20
  425.1 57.8 %collective-permute-start.73 = (bf16[512,128]{1,0:T(8,128)(2,1)S(1)}, bf16[512,128]{1,0:T(8,128)(2,1)}, u32[]{:S(2)}, u32[]{:S(2)}) collective-permute-start(bf16[512,128]{1,0:T(8,128)(2,1)S(1)} %collective-permute-done.72.refs_14_), channel_id=1, source_target_pairs={{0,4},{4,0},{8,12},{12,8},{16,20},{20,16},{24,28},{28,24},{1,5},{5... | collective-permute-start | bytes 393224 | tf_op jit(solution)/shard_map/ppermute | solution.py:20
  495.0 29.8 %collective-permute-start.59 = (bf16[128,1024]{1,0:T(8,128)(2,1)}, bf16[128,1024]{1,0:T(8,128)(2,1)}, u32[]{:S(2)}, u32[]{:S(2)}) collective-permute-start(bf16[128,1024]{1,0:T(8,128)(2,1)} %get-tuple-element.231), channel_id=1, source_target_pairs={{0,3},{1,2},{2,1},{3,0},{4,7},{5,6},{6,5},{7,4},{8,11},{9,10},{10,... | collective-permute-start | bytes 786440 | tf_op jit(solution)/shard_map/ppermute | solution.py:20
  497.2 27.8 %collective-permute-start.58 = (bf16[128,1024]{1,0:T(8,128)(2,1)}, bf16[128,1024]{1,0:T(8,128)(2,1)}, u32[]{:S(2)}, u32[]{:S(2)}) collective-permute-start(bf16[128,1024]{1,0:T(8,128)(2,1)} %get-tuple-element.232), channel_id=1, source_target_pairs={{0,2},{1,3},{2,0},{3,1},{4,6},{5,7},{6,4},{7,5},{8,10},{9,11},{10,... | collective-permute-start | bytes 786440 | tf_op jit(solution)/shard_map/ppermute | solution.py:20
  497.2 28.3 %collective-permute-start.57 = (bf16[128,1024]{1,0:T(8,128)(2,1)}, bf16[128,1024]{1,0:T(8,128)(2,1)}, u32[]{:S(2)}, u32[]{:S(2)}) collective-permute-start(bf16[128,1024]{1,0:T(8,128)(2,1)} %get-tuple-element.230), channel_id=1, source_target_pairs={{0,1},{1,0},{2,3},{3,2},{4,5},{5,4},{6,7},{7,6},{8,9},{9,8},{10,11... | collective-permute-start | bytes 786440 | tf_op jit(solution)/shard_map/ppermute | solution.py:20
  499.4 53.5 %collective-permute-start.104 = (bf16[320,1024]{1,0:T(8,128)(2,1)}, bf16[320,1024]{1,0:T(8,128)(2,1)}, u32[]{:S(2)}, u32[]{:S(2)}) collective-permute-start(bf16[320,1024]{1,0:T(8,128)(2,1)} %get-tuple-element.210), channel_id=1, source_target_pairs={{0,4},{4,0},{8,12},{12,8},{16,20},{20,16},{24,28},{28,24},{1,5},{5... | collective-permute-start | bytes 1966088 | tf_op jit(solution)/shard_map/ppermute | solution.py:20
  499.5 56.4 %collective-permute-start.108 = (bf16[320,1024]{1,0:T(8,128)(2,1)}, bf16[320,1024]{1,0:T(8,128)(2,1)}, u32[]{:S(2)}, u32[]{:S(2)}) collective-permute-start(bf16[320,1024]{1,0:T(8,128)(2,1)} %get-tuple-element.212), channel_id=1, source_target_pairs={{0,4},{4,0},{8,12},{12,8},{16,20},{20,16},{24,28},{28,24},{1,5},{5... | collective-permute-start | bytes 1966088 | tf_op jit(solution)/shard_map/ppermute | solution.py:20
  527.9 29.4 %collective-permute-start.106 = (bf16[320,1024]{1,0:T(8,128)(2,1)S(1)}, bf16[320,1024]{1,0:T(8,128)(2,1)}, u32[]{:S(2)}, u32[]{:S(2)}) collective-permute-start(bf16[320,1024]{1,0:T(8,128)(2,1)S(1)} %copy-done.103), channel_id=1, source_target_pairs={{0,4},{4,0},{8,12},{12,8},{16,20},{20,16},{24,28},{28,24},{1,5},{5... | collective-permute-start | bytes 1966088 | tf_op jit(solution)/shard_map/ppermute | solution.py:20
  544.0 34.7 %collective-permute-start.110 = (bf16[320,1024]{1,0:T(8,128)(2,1)S(1)}, bf16[320,1024]{1,0:T(8,128)(2,1)}, u32[]{:S(2)}, u32[]{:S(2)}) collective-permute-start(bf16[320,1024]{1,0:T(8,128)(2,1)S(1)} %copy-done.102), channel_id=1, source_target_pairs={{0,4},{4,0},{8,12},{12,8},{16,20},{20,16},{24,28},{28,24},{1,5},{5... | collective-permute-start | bytes 1966088 | tf_op jit(solution)/shard_map/ppermute | solution.py:20
  549.3 29.3 %all-to-all-start.1 = ((bf16[4,32,1024]{2,1,0:T(8,128)(2,1)}), bf16[4,32,1024]{2,1,0:T(8,128)(2,1)S(1)}, u32[]{:S(2)}, u32[]{:S(2)}) async-start(bf16[4,32,1024]{2,1,0:T(8,128)(2,1)} %bitcast.67), calls=%async_computation.1 | async-start | bytes 524288 | tf_op jit(solution)/shard_map/all_to_all | solution.py:587
  562.5 28.3 %collective-permute-start.107 = (bf16[320,1024]{1,0:T(8,128)(2,1)}, bf16[320,1024]{1,0:T(8,128)(2,1)}, u32[]{:S(2)}, u32[]{:S(2)}) collective-permute-start(bf16[320,1024]{1,0:T(8,128)(2,1)} %get-tuple-element.209), channel_id=1, source_target_pairs={{0,16},{4,20},{8,24},{12,28},{16,0},{20,4},{24,8},{28,12},{1,17},{... | collective-permute-start | bytes 1966088 | tf_op jit(solution)/shard_map/ppermute | solution.py:20
  (207 other events, 2415.2 us)
Sparse Core Ops, SparseCore 0:
  10.9 84.2 all-gather.1

commit v2 on v1

v2 whole, which is shorter than its diff:
```python
import functools

import jax
import jax.numpy as jnp
from jax import lax
from jax.experimental import pallas as pl
from jax.experimental.pallas import tpu as pltpu
from jax.sharding import PartitionSpec as P

ATT_BLOCK = 256
ln_eps = 1e-05
rope_base = 10000.0
MIB = 1 << 20
LANES = 128
TILE = 256
BF = jnp.bfloat16
F32 = jnp.float32
VMEM = pl.BlockSpec(memory_space=pltpu.VMEM)
SMEM = pl.BlockSpec(memory_space=pltpu.SMEM)
ANY = pl.BlockSpec(memory_space=pl.ANY)
CHEAP = pl.CostEstimate(flops=0, bytes_accessed=0, transcendentals=0)
PARAMS = pltpu.CompilerParams(vmem_limit_bytes=56 * MIB)


def swap(value, axis, mask):
    size = lax.axis_size(axis)
    return lax.ppermute(value, axis, [(i, i ^ mask) for i in range(size)])


def gather_blk(value):
    far = [value] + [swap(value, "blk", m) for m in range(2, lax.axis_size("blk"), 2)]
    pieces = []
    for mine in far:
        pieces += [mine, swap(mine, "blk", 1)]
    return pieces


def gather_head(value):
    return [value] + [swap(value, "head", m) for m in range(1, lax.axis_size("head"))]


def hold_kernel(*refs):
    del refs


def hold(value, *tokens):
    return pl.pallas_call(
        hold_kernel,
        out_shape=jax.ShapeDtypeStruct(value.shape, value.dtype),
        in_specs=[ANY] * (1 + len(tokens)),
        out_specs=ANY,
        input_output_aliases={0: 0},
        cost_estimate=CHEAP,
        name="hold",
    )(value, *tokens)


def add_low(left, right):
    return (left.astype(F32) + right.astype(F32)).astype(BF)


def shape(dims, dtype):
    return jax.ShapeDtypeStruct(dims, dtype)


def nt(left, right):
    return lax.dot_general(left, right, (((1,), (1,)), ((), ())), preferred_element_type=F32)


def tn(left, right):
    return lax.dot_general(left, right, (((0,), (0,)), ((), ())), preferred_element_type=F32)


def nn(left, right):
    return jnp.dot(left, right, preferred_element_type=F32)


def turn(values, cosine, sine):
    return values * cosine + pltpu.roll(values, values.shape[-1] // 2, 1) * sine


def block_of(place, blk, head, tok_rows, span):
    return (blk * span + (head ^ (place // tok_rows)) * tok_rows + place % tok_rows) // ATT_BLOCK


def own_allowed(blk, head, tok_rows, span):
    keys = lax.broadcasted_iota(jnp.int32, (span, span), 0)
    queries = lax.broadcasted_iota(jnp.int32, (span, span), 1)
    return block_of(keys, blk, head, tok_rows, span) <= block_of(
        queries, blk, head, tok_rows, span
    )


def norm_of(values):
    centre = jnp.mean(values, -1, keepdims=True)
    shifted = values - centre
    inv_std = lax.rsqrt(jnp.mean(shifted * shifted, -1, keepdims=True) + ln_eps)
    return shifted * inv_std, inv_std


def high_low(values):
    high = values.astype(BF)
    return high, (values - high.astype(F32)).astype(BF)


def gain_row(weights_ref, lane, first):
    rows = weights_ref.shape[0]
    parts = []
    for at in range(0, rows, LANES):
        block = weights_ref[at : at + LANES, first : first + LANES].astype(F32)
        parts.append(block.T[lane : lane + 1])
    return jnp.concatenate(parts, axis=1)


def select(rows_of_lane, valid, from_row):
    return (valid & (from_row == rows_of_lane)).astype(BF)


def pack_kernel(layout, q_ref, k_ref, v_ref, small_ref, ids_ref, out_ref):
    size, mixed, att, head_count, gain_lane = layout
    row = lax.broadcasted_iota(jnp.int32, (LANES, LANES), 0)
    lane = lax.broadcasted_iota(jnp.int32, (LANES, LANES), 1)
    small = small_ref[...]
    rows = small.shape[0]
    packed = 2 * size + mixed + LANES
    for h in range(head_count):
        out_ref[h, :rows, :size] = q_ref[:, h * size : (h + 1) * size]
        out_ref[h, :rows, size : 2 * size] = k_ref[:, h * size : (h + 1) * size]
        out_ref[h, :rows, 2 * size : 2 * size + mixed] = v_ref[:, h * mixed : (h + 1) * mixed]
        out_ref[h, : ids_ref.shape[0], packed:] = ids_ref[...].astype(BF)
        part = lane // att - 1
        source = att * head_count + att * (h ^ part) + lane % att
        source = jnp.where(lane < att, att * h + lane, source)
        source = jnp.where(lane == gain_lane, 2 * att * head_count, source)
        tail = nn(small, select(source, lane <= gain_lane, row))
        out_ref[h, :rows, 2 * size + mixed : packed] = tail.astype(BF)


def project_kernel(layout, heads, groups, named, at_ref, cos_ref, sin_ref, ids_ref, *refs):
    tok_refs, w_refs = refs[:heads], refs[heads : heads + groups]
    qkv_ref, values_ref, gate_ref, weight_ref, all_ref, normed_ref = refs[heads + groups :]
    size, mixed, att, head_count, gain_lane = layout
    blk, head = at_ref[0], at_ref[1]
    rows = w_refs[0].shape[0]
    tok_rows = tok_refs[0].shape[0]
    width = normed_ref.shape[1]
    span = normed_ref.shape[0]
    for mask in range(groups):
        start = pl.multiple_of((blk ^ mask) * rows, rows)
        all_ref[pl.ds(start, rows), :] = w_refs[mask][...]
    gain = gain_row(all_ref, gain_lane, 2 * size + mixed)
    for s in range(heads):
        normal, _ = norm_of(tok_refs[s][...].astype(F32))
        normed_ref[s * tok_rows : (s + 1) * tok_rows, :] = (normal * gain).astype(BF)
    pre = nn(normed_ref[...], all_ref[:, : 2 * size])
    cosine, sine = cos_ref[...], sin_ref[...]
    qkv_ref[:, :size] = turn(pre[:, :size], cosine, sine).astype(BF)
    qkv_ref[:, size : 2 * size] = turn(pre[:, size:], cosine, sine).astype(BF)
    wide = jnp.concatenate([ref[...] for ref in tok_refs])
    marks = []
    for s in range(heads):
        ids = ids_ref[head ^ s].astype(F32)
        ids = jnp.concatenate([ids, jnp.zeros((LANES - ids.shape[0], tok_rows), F32)])
        marks.append(ids.T.astype(BF))
    marks = jnp.concatenate(marks)
    row = lax.broadcasted_iota(jnp.int32, (LANES, LANES), 0)
    lane = lax.broadcasted_iota(jnp.int32, (LANES, LANES), 1)
    column = named * head_count + named * (head ^ (lane // att - 1))
    column = jnp.where(lane < att, named * head, column)
    valid = lane < att * (head_count + 1)
    expert = lax.broadcasted_iota(jnp.int32, (span, LANES), 1)
    inside = expert < att * (head_count + 1)
    expert = (expert % att).astype(F32)
    hot = jnp.zeros((span, LANES), F32)
    for k in range(named):
        ids = nn(marks, select(column + k, valid, row))
        hot = jnp.where(inside & (ids == expert), 1.0, hot)
    gates = jax.nn.sigmoid(nn(wide, all_ref[:, 2 * size + mixed :]))
    weight = hot * gates
    gate_ref[...] = gates
    weight_ref[...] = weight
    value = jnp.zeros((span, size), F32)
    first = 2 * size
    expert_values = nn(wide, all_ref[:, first : first + mixed])
    values_ref[...] = expert_values
    for e in range(att):
        value += weight[:, e : e + 1] * expert_values[:, e * size : (e + 1) * size]
    qkv_ref[:, 2 * size :] = value.astype(BF)


def attend_kernel(groups, tok_rows, scale, at_ref, *refs):
    refs, (o_ref, lse_ref, top_ref, total_ref, acc_ref) = refs[:groups], refs[-5:]
    span = refs[0].shape[0]
    size = refs[0].shape[1] // 3
    blk, head = at_ref[0], at_ref[1]
    queries = refs[0][:, :size]

    def advance(ref, first):
        scores = nt(ref[:, size : 2 * size], queries) * scale
        if first:
            scores = jnp.where(own_allowed(blk, head, tok_rows, span), scores, -jnp.inf)
            top = jnp.max(scores, 0, keepdims=True)
        else:
            top = jnp.maximum(top_ref[...], jnp.max(scores, 0, keepdims=True))
        weights = jnp.exp(scores - top)
        mass = jnp.sum(weights, 0, keepdims=True)
        term = tn(ref[:, 2 * size :], weights.astype(BF))
        if first:
            total_ref[...] = mass
            acc_ref[...] = term
        else:
            fade = jnp.exp(top_ref[...] - top)
            total_ref[...] = total_ref[...] * fade + mass
            acc_ref[...] = acc_ref[...] * fade + term
        top_ref[...] = top

    advance(refs[0], True)
    for mask in range(1, groups):
        pl.when((blk ^ mask) < blk)(functools.partial(advance, refs[mask], False))
    lse_ref[...] = top_ref[...] + jnp.log(total_ref[...])
    o_ref[...] = (acc_ref[...] / total_ref[...]).T.astype(BF)


def attend(at, qkv, tok_rows, scale, tokens):
    span, size = qkv[0].shape[0], qkv[0].shape[1] // 3
    groups = len(qkv)
    return pl.pallas_call(
        functools.partial(attend_kernel, groups, tok_rows, scale),
        out_shape=(shape((span, size), BF), shape((1, span), F32)),
        in_specs=[SMEM] + [VMEM] * groups + [ANY] * len(tokens),
        out_specs=(VMEM, VMEM),
        scratch_shapes=[
            pltpu.VMEM((1, span), F32),
            pltpu.VMEM((1, span), F32),
            pltpu.VMEM((size, span), F32),
        ],
        compiler_params=PARAMS,
        cost_estimate=CHEAP,
        name="attend",
    )(at, *qkv, *tokens)


def attend_back_kernel(groups, tok_rows, scale, at_ref, *refs):
    own_refs, dout_refs = refs[:groups], refs[groups : 2 * groups]
    dq_ref, dk_ref, dv_ref, dq_acc = refs[-4:]
    size = own_refs[0].shape[1] // 3
    span = own_refs[0].shape[0]
    blk, head = at_ref[0], at_ref[1]
    parts = span // LANES

    def stat(ref, which):
        first = span + 2 * parts * which
        high = ref[first : first + parts, :].astype(F32)
        low = ref[first + parts : first + 2 * parts, :].astype(F32)
        both = high + low
        return jnp.concatenate([both[i : i + 1] for i in range(parts)], axis=1)

    def terms(key_ref, query_ref, dout_ref, own):
        scores = nt(key_ref[:, size : 2 * size], query_ref[:, :size]) * scale
        if own:
            scores = jnp.where(own_allowed(blk, head, tok_rows, span), scores, -jnp.inf)
        prob = jnp.exp(scores - stat(dout_ref, 0))
        prob_grad = nt(key_ref[:, 2 * size :], dout_ref[:span, :])
        score_grad = prob * (prob_grad - stat(dout_ref, 1)) * scale
        return prob.astype(BF), score_grad.astype(BF)

    prob, grad = terms(own_refs[0], own_refs[0], dout_refs[0], True)
    dq_acc[...] = tn(own_refs[0][:, size : 2 * size], grad)
    dk_ref[...] = nn(grad, own_refs[0][:, :size])
    dv_ref[...] = nn(prob, dout_refs[0][:span, :])

    def earlier(mask):
        prob, grad = terms(own_refs[mask], own_refs[0], dout_refs[0], False)
        dq_acc[...] += tn(own_refs[mask][:, size : 2 * size], grad)

    def later(mask):
        prob, grad = terms(own_refs[0], own_refs[mask], dout_refs[mask], False)
        dk_ref[...] += nn(grad, own_refs[mask][:, :size])
        dv_ref[...] += nn(prob, dout_refs[mask][:span, :])

    for mask in range(1, groups):
        pl.when((blk ^ mask) < blk)(functools.partial(earlier, mask))
        pl.when((blk ^ mask) > blk)(functools.partial(later, mask))
    dq_ref[...] = dq_acc[...].T


def attend_back(at, qkv, douts, tok_rows, scale, tokens):
    span, size = qkv[0].shape[0], qkv[0].shape[1] // 3
    groups = len(qkv)
    return pl.pallas_call(
        functools.partial(attend_back_kernel, groups, tok_rows, scale),
        out_shape=(shape((span, size), F32),) * 3,
        in_specs=[SMEM] + [VMEM] * (2 * groups) + [ANY] * len(tokens),
        out_specs=(VMEM,) * 3,
        scratch_shapes=[pltpu.VMEM((size, span), F32)],
        compiler_params=PARAMS,
        cost_estimate=CHEAP,
        name="attend_back",
    )(at, *qkv, *douts, *tokens)


def mix_kernel(layout, heads, at_ref, *refs):
    o_refs, tok_refs = refs[:heads], refs[heads : 2 * heads]
    weight_ref, wo_ref = refs[2 * heads : 2 * heads + 2]
    x1_ref, low_ref, u_ref = refs[-3:]
    size, mixed, att, _, _ = layout
    head = at_ref[1]
    span = weight_ref.shape[0]
    tok_rows = span // heads

    @pl.when(pl.program_id(0) == 0)
    def _():
        for s in range(heads):
            start = (head ^ s) * mixed
            for r in range(heads):
                rows = slice(r * tok_rows, (r + 1) * tok_rows)
                there = slice((r ^ s) * tok_rows, ((r ^ s) + 1) * tok_rows)
                out = o_refs[s][there, :].astype(F32)
                for e in range(att):
                    lane = att + att * s + e
                    u_ref[rows, pl.ds(pl.multiple_of(start + e * size, size), size)] = (
                        weight_ref[rows, lane : lane + 1] * out
                    ).astype(BF)

    own = jnp.concatenate([ref[...] for ref in tok_refs]).astype(F32)
    x1 = own + nn(u_ref[...], wo_ref[...])
    x1_ref[...] = x1[:tok_rows]
    low_ref[...] = x1.astype(BF)


def mix(layout, at, outs, tok_pieces, weight, w_output, tokens):
    heads = len(outs)
    span = weight.shape[0]
    depth, width = w_output.shape
    step = min(width, 256)

    def whole(array):
        return pl.BlockSpec(array.shape, lambda i: (0, 0))

    def columns(rows):
        return pl.BlockSpec((rows, step), lambda i: (0, i))

    return pl.pallas_call(
        functools.partial(mix_kernel, layout, heads),
        grid=(width // step,),
        out_shape=(
            shape((span // heads, width), F32),
            shape((span, width), BF),
            shape((span, depth), BF),
        ),
        in_specs=[SMEM]
        + [whole(o) for o in outs]
        + [columns(span // heads)] * heads
        + [whole(weight), columns(depth)]
        + [ANY] * len(tokens),
        out_specs=(
            columns(span // heads),
            columns(span),
            pl.BlockSpec((span, depth), lambda i: (0, 0)),
        ),
        compiler_params=PARAMS,
        cost_estimate=CHEAP,
        name="mix",
    )(at, *outs, *tok_pieces, weight, w_output, *tokens)


SLOTS = 16


def experts_kernel(plan, heads, experts, top, at_ref, *refs):
    chosen, far, count, tokens = plan
    x_refs = refs[:count]
    g_hbm, up_hbm, down_hbm, route_ref = refs[count : count + 4]
    groups = len(chosen)
    outs = refs[count + 4 + tokens :]
    out_refs, dx_refs = outs[:groups], outs[groups : 2 * groups]
    xs_hbm, gs_hbm, hidden_ref, da_ref = outs[2 * groups : 2 * groups + 4]
    xbuf, gbuf, xslot, gslot, dslot, up_ref, down_ref, back, in_sem, out_sem = outs[
        2 * groups + 4 :
    ]
    oslot = xbuf
    tok_rows = gbuf.shape[2] - top
    span, width = heads * tok_rows, xbuf.shape[2]
    tall = tok_rows + top
    unit = up_ref.shape[1] // experts
    arrivals = []
    sem = 0
    for p in range(groups):
        moves = []
        row = 0
        for index in chosen[p]:
            size = x_refs[index].shape[0]
            place = xbuf.at[p, pl.ds(row, size)]
            moves.append(pltpu.make_async_copy(x_refs[index], place, in_sem.at[sem]))
            row += size
            sem += 1
        for s in range(heads):
            device = (at_ref[0] ^ (far + p)) * heads + (at_ref[1] ^ s)
            source = g_hbm.at[pl.ds(pl.multiple_of(device * tall, 16), tall)]
            moves.append(pltpu.make_async_copy(source, gbuf.at[p, s], in_sem.at[sem]))
            sem += 1
        arrivals.append(moves)
    weights = [
        pltpu.make_async_copy(up_hbm, up_ref, in_sem.at[sem]),
        pltpu.make_async_copy(down_hbm, down_ref, in_sem.at[sem + 1]),
    ]
    for moves in [*arrivals, weights]:
        for move in moves:
            move.start()

    earlier = lax.broadcasted_iota(jnp.int32, (tok_rows, tok_rows), 0)
    later = lax.broadcasted_iota(jnp.int32, (tok_rows, tok_rows), 1)
    before = (earlier < later).astype(BF)
    place = lax.broadcasted_iota(jnp.int32, (experts, SLOTS, tok_rows), 1).astype(F32)
    for p in range(groups):
        for move in arrivals[p]:
            move.wait()
        for s in range(heads):
            rows = slice(s * tok_rows, (s + 1) * tok_rows)
            ids = gbuf[p, s, tok_rows:, :tok_rows].astype(F32)
            hots = []
            for e in range(experts):
                met = ids == (at_ref[2] + e).astype(F32)
                hots.append(jnp.max(met.astype(F32), 0, keepdims=True))
            hot = jnp.concatenate(hots)
            rank = nn(hot.astype(BF), before)
            rank = jnp.where(hot > 0.0, rank, -1.0)
            here = (rank[:, None, :] == place).astype(F32).reshape(experts * SLOTS, tok_rows)
            sub = p * heads + s
            back[sub] = here.T.astype(BF)
            here = here.astype(BF)
            at = slice(sub * SLOTS, (sub + 1) * SLOTS)
            moved = nn(here, xbuf[p, rows, :]).astype(BF)
            xslot[:experts, at, :] = moved.reshape(experts, SLOTS, width)
            moved = nn(here, gbuf[p, s, :tok_rows, :]).astype(BF)
            gslot[:experts, at, :] = moved.reshape(experts, SLOTS, width)
    saves = [
        pltpu.make_async_copy(xslot.at[pl.ds(0, experts)], xs_hbm, out_sem.at[2 * groups]),
        pltpu.make_async_copy(gslot.at[pl.ds(0, experts)], gs_hbm, out_sem.at[2 * groups + 1]),
    ]
    for move in [*saves]:
        move.start()
    for move in weights:
        move.wait()

    route = route_ref[...]
    held = xslot.shape[1]
    lane = lax.broadcasted_iota(jnp.int32, (held, LANES), 1)
    for e in range(experts):
        cols = slice(e * unit, (e + 1) * unit)
        x, g = xslot[e], gslot[e]
        both = jnp.concatenate([up_ref[:, cols], route], axis=1)
        pre_all = nn(x, both)
        pre, gate = pre_all[:, :unit], jax.nn.sigmoid(pre_all[:, unit + e : unit + e + 1])
        dh = nt(g, down_ref[cols, :])
        sig = jax.nn.sigmoid(pre)
        act = pre * sig
        hidden = (act * gate).astype(BF)
        da = (dh * gate * (sig + act * (1.0 - sig))).astype(BF)
        dsm = jnp.sum(dh * act, -1, keepdims=True) * gate * (1.0 - gate)
        dsm = jnp.where(lane == e, dsm, 0.0).astype(BF)
        da = jnp.concatenate([da, dsm], axis=1)
        hidden_ref[e] = hidden
        da_ref[e] = da
        dslot[e] = nt(da, both).astype(BF)
        oslot[e] = nn(hidden, down_ref[cols, :]).astype(BF)
    for move in saves:
        move.wait()

    sends = []
    for which, slots, buf, target in ((0, dslot, gslot, dx_refs), (1, oslot, xslot, out_refs)):
        for p in range(groups):
            for s in range(heads):
                rows = slice(s * tok_rows, (s + 1) * tok_rows)
                sub = p * heads + s
                at = slice(sub * SLOTS, (sub + 1) * SLOTS)
                values = slots[:experts, at, :].reshape(experts * SLOTS, width)
                buf[p, rows, :] = nn(back[sub], values).astype(BF)
            move = pltpu.make_async_copy(buf.at[p], target[p], out_sem.at[which * groups + p])
            move.start()
            sends.append(move)
    for move in sends:
        move.wait()


def run_experts(at, far, xs, g_all, up, down, route, experts, top, heads, tokens):
    groups = len(xs)
    width, units = up.shape
    span = sum(x.shape[0] for x in xs[0])
    tok_rows = span // heads
    held = groups * heads * SLOTS
    chosen, flat = [], []
    for arrays in xs:
        chosen.append(tuple(range(len(flat), len(flat) + len(arrays))))
        flat += arrays
    plan = (chosen, far, len(flat), len(tokens))
    subs = groups * heads
    slots = pltpu.VMEM((max(experts, groups), max(held, span), width), BF)
    return pl.pallas_call(
        functools.partial(experts_kernel, plan, heads, experts, top),
        out_shape=(shape((span, width), BF),) * (2 * groups)
        + (shape((experts, held, width), BF),) * 2
        + (
            shape((experts, held, units // experts), BF),
            shape((experts, held, units // experts + LANES), BF),
        ),
        in_specs=[SMEM] + [ANY] * (len(flat) + 3) + [VMEM] + [ANY] * len(tokens),
        out_specs=(ANY,) * (2 * groups + 2) + (VMEM, VMEM),
        scratch_shapes=[
            slots,
            pltpu.VMEM((groups, heads, tok_rows + top, width), BF),
            slots,
            slots,
            pltpu.VMEM((experts, held, width), BF),
            pltpu.VMEM((width, units), BF),
            pltpu.VMEM((units, width), BF),
            pltpu.VMEM((subs, tok_rows, experts * SLOTS), BF),
            pltpu.SemaphoreType.DMA((len(flat) + subs + 2,)),
            pltpu.SemaphoreType.DMA((2 * groups + 2,)),
        ],
        compiler_params=pltpu.CompilerParams(vmem_limit_bytes=60 * MIB),
        cost_estimate=CHEAP,
        name="experts",
    )(at, *flat, g_all, up, down, route, *tokens)


def expert_grads_kernel(halves, *refs):
    x_refs, g_refs, hidden_refs, da_refs = (
        refs[i * halves : (i + 1) * halves] for i in range(4)
    )
    up_ref, down_ref, route_ref = refs[-3:]
    unit = up_ref.shape[1]
    up = down = None
    for x_ref, g_ref, hidden_ref, da_ref in zip(x_refs, g_refs, hidden_refs, da_refs):
        term = tn(x_ref[0], da_ref[0])
        up = term if up is None else up + term
        term = tn(hidden_ref[0], g_ref[0])
        down = term if down is None else down + term
    up_ref[...] = up[:, :unit]
    down_ref[...] = down

    @pl.when(pl.program_id(0) == 0)
    def _():
        route_ref[...] = up[:, unit:]

    @pl.when(pl.program_id(0) > 0)
    def _():
        route_ref[...] += up[:, unit:]


def expert_grads(results, tokens):
    halves = len(results)
    experts, held, width = results[0][0].shape
    unit = results[0][2].shape[2]

    def block(array):
        return pl.BlockSpec((1,) + array.shape[1:], lambda e: (e, 0, 0))

    flat = [result[i] for i in range(4) for result in results]
    return pl.pallas_call(
        functools.partial(expert_grads_kernel, halves),
        grid=(experts,),
        out_shape=(
            shape((width, experts * unit), F32),
            shape((experts * unit, width), F32),
            shape((width, LANES), F32),
        ),
        in_specs=[block(array) for array in flat] + [ANY] * len(tokens),
        out_specs=(
            pl.BlockSpec((width, unit), lambda e: (0, e)),
            pl.BlockSpec((unit, width), lambda e: (e, 0)),
            pl.BlockSpec((width, LANES), lambda e: (0, 0)),
        ),
        compiler_params=PARAMS,
        cost_estimate=CHEAP,
        name="expert_grads",
    )(*flat, *tokens)


def spread_kernel(layout, heads, terms, at_ref, *refs):
    term_refs = refs[:terms]
    grad_ref, wo_ref, weight_ref = refs[terms : terms + 3]
    o_refs = refs[terms + 3 : terms + 3 + heads]
    g1_ref, low_ref = refs[-2 - heads : -heads]
    send_refs = refs[-heads:]
    size, mixed, att, _, _ = layout
    head = at_ref[1]
    span = g1_ref.shape[0]
    tok_rows = span // heads
    total = term_refs[0][...].astype(F32)
    for ref in term_refs[1:]:
        total += ref[...].astype(F32)
    g1_ref[...] = total
    g1_ref[:tok_rows, :] += grad_ref[...].astype(F32)
    low_ref[...] = g1_ref[...].astype(BF)
    lane = lax.broadcasted_iota(jnp.int32, (tok_rows, LANES), 1)
    for s in range(heads):
        start = pl.multiple_of((head ^ s) * mixed, LANES)
        du = nt(low_ref[...], wo_ref[pl.ds(start, mixed), :])
        for r in range(heads):
            rows = slice(r * tok_rows, (r + 1) * tok_rows)
            there = slice((r ^ s) * tok_rows, ((r ^ s) + 1) * tok_rows)
            out = o_refs[s][there, :].astype(F32)
            dout = jnp.zeros((tok_rows, size), F32)
            dots = jnp.zeros((tok_rows, LANES), F32)
            for e in range(att):
                at = att + att * s + e
                term = du[rows, e * size : (e + 1) * size]
                dout += weight_ref[rows, at : at + 1] * term
                dots = jnp.where(lane == e, jnp.sum(term * out, -1, keepdims=True), dots)
            send_refs[s][there, :] = dout.astype(BF)
            high, low = high_low(dots.T[:8, :])
            first = span + 16 * (r ^ s)
            send_refs[s][first : first + 16, :] = jnp.concatenate([high, low])


def spread(layout, at, terms, out_grad, w_output, weight, outs, tokens):
    heads = len(outs)
    span, width = terms[0].shape
    tok_rows = span // heads
    size = outs[0].shape[1]
    return pl.pallas_call(
        functools.partial(spread_kernel, layout, heads, len(terms)),
        out_shape=(shape((span, width), F32), shape((span, width), BF))
        + (shape((span + 16 * heads, size), BF),) * heads,
        in_specs=[SMEM] + [VMEM] * (len(terms) + 3 + heads) + [ANY] * len(tokens),
        out_specs=(VMEM,) * (2 + heads),
        compiler_params=PARAMS,
        cost_estimate=CHEAP,
        name="spread",
    )(at, *terms, out_grad, w_output, weight, *outs, *tokens)


def join_kernel(heads, att, *refs):
    got_refs, (o_ref, lse_ref, gate_ref, weight_ref) = refs[:heads], refs[heads : heads + 4]
    dout_ref, dso_ref = refs[-2:]
    span, size = o_ref.shape
    tok_rows = span // heads
    parts = span // LANES
    total = got_refs[0][...].astype(F32)
    for ref in got_refs[1:]:
        total += ref[...].astype(F32)
    low = total[:span].astype(BF)
    dout_ref[:span, :] = low
    product = low.astype(F32) * o_ref[...].astype(F32)
    stats = []
    lse = lse_ref[...]
    rows = [lse[:, i * LANES : (i + 1) * LANES] for i in range(parts)]
    stats += high_low(jnp.concatenate(rows))
    rows = [
        jnp.sum(product[i * LANES : (i + 1) * LANES].T, 0, keepdims=True) for i in range(parts)
    ]
    stats += high_low(jnp.concatenate(rows))
    dout_ref[span:, :] = jnp.concatenate(stats)
    for r in range(heads):
        first = span + 16 * r
        sums = total[first : first + 8] + total[first + 8 : first + 16]
        sums = jnp.concatenate([sums, jnp.zeros((LANES - 8, LANES), F32)]).T
        rows = slice(r * tok_rows, (r + 1) * tok_rows)
        moved = pltpu.roll(sums, att, 1)
        dso_ref[rows, :] = (moved * weight_ref[rows, :] * (1.0 - gate_ref[rows, :])).astype(BF)


def join(got, mine, log_total, gate, weight, att, tokens):
    heads = len(got)
    span, size = mine.shape
    parts = span // LANES
    return pl.pallas_call(
        functools.partial(join_kernel, heads, att),
        out_shape=(shape((span + 4 * parts, size), BF), shape((span, LANES), BF)),
        in_specs=[VMEM] * (heads + 4) + [ANY] * len(tokens),
        out_specs=(VMEM, VMEM),
        compiler_params=PARAMS,
        cost_estimate=CHEAP,
        name="join",
    )(*got, mine, log_total, gate, weight, *tokens)


def output_grad_kernel(rows, groups, at_ref, u_ref, g_ref, even_ref, odd_ref, all_ref):
    all_ref[...] = tn(u_ref[...], g_ref[...]).astype(BF)
    for mask in range(groups):
        place = pl.ds(pl.multiple_of((at_ref[0] ^ mask) * rows, rows), rows)
        ref = odd_ref if mask % 2 else even_ref
        ref[mask // 2 * rows : (mask // 2 + 1) * rows, :] = all_ref[place, :]


def output_grad(at, u, g, groups):
    depth, width = u.shape[1], g.shape[1]
    half = shape((depth // 2, width), BF)
    return pl.pallas_call(
        functools.partial(output_grad_kernel, depth // groups, groups),
        out_shape=(half, half),
        in_specs=[SMEM, VMEM, VMEM],
        out_specs=(VMEM, VMEM),
        scratch_shapes=[pltpu.VMEM((depth, width), BF)],
        compiler_params=PARAMS,
        cost_estimate=CHEAP,
        name="output_grad",
    )(at, u, g)


def branch_kernel(heads, *refs):
    x1_ref, own_ref, send_refs = refs[0], refs[-heads], refs[1 - heads :]
    rows = x1_ref.shape[0]
    for s in range(heads):
        at = slice(s * rows, (s + 1) * rows)
        total = sum(ref[at, :].astype(F32) for ref in refs[1:-heads])
        if s == 0:
            own_ref[...] = x1_ref[...] + total
        else:
            send_refs[s - 1][...] = total.astype(BF)


def branch(x1, terms, heads):
    return pl.pallas_call(
        functools.partial(branch_kernel, heads),
        out_shape=(shape(x1.shape, F32),) + (shape(x1.shape, BF),) * (heads - 1),
        in_specs=[VMEM] * (1 + len(terms)),
        out_specs=(VMEM,) * heads,
        compiler_params=PARAMS,
        cost_estimate=CHEAP,
        name="branch",
    )(x1, *terms)


def finish_kernel(layout, heads, groups, at_ref, *refs):
    (
        dq_ref, dk_ref, dv_ref, cos_ref, sin_ref, values_ref, gate_ref, weight_ref, dso_ref,
        normed_ref, all_ref, g1_ref,
    ) = refs[:12]
    tok_refs = refs[12 : 12 + heads]
    part_refs = refs[-4 - heads : -4]
    even_ref, odd_ref, product_ref, all_grads = refs[-4:]
    size, mixed, att, _, gain_lane = layout
    blk = at_ref[0]
    span, width = normed_ref.shape
    tok_rows = span // heads
    cosine, sine = cos_ref[...], -sin_ref[...]
    query_back = turn(dq_ref[...], cosine, sine).astype(BF)
    key_back = turn(dk_ref[...], cosine, sine).astype(BF)
    qk_back = jnp.concatenate([query_back, key_back], axis=1)
    value_back = dv_ref[...].astype(BF).astype(F32)
    lane = lax.broadcasted_iota(jnp.int32, (span, LANES), 1)
    dots = jnp.zeros((span, LANES), F32)
    columns = []
    for e in range(att):
        columns.append((weight_ref[:, e : e + 1] * value_back).astype(BF))
        dot = jnp.sum(value_back * values_ref[:, e * size : (e + 1) * size], -1, keepdims=True)
        dots = jnp.where(lane == e, dot, dots)
    gates = gate_ref[...]
    tail = (dots * weight_ref[...] * (1.0 - gates)).astype(BF)
    tail = jnp.where(lane < att, tail, jnp.where(lane < 2 * att, dso_ref[...], jnp.zeros_like(tail)))
    v_back = jnp.concatenate(columns + [tail], axis=1)
    gain = gain_row(all_ref, gain_lane, 2 * size + mixed)
    grad_normed = nt(qk_back, all_ref[:, : 2 * size])
    grad_wide = nt(v_back, all_ref[:, 2 * size :])
    for s in range(heads):
        rows = slice(s * tok_rows, (s + 1) * tok_rows)
        normal, inv_std = norm_of(tok_refs[s][...].astype(F32))
        product_ref[rows, :] = (grad_normed[rows] * normal).astype(BF)
        grad_normal = grad_normed[rows] * gain
        part = (
            g1_ref[rows, :]
            + grad_wide[rows]
            + inv_std
            * (
                grad_normal
                - jnp.mean(grad_normal, -1, keepdims=True)
                - normal * jnp.mean(grad_normal * normal, -1, keepdims=True)
            )
        )
        part_refs[s][...] = part if s == 0 else part.astype(BF)
    own = width // groups
    gain_pick = (lane == gain_lane).astype(BF)
    wide = jnp.concatenate([ref[...] for ref in tok_refs])
    all_grads[:, : 2 * size] = tn(normed_ref[...], qk_back).astype(BF)
    from_tokens = tn(wide, v_back)
    all_grads[:, 2 * size : 2 * size + mixed] = from_tokens[:, :mixed].astype(BF)
    all_grads[:, 2 * size + mixed :] = (
        from_tokens[:, mixed:] + tn(product_ref[...], gain_pick)
    ).astype(BF)
    for mask in range(groups):
        place = pl.ds(pl.multiple_of((blk ^ mask) * own, own), own)
        ref = odd_ref if mask % 2 else even_ref
        ref[mask // 2 * own : (mask // 2 + 1) * own, :] = all_grads[place, :]


def finish(layout, heads, groups, at, tokens, *arrays):
    span, width = arrays[9].shape
    packed = arrays[10].shape[1]
    half = (width // 2, packed)
    return pl.pallas_call(
        functools.partial(finish_kernel, layout, heads, groups),
        out_shape=(shape((span // heads, width), F32),)
        + (shape((span // heads, width), BF),) * (heads - 1)
        + (shape(half, BF), shape(half, BF)),
        in_specs=[SMEM] + [VMEM] * len(arrays) + [ANY] * len(tokens),
        out_specs=(VMEM,) * (heads + 2),
        scratch_shapes=[pltpu.VMEM((span, width), BF), pltpu.VMEM((width, packed), BF)],
        compiler_params=PARAMS,
        cost_estimate=CHEAP,
        name="finish",
    )(at, *arrays, *tokens)


def on_device(
    tokens,
    out_grad,
    ln_gain,
    w_query,
    w_key,
    w_value,
    w_output,
    route_value,
    route_output,
    route_expert,
    w_up,
    w_down,
    value_ids,
    output_ids,
    expert_ids,
):
    groups, heads = lax.axis_size("blk"), lax.axis_size("head")
    blk, head = lax.axis_index("blk"), lax.axis_index("head")
    tok_rows, width = tokens.shape
    head_count, named = value_ids.shape[1:]
    att = route_value.shape[1] // head_count
    size = w_query.shape[1] // head_count
    experts = route_expert.shape[1]
    top = expert_ids.shape[1]
    span = tok_rows * heads
    own_rows = w_query.shape[0]
    mixed = att * size
    scale = size ** (-0.5)
    device = blk * heads + head
    at = jnp.stack([blk, head, device * experts]).astype(jnp.int32)
    gain_lane = att + head_count * att
    layout = (size, mixed, att, head_count, gain_lane)
    used = 2 * size + mixed + gain_lane + 1
    packed = 2 * size + mixed + LANES

    small = jnp.concatenate(
        [
            route_value,
            route_output,
            ln_gain[:, None],
            jnp.zeros((own_rows, LANES - 2 * head_count * att - 1), BF),
        ],
        axis=1,
    )
    ids_rows = 2 * named * head_count + top
    ids = jnp.concatenate(
        [
            value_ids.transpose(1, 2, 0).reshape(-1, tok_rows),
            output_ids.transpose(1, 2, 0).reshape(-1, tok_rows),
            expert_ids.T,
        ]
    )
    by_head = pl.pallas_call(
        functools.partial(pack_kernel, layout),
        out_shape=shape((head_count, max(own_rows, ids_rows), packed + tok_rows), BF),
        in_specs=[VMEM] * 5,
        out_specs=VMEM,
        compiler_params=PARAMS,
        name="pack",
    )(w_query, w_key, w_value, small, ids)
    tok_pieces = gather_head(tokens)
    by_head = lax.all_to_all(by_head, "head", 0, 0, tiled=True)
    ids_group = by_head[:, :ids_rows, packed:]
    w_pieces = gather_blk(by_head[:, :own_rows, :packed].reshape(heads * own_rows, packed))

    wo_full = lax.all_gather(w_output, ("blk", "head"), axis=0, tiled=True)

    places = jnp.arange(span)
    places = blk * span + (head ^ (places // tok_rows)) * tok_rows + places % tok_rows
    half = size // 2
    frequency = rope_base ** (-jnp.arange(half, dtype=F32) / half)
    angles = places.astype(F32)[:, None] * frequency[None, :]
    cosine, sine = jnp.cos(angles), jnp.sin(angles)
    cosine = jnp.concatenate([cosine, cosine], axis=1)
    sine = jnp.concatenate([-sine, sine], axis=1)

    qkv, expert_values, gate, weight, weights, normed = pl.pallas_call(
        functools.partial(project_kernel, layout, heads, groups, named),
        out_shape=(
            shape((span, 3 * size), BF),
            shape((span, mixed), F32),
            shape((span, LANES), F32),
            shape((span, LANES), F32),
            shape((width, packed), BF),
            shape((span, width), BF),
        ),
        in_specs=[SMEM] + [VMEM] * (3 + heads + groups),
        out_specs=(VMEM,) * 6,
        compiler_params=PARAMS,
        cost_estimate=CHEAP,
        name="project",
    )(at, cosine, sine, ids_group, *tok_pieces, *w_pieces)

    ids_row = jnp.pad(expert_ids.T.astype(BF), ((0, 0), (0, width - tok_rows)))
    g_all = lax.all_gather(
        hold(jnp.concatenate([out_grad, ids_row]), qkv), ("blk", "head"), axis=0, tiled=True
    )

    qkv_pieces = gather_blk(qkv)
    mine, log_total = attend(at, qkv_pieces, tok_rows, scale, [])
    outs = gather_head(mine)
    x1, middle, mixed_heads = mix(layout, at, outs, tok_pieces, weight, wo_full, [])

    route = jnp.pad(route_expert, ((0, 0), (0, LANES - experts)))
    near = 8
    branch_terms = grad_terms = weight_grads = None

    def pair_sum(parts, mask):
        return add_low(parts[mask], swap(parts[mask + 1], "blk", 1))

    for far in range(0, groups, near):
        base = middle
        if far:
            base, *old = lax.optimization_barrier(
                (base, branch_terms, grad_terms, *weight_grads)
            )
            branch_terms, grad_terms, *weight_grads = old
            base = swap(base, "blk", far)
        even = {0: [base], 2: [swap(base, "blk", 2)], 4: [swap(base, "blk", 4)]}
        even[6] = [
            swap(even[2][0][: span // 2], "blk", 4),
            swap(even[4][0][span // 2 :], "blk", 2),
        ]
        xs = []
        for mask in range(0, near, 2):
            xs += [even[mask], [swap(x, "blk", 1) for x in even[mask]]]
        done = run_experts(
            at, far, xs, g_all, w_up, w_down, route, experts, top, heads, []
        )
        outs_all, dxs_all = done[:near], done[near : 2 * near]
        sums = [pair_sum(dxs_all, m) for m in (2, 4, 6)]
        grad_round = [dxs_all[0], swap(dxs_all[1], "blk", 1)]
        grad_round += [swap(value, "blk", m) for m, value in zip((2, 4, 6), sums)]
        terms = expert_grads([done[2 * near :]], sums)
        out_sums = [hold(pair_sum(outs_all, m), sums[-1]) for m in (2, 4, 6)]
        branch_round = [outs_all[0], swap(outs_all[1], "blk", 1)]
        out_sums = [hold(value, grad_round[-1]) for value in out_sums]
        branch_round += [swap(value, "blk", m) for m, value in zip((2, 4), out_sums)]
        if groups > near:
            branch_round.append(swap(out_sums[2], "blk", 6))
        if groups > near:
            def whole(terms):
                return functools.reduce(lambda a, b: a + b, [t.astype(F32) for t in terms])

            out_sum, dx_sum = whole(branch_round), whole(grad_round)
            if far:
                out_sum = branch_terms + swap(out_sum.astype(BF), "blk", far).astype(F32)
                dx_sum = grad_terms + swap(dx_sum.astype(BF), "blk", far).astype(F32)
                weight_grads = [old + new for old, new in zip(weight_grads, terms)]
            else:
                weight_grads = terms
            branch_terms, grad_terms = out_sum, dx_sum
        else:
            branch_terms, grad_terms, weight_grads = branch_round, grad_round, terms
    early = [*out_sums, weight_grads[2]]
    arrived = branch_round[2:4]
    if groups > near:
        branch_terms, grad_terms = [branch_terms], [grad_terms]
    grad_up, grad_down, grad_route_expert = weight_grads
    grad_route_expert = grad_route_expert[:, :experts]

    g1, g1_low, *sends = spread(layout, at, grad_terms, out_grad, wo_full, weight, outs, early)
    even, odd = output_grad(at, mixed_heads, g1_low, groups)
    got = [sends[0]] + [swap(sends[m], "head", m) for m in range(1, heads)]
    dout, dso = join(got, mine, log_total, gate, weight, att, [odd])
    dout_pieces = gather_blk(hold(dout, *arrived))
    dq, dk, dv = attend_back(at, qkv_pieces, dout_pieces, tok_rows, scale, [])

    if groups == near:
        branch_terms = branch_terms + [swap(hold(out_sums[2], *dout_pieces), "blk", 6)]
    layer_out, *outputs = branch(x1, branch_terms, heads)

    out_rows = w_output.shape[0]
    pair_sums = add_low(even, swap(hold(odd, *dout_pieces), "blk", 1))
    pair_sums = hold(pair_sums, outputs[0]).reshape(groups // 2, heads * out_rows, width)
    rows_sum = pair_sums[0].astype(F32)
    for index in range(1, groups // 2):
        rows_sum = rows_sum + swap(pair_sums[index], "blk", 2 * index).astype(F32)
    rows_sum = rows_sum.reshape(heads, out_rows, width)
    grad_output = lax.dynamic_index_in_dim(rows_sum, head, 0, keepdims=False)
    for mask in range(1, heads):
        part = lax.dynamic_index_in_dim(rows_sum, head ^ mask, 0, keepdims=False).astype(BF)
        grad_output = grad_output + swap(part, "head", mask).astype(F32)
        layer_out = layer_out + swap(outputs[mask - 1], "head", mask).astype(F32)

    grad_input, *parts, even_rows, odd_rows = finish(
        layout, heads, groups, at, [pair_sums], dq, dk, dv, cosine, sine, expert_values, gate, weight, dso,
        normed, weights, g1, *tok_pieces,
    )
    pairs = add_low(even_rows, swap(odd_rows, "blk", 1))
    own = width // groups
    summed = pairs[:own].astype(F32)
    for index in range(1, groups // 2):
        piece = pairs[index * own : (index + 1) * own]
        summed = summed + swap(piece, "blk", 2 * index).astype(F32)
    for mask in range(1, heads):
        grad_input = grad_input + swap(parts[mask - 1], "head", mask).astype(F32)
    summed = lax.all_to_all(
        summed.astype(BF).reshape(heads, own_rows, packed), "head", 0, 0, tiled=True
    ).astype(F32)

    def columns(first, count):
        return summed[:, :, first : first + count].transpose(1, 0, 2).reshape(own_rows, -1)

    grad_query = columns(0, size)
    grad_key = columns(size, size)
    grad_value = columns(2 * size, mixed)
    grad_value_router = columns(2 * size + mixed, att)
    grad_output_router = columns(2 * size + mixed + att, att)
    grad_gain = jnp.sum(summed[:, :, used - 1], 0)

    return (
        layer_out,
        grad_input,
        grad_gain,
        grad_query,
        grad_key,
        grad_value,
        grad_output,
        grad_value_router,
        grad_output_router,
        grad_route_expert,
        grad_up,
        grad_down,
    )


def solution(mesh):
    both = P(("blk", "head"), None)
    columns = P(None, ("blk", "head"))
    vector = P(("blk", "head"))
    triple = P(("blk", "head"), None, None)
    return jax.shard_map(
        on_device,
        mesh=mesh,
        in_specs=(
            both, both, vector, both, both, both, both, both, both, columns, columns, both,
            triple, triple, both,
        ),
        out_specs=(
            both, both, vector, both, both, both, both, both, both, columns, columns, both,
        ),
        check_vma=False,
    )
```

time: 628 us -> 487 us (0.78)
  the two profiles are of different devices: /device:TPU:0 before, /device:TPU:8 now
where the time goes in v2:
time: 487 us; the launch traced here: 479 us
  waiting for transfers between devices  237 us (49%)
  Pallas kernels  117 us (24%)
  starting transfers between devices  67.9 us (14%)
  other arithmetic  25.2 us (5%)
  local copies, waits for them, and re-layouts  16.1 us (3%)
  between operations  15 us (3%)
    ppermute x70, waiting for transfers between devices, swap(): return lax.ppermute(value, axis, [(i, i ^ mask) for i in range(size)])  217 us
    ppermute x70, starting transfers between devices, swap(): return lax.ppermute(value, axis, [(i, i ^ mask) for i in range(size)])  57.2 us
    pallas_call x1, Pallas kernels, run_experts(): pl.pallas_call(functools.partial(experts_kernel, plan, heads, experts, to...  36.7 us
    pallas_call x1, Pallas kernels, expert_grads(): pl.pallas_call(functools.partial(expert_grads_kernel, halves), grid=(expe...  13.6 us
    convert_element_type x8, other arithmetic, add_low(): return (left.astype(F32) + right.astype(F32)).astype(BF)  13.5 us
    pallas_call x1, Pallas kernels, attend_back(): pl.pallas_call(functools.partial(attend_back_kernel, groups, tok_rows, sc...  13.2 us
    all_gather x1, waiting for transfers between devices, on_device(): lax.all_gather(hold(jnp.concatenate([out_grad, ids_row]), qkv), ('blk', '...  11.7 us
    pallas_call x1, Pallas kernels, spread(): pl.pallas_call(functools.partial(spread_kernel, layout, heads, len(terms)...  10.4 us
  transfers between devices with their start and end apart: 74, of which 33 were waited for; matrix products, arithmetic and copies ran while one was open for 6% of the time, Pallas kernels for 15%

profile of v2, /device:TPU:8, one launch (start us, length us, event | category | flops | bytes accessed | tf_op | source)
XLA Modules:
  0.0 478.6 jit_solution(6604787820034702530)
XLA Ops:
  14.2 5.3 %all-to-all-start = ((bf16[4,32,1152]{2,1,0:T(8,128)(2,1)}), bf16[4,32,1152]{2,1,0:T(8,128)(2,1)S(1)}, u32[]{:S(2)}, u32[]{:S(2)}) async-start(bf16[4,32,1152]{2,1,0:T(8,128)(2,1)} %pack.1), calls=%async_computation | async-start | bytes 589824 | tf_op jit(solution)/shard_map/all_to_all | solution.py:868
  19.5 2.9 collective-permute-start.1
  23.1 7.9 %all-to-all-done = bf16[4,32,1152]{2,1,0:T(8,128)(2,1)S(1)} async-done(((bf16[4,32,1152]{2,1,0:T(8,128)(2,1)}), bf16[4,32,1152]{2,1,0:T(8,128)(2,1)S(1)}, u32[]{:S(2)}, u32[]{:S(2)}) %all-to-all-start) | async-done | bytes 294944 | tf_op jit(solution)/shard_map/all_to_all | solution.py:868
  35.6 2.7 collective-permute-done.refs_1_.refs_5_.refs_13_
  38.6 3.8 collective-permute-done.1.refs_2_.refs_6_.refs_14_
  46.4 14.2 %collective-permute-done.2.refs_3_.refs_7_.refs_15_ = bf16[128,1024]{1,0:T(8,128)(2,1)S(1)} collective-permute-done((bf16[128,1024]{1,0:T(8,128)(2,1)S(1)}, bf16[128,1024]{1,0:T(8,128)(2,1)S(1)}, u32[]{:S(2)}, u32[]{:S(2)}) %collective-permute-start.2) | collective-permute-done | bytes 262176 | tf_op jit(solution)/shard_map/ppermute | solution.py:27
  61.6 5.8 %project.1 = (bf16[512,384]{1,0:T(8,128)(2,1)}, f32[512,640]{1,0:T(8,128)}, f32[512,128]{1,0:T(8,128)}, f32[512,128]{1,0:T(8,128)}, bf16[1024,1024]{1,0:T(8,128)(2,1)}, /*index=5*/bf16[512,1024]{1,0:T(8,128)(2,1)}) custom-call(s32[3]{0:T(128)} %pad_add_fusion.1.at_ref, f32[512,128]{1,0:T(8,128)} %get-tuple-element.190.cos_ref.refs_3_, ...), custom_call_target="tpu_custom_call" | custom-call | tf_op jit(solution)/shard_map/project/pallas_call | solution.py:883
  71.0 14.9 %collective-permute-done.11.refs_2_ = bf16[512,384]{1,0:T(8,128)(2,1)S(1)} collective-permute-done((bf16[512,384]{1,0:T(8,128)(2,1)}, bf16[512,384]{1,0:T(8,128)(2,1)S(1)}, u32[]{:S(2)}, u32[]{:S(2)}) %collective-permute-start.11) | collective-permute-done | bytes 393248 | tf_op jit(solution)/shard_map/ppermute | solution.py:27
  86.5 8.4 %collective-permute-done.15.refs_6_ = bf16[512,384]{1,0:T(8,128)(2,1)S(1)} collective-permute-done((bf16[512,384]{1,0:T(8,128)(2,1)}, bf16[512,384]{1,0:T(8,128)(2,1)S(1)}, u32[]{:S(2)}, u32[]{:S(2)}) %collective-permute-start.15) | collective-permute-done | bytes 393248 | tf_op jit(solution)/shard_map/ppermute | solution.py:27
  97.4 4.1 attend.1
  101.4 2.9 collective-permute-start.18
  104.9 3.1 collective-permute-done.17.refs_1_.refs_9_
  108.0 8.4 %collective-permute-done.18.refs_2_.refs_10_ = bf16[512,128]{1,0:T(8,128)(2,1)S(1)} collective-permute-done((bf16[512,128]{1,0:T(8,128)(2,1)}, bf16[512,128]{1,0:T(8,128)(2,1)S(1)}, u32[]{:S(2)}, u32[]{:S(2)}) %collective-permute-start.18) | collective-permute-done | bytes 131104 | tf_op jit(solution)/shard_map/ppermute | solution.py:27
  116.4 6.9 %collective-permute-done.19.refs_3_.refs_11_ = bf16[512,128]{1,0:T(8,128)(2,1)S(1)} collective-permute-done((bf16[512,128]{1,0:T(8,128)(2,1)}, bf16[512,128]{1,0:T(8,128)(2,1)S(1)}, u32[]{:S(2)}, u32[]{:S(2)}) %collective-permute-start.19) | collective-permute-done | bytes 131104 | tf_op jit(solution)/shard_map/ppermute | solution.py:27
  124.0 8.4 %mix.1 = (f32[128,1024]{1,0:T(8,128)}, bf16[512,1024]{1,0:T(8,128)(2,1)}, bf16[512,2560]{1,0:T(8,128)(2,1)}) custom-call(s32[3]{0:T(128)} %pad_add_fusion.1.at_ref, bf16[512,128]{1,0:T(8,128)(2,1)} %get-tuple-element.70.refs_0_.refs_8_.refs_4_, bf16[512,128]{1,0:T(8,128)(2,1)} %copy-done.38, bf16[512,128]{1,0:T(8,128)(2,1)} %copy-done.39, ...), custom_call_target="tpu_custom_call" | custom-call | tf_op jit(solution)/shard_map/mix/pallas_call | solution.py:343
  132.4 2.1 collective-permute-start.21
  134.5 3.0 collective-permute-start.23
  137.5 28.2 %collective-permute-done.21.refs_2_ = bf16[512,1024]{1,0:T(8,128)(2,1)S(1)} collective-permute-done((bf16[512,1024]{1,0:T(8,128)(2,1)}, bf16[512,1024]{1,0:T(8,128)(2,1)S(1)}, u32[]{:S(2)}, u32[]{:S(2)}) %collective-permute-start.21) | collective-permute-done | bytes 1048608 | tf_op jit(solution)/shard_map/ppermute | solution.py:27
  165.7 2.7 collective-permute-start.25
  169.6 22.4 %collective-permute-done.25.refs_6_ = bf16[256,1024]{1,0:T(8,128)(2,1)} collective-permute-done((bf16[256,1024]{1,0:T(8,128)(2,1)S(1)}, bf16[256,1024]{1,0:T(8,128)(2,1)}, u32[]{:S(2)}, u32[]{:S(2)}) %collective-permute-start.25) | collective-permute-done | bytes 524320 | tf_op jit(solution)/shard_map/ppermute | solution.py:27
  192.1 2.8 collective-permute-done.26.refs_7_
  197.1 11.7 %all-gather.5.cloned.1.call-done.refs_10_ = bf16[4608,1024]{1,0:T(8,128)(2,1)} async-done(((bf16[144,1024]{1,0:T(8,128)(2,1)}), bf16[4608,1024]{1,0:T(8,128)(2,1)}) %all-gather.5.cloned.1.call-update) | async-done | bytes 9437200 | tf_op jit(solution)/shard_map/all_gather | solution.py:901
  208.8 36.7 %experts.1 = (bf16[512,1024]{1,0:T(8,128)(2,1)}, bf16[512,1024]{1,0:T(8,128)(2,1)}, bf16[512,1024]{1,0:T(8,128)(2,1)}, bf16[512,1024]{1,0:T(8,128)(2,1)}, bf16[5...) custom-call(s32[3]{0:T(128)} %pad_add_fusion.1.at_ref, ...), custom_call_target="tpu_custom_call" | custom-call | tf_op jit(solution)/shard_map/experts/pallas_call | solution.py:499
  259.7 18.7 %collective-permute-done.32.refs_1_.refs_4_ = bf16[512,1024]{1,0:T(8,128)(2,1)S(1)} collective-permute-done((bf16[512,1024]{1,0:T(8,128)(2,1)S(1)}, bf16[512,1024]{1,0:T(8,128)(2,1)S(1)}, u32[]{:S(2)}, u32[]{:S(2)}) %collective-permute-start.32) | collective-permute-done | bytes 1048608 | tf_op jit(solution)/shard_map/ppermute | solution.py:27
  281.2 2.9 add_convert_fusion.4.refs_0_
  284.2 13.6 %expert_grads.1 = (f32[1024,1024]{1,0:T(8,128)}, f32[1024,1024]{1,0:T(8,128)}, f32[1024,128]{1,0:T(8,128)}) custom-call(bf16[8,512,1024]{2,1,0:T(8,128)(2,1)} %get-tuple-element.90.refs_0_, bf16[8,512,1024]{2,1,0:T(8,128)(2,1)} %get-tuple-element.91.refs_1_, bf16[8,512,128]{2,1,0:T(8,128)(2,1)} %get-tuple-element.92.refs_2_, ...), custom_call_target="tpu_custom_call" | custom-call | tf_op jit(solution)/shard_map/expert_grads/pallas_call | solution.py:560
  297.8 2.5 collective-permute-done.41.refs_3_
  300.3 10.4 %spread.1 = (f32[512,1024]{1,0:T(8,128)}, bf16[512,1024]{1,0:T(8,128)(2,1)}, bf16[576,128]{1,0:T(8,128)(2,1)}, bf16[576,128]{1,0:T(8,128)(2,1)}, bf16[576,128]{1,0:T(8,128)(2,1)}, /*index=5*/bf16[576,128]{1,0:T(8,128)(2,1)}) custom-call(s32[3]{0:T(128)} %pad_add_fusion.1.at_ref, bf16[512,1024]{1,0:T(8,128)(2,1)} %get-tuple-element.84.refs_0_, ...), custom_call_target="tpu_custom_call" | custom-call | tf_op jit(solution)/shard_map/spread/pallas_call | solution.py:622
  314.2 7.4 %output_grad.1 = (bf16[1280,1024]{1,0:T(8,128)(2,1)}, bf16[1280,1024]{1,0:T(8,128)(2,1)}) custom-call(s32[3]{0:T(128)} %pad_add_fusion.1.at_ref, bf16[512,2560]{1,0:T(8,128)(2,1)} %get-tuple-element.101.u_ref, bf16[512,1024]{1,0:T(8,128)(2,1)} %get-tuple-element.102.g_ref), custom_call_target="tpu_custom_call" | custom-call | tf_op jit(solution)/shard_map/output_grad/pallas_call | solution.py:690
  321.6 2.6 collective-permute-done.43.refs_2_
  324.2 3.2 collective-permute-done.44.refs_3_
  328.0 2.4 join.1
  335.2 3.0 collective-permute-done.46.refs_3_.refs_10_
  344.3 13.2 %attend_back.1 = (f32[512,128]{1,0:T(8,128)}, f32[512,128]{1,0:T(8,128)}, f32[512,128]{1,0:T(8,128)}) custom-call(s32[3]{0:T(128)} %pad_add_fusion.1.at_ref, bf16[512,384]{1,0:T(8,128)(2,1)} %get-tuple-element.69.refs_0_.refs_1_, bf16[512,384]{1,0:T(8,128)(2,1)} %copy-done.18, bf16[512,384]{1,0:T(8,128)(2,1)} %copy-done.15, bf16[512,384]{1,0:T(8,128)(2,1)} %copy-done.19, ...), custom_call_target="tpu_custom_call" | custom-call | tf_op jit(solution)/shard_map/attend_back/pallas_call | solution.py:290
  357.5 12.3 %collective-permute-done.52.refs_5_ = bf16[512,1024]{1,0:T(8,128)(2,1)S(1)} collective-permute-done((bf16[512,1024]{1,0:T(8,128)(2,1)}, bf16[512,1024]{1,0:T(8,128)(2,1)S(1)}, u32[]{:S(2)}, u32[]{:S(2)}) %collective-permute-start.52) | collective-permute-done | bytes 1048608 | tf_op jit(solution)/shard_map/ppermute | solution.py:27
  370.8 4.1 branch.1
  375.0 2.8 add_convert_fusion.refs_0_
  377.7 9.4 %finish.1 = (f32[128,1024]{1,0:T(8,128)}, bf16[128,1024]{1,0:T(8,128)(2,1)}, bf16[128,1024]{1,0:T(8,128)(2,1)}, bf16[128,1024]{1,0:T(8,128)(2,1)}, bf16[512,1024]{1,0:T(8,128)(2,1)}, /*index=5*/bf16[512,1024]{1,0:T(8,128)(2,1)}) custom-call(s32[3]{0:T(128)} %pad_add_fusion.1.at_ref, f32[512,128]{1,0:T(8,128)} %get-tuple-element.109.refs_0_, ...), custom_call_target="tpu_custom_call" | custom-call | tf_op jit(solution)/shard_map/finish/pallas_call | solution.py:792
  387.9 2.5 collective-permute-start.54
  392.3 6.8 %collective-permute-done.53 = bf16[128,1024]{1,0:T(8,128)(2,1)S(1)} collective-permute-done((bf16[128,1024]{1,0:T(8,128)(2,1)S(1)}, bf16[128,1024]{1,0:T(8,128)(2,1)S(1)}, u32[]{:S(2)}, u32[]{:S(2)}) %collective-permute-start.53) | collective-permute-done | bytes 262176 | tf_op jit(solution)/shard_map/ppermute | solution.py:27
  399.8 8.9 %collective-permute-done.54 = bf16[128,1024]{1,0:T(8,128)(2,1)S(1)} collective-permute-done((bf16[128,1024]{1,0:T(8,128)(2,1)}, bf16[128,1024]{1,0:T(8,128)(2,1)S(1)}, u32[]{:S(2)}, u32[]{:S(2)}) %collective-permute-start.54) | collective-permute-done | bytes 262176 | tf_op jit(solution)/shard_map/ppermute | solution.py:27
  410.2 4.7 collective-permute-done.55
  415.8 2.5 collective-permute-start.58
  420.9 8.8 %collective-permute-done.65 = bf16[320,1024]{1,0:T(8,128)(2,1)S(1)} collective-permute-done((bf16[320,1024]{1,0:T(8,128)(2,1)S(1)}, bf16[320,1024]{1,0:T(8,128)(2,1)S(1)}, u32[]{:S(2)}, u32[]{:S(2)}) %collective-permute-start.65) | collective-permute-done | bytes 655392 | tf_op jit(solution)/shard_map/ppermute | solution.py:27
  433.5 9.1 %collective-permute-done.62 = bf16[128,1024]{1,0:T(8,128)(2,1)S(1)} collective-permute-done((bf16[128,1024]{1,0:T(8,128)(2,1)S(1)}, bf16[128,1024]{1,0:T(8,128)(2,1)S(1)}, u32[]{:S(2)}, u32[]{:S(2)}) %collective-permute-start.62) | collective-permute-done | bytes 262176 | tf_op jit(solution)/shard_map/ppermute | solution.py:27
  442.6 2.5 collective-permute-start.67
  446.4 5.4 %all-to-all-start.1 = ((bf16[4,32,1024]{2,1,0:T(8,128)(2,1)}), bf16[4,32,1024]{2,1,0:T(8,128)(2,1)S(1)}, u32[]{:S(2)}, u32[]{:S(2)}) async-start(bf16[4,32,1024]{2,1,0:T(8,128)(2,1)} %bitcast.11), calls=%async_computation.1 | async-start | bytes 524288 | tf_op jit(solution)/shard_map/all_to_all | solution.py:1004
  454.2 11.3 %collective-permute-done.69 = bf16[80,1024]{1,0:T(8,128)(2,1)S(1)} collective-permute-done((bf16[80,1024]{1,0:T(8,128)(2,1)S(1)}, bf16[80,1024]{1,0:T(8,128)(2,1)S(1)}, u32[]{:S(2)}, u32[]{:S(2)}) %collective-permute-start.69) | collective-permute-done | bytes 163872 | tf_op jit(solution)/shard_map/ppermute | solution.py:27
  (286 shorter events, 83.5 us)
Async XLA Ops:
  7.2 116.1 %all-gather.3.cloned.1.call-start = ((), (), s32[]{:S(2)}) async-start(), calls=%async_computation.2 | async-start | bytes 5406720 | tf_op jit(solution)/shard_map/all_gather | solution.py:872
  14.2 16.8 %all-to-all-start = ((bf16[4,32,1152]{2,1,0:T(8,128)(2,1)}), bf16[4,32,1152]{2,1,0:T(8,128)(2,1)S(1)}, u32[]{:S(2)}, u32[]{:S(2)}) async-start(bf16[4,32,1152]{2,1,0:T(8,128)(2,1)} %pack.1), calls=%async_computation | async-start | bytes 589824 | tf_op jit(solution)/shard_map/all_to_all | solution.py:868
  19.5 189.3 %all-gather.5.cloned.1.call-start = ((), (), s32[]{:S(2)}) async-start(), calls=%async_computation.3 | async-start | bytes 9732096 | tf_op jit(solution)/shard_map/all_gather | solution.py:901
  19.5 18.8 %collective-permute-start = (bf16[128,1024]{1,0:T(8,128)(2,1)}, bf16[128,1024]{1,0:T(8,128)(2,1)S(1)}, u32[]{:S(2)}, u32[]{:S(2)}) collective-permute-start(bf16[128,1024]{1,0:T(8,128)(2,1)} %refs_12_.3), channel_id=1, source_target_pairs={{0,1},{1,0},{2,3},{3,2},{4,5},{5,4},{6,7},{7,6},{8,9},{9,8},{10,11... | collective-permute-start | bytes 786440 | tf_op jit(solution)/shard_map/ppermute | solution.py:27
  19.5 22.8 %collective-permute-start.1 = (bf16[128,1024]{1,0:T(8,128)(2,1)}, bf16[128,1024]{1,0:T(8,128)(2,1)S(1)}, u32[]{:S(2)}, u32[]{:S(2)}) collective-permute-start(bf16[128,1024]{1,0:T(8,128)(2,1)} %refs_12_.3), channel_id=1, source_target_pairs={{0,2},{1,3},{2,0},{3,1},{4,6},{5,7},{6,4},{7,5},{8,10},{9,11},{10,... | collective-permute-start | bytes 786440 | tf_op jit(solution)/shard_map/ppermute | solution.py:27
  38.3 22.3 %collective-permute-start.2 = (bf16[128,1024]{1,0:T(8,128)(2,1)S(1)}, bf16[128,1024]{1,0:T(8,128)(2,1)S(1)}, u32[]{:S(2)}, u32[]{:S(2)}) collective-permute-start(bf16[128,1024]{1,0:T(8,128)(2,1)S(1)} %copy-done.8), channel_id=1, source_target_pairs={{0,3},{1,2},{2,1},{3,0},{4,7},{5,6},{6,5},{7,4},{8,11},{9,10},{10,... | collective-permute-start | bytes 786440 | tf_op jit(solution)/shard_map/ppermute | solution.py:27
  42.4 18.2 %collective-permute-start.3 = (bf16[128,1024]{1,0:T(8,128)(2,1)S(1)}, bf16[128,1024]{1,0:T(8,128)(2,1)S(1)}, u32[]{:S(2)}, u32[]{:S(2)}) collective-permute-start(bf16[128,1024]{1,0:T(8,128)(2,1)S(1)} %bitcast.60), channel_id=1, source_target_pairs={{0,4},{4,0},{8,12},{12,8},{16,20},{20,16},{24,28},{28,24},{1,5},{5... | collective-permute-start | bytes 786440 | tf_op jit(solution)/shard_map/ppermute | solution.py:27
  42.4 18.2 %collective-permute-start.5 = (bf16[128,1024]{1,0:T(8,128)(2,1)S(1)}, bf16[128,1024]{1,0:T(8,128)(2,1)S(1)}, u32[]{:S(2)}, u32[]{:S(2)}) collective-permute-start(bf16[128,1024]{1,0:T(8,128)(2,1)S(1)} %collective-permute-done.4.refs_6_), channel_id=1, source_target_pairs={{0,4},{4,0},{8,12},{12,8},{16,20},{20,16},{24,28},{28,24},{1,5},{5... | collective-permute-start | bytes 786440 | tf_op jit(solution)/shard_map/ppermute | solution.py:27
  42.9 17.7 %collective-permute-start.7 = (bf16[128,1024]{1,0:T(8,128)(2,1)S(1)}, bf16[128,1024]{1,0:T(8,128)(2,1)S(1)}, u32[]{:S(2)}, u32[]{:S(2)}) collective-permute-start(bf16[128,1024]{1,0:T(8,128)(2,1)S(1)} %collective-permute-done.6.refs_8_), channel_id=1, source_target_pairs={{0,4},{4,0},{8,12},{12,8},{16,20},{20,16},{24,28},{28,24},{1,5},{5... | collective-permute-start | bytes 786440 | tf_op jit(solution)/shard_map/ppermute | solution.py:27
  43.0 17.7 %collective-permute-start.9 = (bf16[128,1024]{1,0:T(8,128)(2,1)S(1)}, bf16[128,1024]{1,0:T(8,128)(2,1)S(1)}, u32[]{:S(2)}, u32[]{:S(2)}) collective-permute-start(bf16[128,1024]{1,0:T(8,128)(2,1)S(1)} %collective-permute-done.8.refs_10_), channel_id=1, source_target_pairs={{0,4},{4,0},{8,12},{12,8},{16,20},{20,16},{24,28},{28,24},{1,5},{5... | collective-permute-start | bytes 786440 | tf_op jit(solution)/shard_map/ppermute | solution.py:27
  67.5 18.5 %collective-permute-start.11 = (bf16[512,384]{1,0:T(8,128)(2,1)}, bf16[512,384]{1,0:T(8,128)(2,1)S(1)}, u32[]{:S(2)}, u32[]{:S(2)}) collective-permute-start(bf16[512,384]{1,0:T(8,128)(2,1)} %get-tuple-element.69.refs_0_.refs_1_), channel_id=1, source_target_pairs={{0,8},{4,12},{8,0},{12,4},{16,24},{20,28},{24,16},{28,20},{1,9},{5... | collective-permute-start | bytes 1179656 | tf_op jit(solution)/shard_map/ppermute | solution.py:27
  69.0 17.0 %collective-permute-start.13 = (bf16[512,384]{1,0:T(8,128)(2,1)}, bf16[512,384]{1,0:T(8,128)(2,1)S(1)}, u32[]{:S(2)}, u32[]{:S(2)}) collective-permute-start(bf16[512,384]{1,0:T(8,128)(2,1)} %get-tuple-element.69.refs_0_.refs_1_), channel_id=1, source_target_pairs={{0,16},{4,20},{8,24},{12,28},{16,0},{20,4},{24,8},{28,12},{1,17},{... | collective-permute-start | bytes 1179656 | tf_op jit(solution)/shard_map/ppermute | solution.py:27
  70.5 24.3 %collective-permute-start.15 = (bf16[512,384]{1,0:T(8,128)(2,1)}, bf16[512,384]{1,0:T(8,128)(2,1)S(1)}, u32[]{:S(2)}, u32[]{:S(2)}) collective-permute-start(bf16[512,384]{1,0:T(8,128)(2,1)} %get-tuple-element.69.refs_0_.refs_1_), channel_id=1, source_target_pairs={{0,24},{4,28},{8,16},{12,20},{16,8},{20,12},{24,0},{28,4},{1,25},{... | collective-permute-start | bytes 1179656 | tf_op jit(solution)/shard_map/ppermute | solution.py:27
  71.0 23.8 %collective-permute-start.10 = (bf16[512,384]{1,0:T(8,128)(2,1)}, bf16[512,384]{1,0:T(8,128)(2,1)S(1)}, u32[]{:S(2)}, u32[]{:S(2)}) collective-permute-start(bf16[512,384]{1,0:T(8,128)(2,1)} %get-tuple-element.69.refs_0_.refs_1_), channel_id=1, source_target_pairs={{0,4},{4,0},{8,12},{12,8},{16,20},{20,16},{24,28},{28,24},{1,5},{5... | collective-permute-start | bytes 1179656 | tf_op jit(solution)/shard_map/ppermute | solution.py:27
  101.4 15.0 %collective-permute-start.18 = (bf16[512,128]{1,0:T(8,128)(2,1)}, bf16[512,128]{1,0:T(8,128)(2,1)S(1)}, u32[]{:S(2)}, u32[]{:S(2)}) collective-permute-start(bf16[512,128]{1,0:T(8,128)(2,1)} %get-tuple-element.70.refs_0_.refs_8_.refs_4_), channel_id=1, source_target_pairs={{0,2},{1,3},{2,0},{3,1},{4,6},{5,7},{6,4},{7,5},{8,10},{9,11},{10,... | collective-permute-start | bytes 393224 | tf_op jit(solution)/shard_map/ppermute | solution.py:27
  104.3 19.0 %collective-permute-start.19 = (bf16[512,128]{1,0:T(8,128)(2,1)}, bf16[512,128]{1,0:T(8,128)(2,1)S(1)}, u32[]{:S(2)}, u32[]{:S(2)}) collective-permute-start(bf16[512,128]{1,0:T(8,128)(2,1)} %get-tuple-element.70.refs_0_.refs_8_.refs_4_), channel_id=1, source_target_pairs={{0,3},{1,2},{2,1},{3,0},{4,7},{5,6},{6,5},{7,4},{8,11},{9,10},{10,... | collective-permute-start | bytes 393224 | tf_op jit(solution)/shard_map/ppermute | solution.py:27
  132.4 33.3 %collective-permute-start.21 = (bf16[512,1024]{1,0:T(8,128)(2,1)}, bf16[512,1024]{1,0:T(8,128)(2,1)S(1)}, u32[]{:S(2)}, u32[]{:S(2)}) collective-permute-start(bf16[512,1024]{1,0:T(8,128)(2,1)} %get-tuple-element.73.refs_0_), channel_id=1, source_target_pairs={{0,8},{4,12},{8,0},{12,4},{16,24},{20,28},{24,16},{28,20},{1,9},{5... | collective-permute-start | bytes 3145736 | tf_op jit(solution)/shard_map/ppermute | solution.py:27
  134.5 33.9 %collective-permute-start.23 = (bf16[512,1024]{1,0:T(8,128)(2,1)}, bf16[512,1024]{1,0:T(8,128)(2,1)S(1)}, u32[]{:S(2)}, u32[]{:S(2)}) collective-permute-start(bf16[512,1024]{1,0:T(8,128)(2,1)} %get-tuple-element.73.refs_0_), channel_id=1, source_target_pairs={{0,16},{4,20},{8,24},{12,28},{16,0},{20,4},{24,8},{28,12},{1,17},{... | collective-permute-start | bytes 3145736 | tf_op jit(solution)/shard_map/ppermute | solution.py:27
  137.5 58.3 %collective-permute-start.20 = (bf16[512,1024]{1,0:T(8,128)(2,1)}, bf16[512,1024]{1,0:T(8,128)(2,1)S(1)}, u32[]{:S(2)}, u32[]{:S(2)}) collective-permute-start(bf16[512,1024]{1,0:T(8,128)(2,1)} %get-tuple-element.73.refs_0_), channel_id=1, source_target_pairs={{0,4},{4,0},{8,12},{12,8},{16,20},{20,16},{24,28},{28,24},{1,5},{5... | collective-permute-start | bytes 3145736 | tf_op jit(solution)/shard_map/ppermute | solution.py:27
  165.7 26.3 %collective-permute-start.25 = (bf16[256,1024]{1,0:T(8,128)(2,1)S(1)}, bf16[256,1024]{1,0:T(8,128)(2,1)}, u32[]{:S(2)}, u32[]{:S(2)}) collective-permute-start(bf16[256,1024]{1,0:T(8,128)(2,1)S(1)} %slice.82), channel_id=1, source_target_pairs={{0,16},{4,20},{8,24},{12,28},{16,0},{20,4},{24,8},{28,12},{1,17},{... | collective-permute-start | bytes 1572872 | tf_op jit(solution)/shard_map/ppermute | solution.py:27
  168.4 27.4 %collective-permute-start.22 = (bf16[512,1024]{1,0:T(8,128)(2,1)S(1)}, bf16[512,1024]{1,0:T(8,128)(2,1)}, u32[]{:S(2)}, u32[]{:S(2)}) collective-permute-start(bf16[512,1024]{1,0:T(8,128)(2,1)S(1)} %collective-permute-done.21.refs_2_), channel_id=1, source_target_pairs={{0,4},{4,0},{8,12},{12,8},{16,20},{20,16},{24,28},{28,24},{1,5},{5... | collective-permute-start | bytes 3145736 | tf_op jit(solution)/shard_map/ppermute | solution.py:27
  168.5 27.3 %collective-permute-start.24 = (bf16[512,1024]{1,0:T(8,128)(2,1)S(1)}, bf16[512,1024]{1,0:T(8,128)(2,1)}, u32[]{:S(2)}, u32[]{:S(2)}) collective-permute-start(bf16[512,1024]{1,0:T(8,128)(2,1)S(1)} %collective-permute-done.23.refs_4_), channel_id=1, source_target_pairs={{0,4},{4,0},{8,12},{12,8},{16,20},{20,16},{24,28},{28,24},{1,5},{5... | collective-permute-start | bytes 3145736 | tf_op jit(solution)/shard_map/ppermute | solution.py:27
  169.0 25.8 %collective-permute-start.26 = (bf16[256,1024]{1,0:T(8,128)(2,1)S(1)}, bf16[256,1024]{1,0:T(8,128)(2,1)}, u32[]{:S(2)}, u32[]{:S(2)}) collective-permute-start(bf16[256,1024]{1,0:T(8,128)(2,1)S(1)} %slice.83), channel_id=1, source_target_pairs={{0,8},{4,12},{8,0},{12,4},{16,24},{20,28},{24,16},{28,20},{1,9},{5... | collective-permute-start | bytes 1572872 | tf_op jit(solution)/shard_map/ppermute | solution.py:27
  246.6 32.8 %collective-permute-start.36 = (bf16[512,1024]{1,0:T(8,128)(2,1)}, bf16[512,1024]{1,0:T(8,128)(2,1)}, u32[]{:S(2)}, u32[]{:S(2)}) collective-permute-start(bf16[512,1024]{1,0:T(8,128)(2,1)} %get-tuple-element.83), channel_id=1, source_target_pairs={{0,4},{4,0},{8,12},{12,8},{16,20},{20,16},{24,28},{28,24},{1,5},{5... | collective-permute-start | bytes 3145736 | tf_op jit(solution)/shard_map/ppermute | solution.py:27
  251.5 26.9 %collective-permute-start.32 = (bf16[512,1024]{1,0:T(8,128)(2,1)S(1)}, bf16[512,1024]{1,0:T(8,128)(2,1)S(1)}, u32[]{:S(2)}, u32[]{:S(2)}) collective-permute-start(bf16[512,1024]{1,0:T(8,128)(2,1)S(1)} %add_convert_fusion.6.refs_1_.refs_6_), channel_id=1, source_target_pairs={{0,24},{4,28},{8,16},{12,20},{16,8},{20,12},{24,0},{28,4},{1,25},{... | collective-permute-start | bytes 3145736 | tf_op jit(solution)/shard_map/ppermute | solution.py:27
  253.2 44.6 %collective-permute-start.37 = (bf16[512,1024]{1,0:T(8,128)(2,1)}, bf16[512,1024]{1,0:T(8,128)(2,1)}, u32[]{:S(2)}, u32[]{:S(2)}) collective-permute-start(bf16[512,1024]{1,0:T(8,128)(2,1)} %get-tuple-element.85), channel_id=1, source_target_pairs={{0,4},{4,0},{8,12},{12,8},{16,20},{20,16},{24,28},{28,24},{1,5},{5... | collective-permute-start | bytes 3145736 | tf_op jit(solution)/shard_map/ppermute | solution.py:27
  254.7 45.6 %collective-permute-start.41 = (bf16[512,1024]{1,0:T(8,128)(2,1)S(1)}, bf16[512,1024]{1,0:T(8,128)(2,1)}, u32[]{:S(2)}, u32[]{:S(2)}) collective-permute-start(bf16[512,1024]{1,0:T(8,128)(2,1)S(1)} %add_convert_fusion.2.refs_5_), channel_id=1, source_target_pairs={{0,16},{4,20},{8,24},{12,28},{16,0},{20,4},{24,8},{28,12},{1,17},{... | collective-permute-start | bytes 3145736 | tf_op jit(solution)/shard_map/ppermute | solution.py:27
  257.3 43.0 %collective-permute-start.39 = (bf16[512,1024]{1,0:T(8,128)(2,1)}, bf16[512,1024]{1,0:T(8,128)(2,1)}, u32[]{:S(2)}, u32[]{:S(2)}) collective-permute-start(bf16[512,1024]{1,0:T(8,128)(2,1)} %add_convert_fusion.3.refs_4_), channel_id=1, source_target_pairs={{0,8},{4,12},{8,0},{12,4},{16,24},{20,28},{24,16},{28,20},{1,9},{5... | collective-permute-start | bytes 3145736 | tf_op jit(solution)/shard_map/ppermute | solution.py:27
  279.4 51.0 %collective-permute-start.35 = (bf16[512,1024]{1,0:T(8,128)(2,1)}, bf16[512,1024]{1,0:T(8,128)(2,1)S(1)}, u32[]{:S(2)}, u32[]{:S(2)}) collective-permute-start(bf16[512,1024]{1,0:T(8,128)(2,1)} %hold.15.refs_13_), channel_id=1, source_target_pairs={{0,16},{4,20},{8,24},{12,28},{16,0},{20,4},{24,8},{28,12},{1,17},{... | collective-permute-start | bytes 3145736 | tf_op jit(solution)/shard_map/ppermute | solution.py:27
  279.5 51.0 %collective-permute-start.33 = (bf16[512,1024]{1,0:T(8,128)(2,1)}, bf16[512,1024]{1,0:T(8,128)(2,1)S(1)}, u32[]{:S(2)}, u32[]{:S(2)}) collective-permute-start(bf16[512,1024]{1,0:T(8,128)(2,1)} %hold.13.refs_12_), channel_id=1, source_target_pairs={{0,8},{4,12},{8,0},{12,4},{16,24},{20,28},{24,16},{28,20},{1,9},{5... | collective-permute-start | bytes 3145736 | tf_op jit(solution)/shard_map/ppermute | solution.py:27
  313.3 14.1 %collective-permute-start.44 = (bf16[576,128]{1,0:T(8,128)(2,1)}, bf16[576,128]{1,0:T(8,128)(2,1)S(1)}, u32[]{:S(2)}, u32[]{:S(2)}) collective-permute-start(bf16[576,128]{1,0:T(8,128)(2,1)} %get-tuple-element.98), channel_id=1, source_target_pairs={{0,3},{1,2},{2,1},{3,0},{4,7},{5,6},{6,5},{7,4},{8,11},{9,10},{10,... | collective-permute-start | bytes 442376 | tf_op jit(solution)/shard_map/ppermute | solution.py:27
  343.0 32.0 %collective-permute-start.56 = (bf16[1280,1024]{1,0:T(8,128)(2,1)}, bf16[1280,1024]{1,0:T(8,128)(2,1)S(1)}, u32[]{:S(2)}, u32[]{:S(2)}) collective-permute-start(bf16[1280,1024]{1,0:T(8,128)(2,1)} %hold.20), channel_id=1, source_target_pairs={{0,4},{4,0},{8,12},{12,8},{16,20},{20,16},{24,28},{28,24},{1,5},{5... | collective-permute-start | bytes 7864328 | tf_op jit(solution)/shard_map/ppermute | solution.py:27
  343.1 14.3 %collective-permute-start.29 = (bf16[512,1024]{1,0:T(8,128)(2,1)}, bf16[512,1024]{1,0:T(8,128)(2,1)}, u32[]{:S(2)}, u32[]{:S(2)}) collective-permute-start(bf16[512,1024]{1,0:T(8,128)(2,1)} %get-tuple-element.75), channel_id=1, source_target_pairs={{0,4},{4,0},{8,12},{12,8},{16,20},{20,16},{24,28},{28,24},{1,5},{5... | collective-permute-start | bytes 3145736 | tf_op jit(solution)/shard_map/ppermute | solution.py:27
  343.5 26.3 %collective-permute-start.52 = (bf16[512,1024]{1,0:T(8,128)(2,1)}, bf16[512,1024]{1,0:T(8,128)(2,1)S(1)}, u32[]{:S(2)}, u32[]{:S(2)}) collective-permute-start(bf16[512,1024]{1,0:T(8,128)(2,1)} %hold.19), channel_id=1, source_target_pairs={{0,24},{4,28},{8,16},{12,20},{16,8},{20,12},{24,0},{28,4},{1,25},{... | collective-permute-start | bytes 3145736 | tf_op jit(solution)/shard_map/ppermute | solution.py:27
  387.1 28.7 %collective-permute-start.60 = (bf16[512,1024]{1,0:T(8,128)(2,1)}, bf16[512,1024]{1,0:T(8,128)(2,1)}, u32[]{:S(2)}, u32[]{:S(2)}) collective-permute-start(bf16[512,1024]{1,0:T(8,128)(2,1)} %get-tuple-element.123), channel_id=1, source_target_pairs={{0,4},{4,0},{8,12},{12,8},{16,20},{20,16},{24,28},{28,24},{1,5},{5... | collective-permute-start | bytes 3145736 | tf_op jit(solution)/shard_map/ppermute | solution.py:27
  387.9 20.7 %collective-permute-start.54 = (bf16[128,1024]{1,0:T(8,128)(2,1)}, bf16[128,1024]{1,0:T(8,128)(2,1)S(1)}, u32[]{:S(2)}, u32[]{:S(2)}) collective-permute-start(bf16[128,1024]{1,0:T(8,128)(2,1)} %get-tuple-element.107), channel_id=1, source_target_pairs={{0,2},{1,3},{2,0},{3,1},{4,6},{5,7},{6,4},{7,5},{8,10},{9,11},{10,... | collective-permute-start | bytes 786440 | tf_op jit(solution)/shard_map/ppermute | solution.py:27
  390.4 24.5 %collective-permute-start.55 = (bf16[128,1024]{1,0:T(8,128)(2,1)}, bf16[128,1024]{1,0:T(8,128)(2,1)S(1)}, u32[]{:S(2)}, u32[]{:S(2)}) collective-permute-start(bf16[128,1024]{1,0:T(8,128)(2,1)} %get-tuple-element.108), channel_id=1, source_target_pairs={{0,3},{1,2},{2,1},{3,0},{4,7},{5,6},{6,5},{7,4},{8,11},{9,10},{10,... | collective-permute-start | bytes 786440 | tf_op jit(solution)/shard_map/ppermute | solution.py:27
  391.6 28.4 %collective-permute-start.64 = (bf16[320,1024]{1,0:T(8,128)(2,1)S(1)}, bf16[320,1024]{1,0:T(8,128)(2,1)S(1)}, u32[]{:S(2)}, u32[]{:S(2)}) collective-permute-start(bf16[320,1024]{1,0:T(8,128)(2,1)S(1)} %get-tuple-element.174), channel_id=1, source_target_pairs={{0,8},{4,12},{8,0},{12,4},{16,24},{20,28},{24,16},{28,20},{1,9},{5... | collective-permute-start | bytes 1966088 | tf_op jit(solution)/shard_map/ppermute | solution.py:27
  399.2 30.6 %collective-permute-start.65 = (bf16[320,1024]{1,0:T(8,128)(2,1)S(1)}, bf16[320,1024]{1,0:T(8,128)(2,1)S(1)}, u32[]{:S(2)}, u32[]{:S(2)}) collective-permute-start(bf16[320,1024]{1,0:T(8,128)(2,1)S(1)} %get-tuple-element.176), channel_id=1, source_target_pairs={{0,16},{4,20},{8,24},{12,28},{16,0},{20,4},{24,8},{28,12},{1,17},{... | collective-permute-start | bytes 1966088 | tf_op jit(solution)/shard_map/ppermute | solution.py:27
  408.7 21.7 %collective-permute-start.66 = (bf16[320,1024]{1,0:T(8,128)(2,1)S(1)}, bf16[320,1024]{1,0:T(8,128)(2,1)S(1)}, u32[]{:S(2)}, u32[]{:S(2)}) collective-permute-start(bf16[320,1024]{1,0:T(8,128)(2,1)S(1)} %get-tuple-element.175), channel_id=1, source_target_pairs={{0,24},{4,28},{8,16},{12,20},{16,8},{20,12},{24,0},{28,4},{1,25},{... | collective-permute-start | bytes 1966088 | tf_op jit(solution)/shard_map/ppermute | solution.py:27
  415.8 36.0 %collective-permute-start.57 = (bf16[128,1024]{1,0:T(8,128)(2,1)}, bf16[128,1024]{1,0:T(8,128)(2,1)S(1)}, u32[]{:S(2)}, u32[]{:S(2)}) collective-permute-start(bf16[128,1024]{1,0:T(8,128)(2,1)} %get-tuple-element.119), channel_id=1, source_target_pairs={{0,1},{1,0},{2,3},{3,2},{4,5},{5,4},{6,7},{7,6},{8,9},{9,8},{10,11... | collective-permute-start | bytes 786440 | tf_op jit(solution)/shard_map/ppermute | solution.py:27
  415.8 37.4 %collective-permute-start.58 = (bf16[128,1024]{1,0:T(8,128)(2,1)}, bf16[128,1024]{1,0:T(8,128)(2,1)S(1)}, u32[]{:S(2)}, u32[]{:S(2)}) collective-permute-start(bf16[128,1024]{1,0:T(8,128)(2,1)} %get-tuple-element.120), channel_id=1, source_target_pairs={{0,2},{1,3},{2,0},{3,1},{4,6},{5,7},{6,4},{7,5},{8,10},{9,11},{10,... | collective-permute-start | bytes 786440 | tf_op jit(solution)/shard_map/ppermute | solution.py:27
  420.0 12.4 %collective-permute-start.61 = (bf16[128,1024]{1,0:T(8,128)(2,1)S(1)}, bf16[128,1024]{1,0:T(8,128)(2,1)S(1)}, u32[]{:S(2)}, u32[]{:S(2)}) collective-permute-start(bf16[128,1024]{1,0:T(8,128)(2,1)S(1)} %get-tuple-element.180), channel_id=1, source_target_pairs={{0,8},{4,12},{8,0},{12,4},{16,24},{20,28},{24,16},{28,20},{1,9},{5... | collective-permute-start | bytes 786440 | tf_op jit(solution)/shard_map/ppermute | solution.py:27
  429.7 12.9 %collective-permute-start.62 = (bf16[128,1024]{1,0:T(8,128)(2,1)S(1)}, bf16[128,1024]{1,0:T(8,128)(2,1)S(1)}, u32[]{:S(2)}, u32[]{:S(2)}) collective-permute-start(bf16[128,1024]{1,0:T(8,128)(2,1)S(1)} %get-tuple-element.182), channel_id=1, source_target_pairs={{0,16},{4,20},{8,24},{12,28},{16,0},{20,4},{24,8},{28,12},{1,17},{... | collective-permute-start | bytes 786440 | tf_op jit(solution)/shard_map/ppermute | solution.py:27
  430.4 14.7 %collective-permute-start.63 = (bf16[128,1024]{1,0:T(8,128)(2,1)S(1)}, bf16[128,1024]{1,0:T(8,128)(2,1)S(1)}, u32[]{:S(2)}, u32[]{:S(2)}) collective-permute-start(bf16[128,1024]{1,0:T(8,128)(2,1)S(1)} %get-tuple-element.181), channel_id=1, source_target_pairs={{0,24},{4,28},{8,16},{12,20},{16,8},{20,12},{24,0},{28,4},{1,25},{... | collective-permute-start | bytes 786440 | tf_op jit(solution)/shard_map/ppermute | solution.py:27
  432.5 20.8 %collective-permute-start.59 = (bf16[128,1024]{1,0:T(8,128)(2,1)S(1)}, bf16[128,1024]{1,0:T(8,128)(2,1)S(1)}, u32[]{:S(2)}, u32[]{:S(2)}) collective-permute-start(bf16[128,1024]{1,0:T(8,128)(2,1)S(1)} %copy-done.55), channel_id=1, source_target_pairs={{0,3},{1,2},{2,1},{3,0},{4,7},{5,6},{6,5},{7,4},{8,11},{9,10},{10,... | collective-permute-start | bytes 786440 | tf_op jit(solution)/shard_map/ppermute | solution.py:27
  446.4 20.9 %all-to-all-start.1 = ((bf16[4,32,1024]{2,1,0:T(8,128)(2,1)}), bf16[4,32,1024]{2,1,0:T(8,128)(2,1)S(1)}, u32[]{:S(2)}, u32[]{:S(2)}) async-start(bf16[4,32,1024]{2,1,0:T(8,128)(2,1)} %bitcast.11), calls=%async_computation.1 | async-start | bytes 524288 | tf_op jit(solution)/shard_map/all_to_all | solution.py:1004
  451.8 13.7 %collective-permute-start.69 = (bf16[80,1024]{1,0:T(8,128)(2,1)S(1)}, bf16[80,1024]{1,0:T(8,128)(2,1)S(1)}, u32[]{:S(2)}, u32[]{:S(2)}) collective-permute-start(bf16[80,1024]{1,0:T(8,128)(2,1)S(1)} %get-tuple-element.178), channel_id=1, source_target_pairs={{0,3},{1,2},{2,1},{3,0},{4,7},{5,6},{6,5},{7,4},{8,11},{9,10},{10,... | collective-permute-start | bytes 491528 | tf_op jit(solution)/shard_map/ppermute | solution.py:27
  (82 other events, 777.7 us)
Sparse Core Ops, SparseCore 0:
  10.9 88.6 all-gather.2
  102.9 105.8 all-gather.4

commit v3 on v2

--- a/solution.py
+++ b/solution.py
@@ -116,12 +116,22 @@
     return (valid & (from_row == rows_of_lane)).astype(BF)
 
 
-def pack_kernel(layout, q_ref, k_ref, v_ref, small_ref, ids_ref, out_ref):
+def pack_kernel(layout, q_ref, k_ref, v_ref, rv_ref, ro_ref, gain_ref, ids_ref, tok_ref, out_ref, *copies):
     size, mixed, att, head_count, gain_lane = layout
     row = lax.broadcasted_iota(jnp.int32, (LANES, LANES), 0)
     lane = lax.broadcasted_iota(jnp.int32, (LANES, LANES), 1)
-    small = small_ref[...]
-    rows = small.shape[0]
+    rows = q_ref.shape[0]
+    few = att * head_count
+    for copy in copies:
+        copy[...] = tok_ref[...]
+    small = jnp.concatenate(
+        [
+            rv_ref[...].astype(F32),
+            ro_ref[...].astype(F32),
+            gain_ref[...].astype(F32),
+            jnp.zeros((LANES - 2 * few - 1, rows), F32),
+        ]
+    ).astype(BF)
     packed = 2 * size + mixed + LANES
     for h in range(head_count):
         out_ref[h, :rows, :size] = q_ref[:, h * size : (h + 1) * size]
@@ -132,7 +142,7 @@
         source = att * head_count + att * (h ^ part) + lane % att
         source = jnp.where(lane < att, att * h + lane, source)
         source = jnp.where(lane == gain_lane, 2 * att * head_count, source)
-        tail = nn(small, select(source, lane <= gain_lane, row))
+        tail = tn(small, select(source, lane <= gain_lane, row))
         out_ref[h, :rows, 2 * size + mixed : packed] = tail.astype(BF)
 
 
@@ -154,8 +164,16 @@
         normed_ref[s * tok_rows : (s + 1) * tok_rows, :] = (normal * gain).astype(BF)
     pre = nn(normed_ref[...], all_ref[:, : 2 * size])
     cosine, sine = cos_ref[...], sin_ref[...]
-    qkv_ref[:, :size] = turn(pre[:, :size], cosine, sine).astype(BF)
-    qkv_ref[:, size : 2 * size] = turn(pre[:, size:], cosine, sine).astype(BF)
+    qkv_ref[:span, :size] = turn(pre[:, :size], cosine, sine).astype(BF)
+    qkv_ref[:span, size : 2 * size] = turn(pre[:, size:], cosine, sine).astype(BF)
+    extra = (qkv_ref.shape[0] - span) // (-(-heads // 3))
+    for s in range(heads):
+        rows = slice(span + s // 3 * extra, span + (s // 3 + 1) * extra)
+        ids = ids_ref[head ^ s, ids_ref.shape[1] - extra :, :]
+        qkv_ref[rows, s % 3 * LANES : (s % 3 + 1) * LANES] = ids
+    for s in range(heads, -(-heads // 3) * 3):
+        rows = slice(span + s // 3 * extra, span + (s // 3 + 1) * extra)
+        qkv_ref[rows, s % 3 * LANES : (s % 3 + 1) * LANES] = jnp.zeros((extra, LANES), BF)
     wide = jnp.concatenate([ref[...] for ref in tok_refs])
     marks = []
     for s in range(heads):
@@ -185,18 +203,17 @@
     values_ref[...] = expert_values
     for e in range(att):
         value += weight[:, e : e + 1] * expert_values[:, e * size : (e + 1) * size]
-    qkv_ref[:, 2 * size :] = value.astype(BF)
-
-
-def attend_kernel(groups, tok_rows, scale, at_ref, *refs):
+    qkv_ref[:span, 2 * size :] = value.astype(BF)
+
+
+def attend_kernel(groups, tok_rows, span, scale, at_ref, *refs):
     refs, (o_ref, lse_ref, top_ref, total_ref, acc_ref) = refs[:groups], refs[-5:]
-    span = refs[0].shape[0]
     size = refs[0].shape[1] // 3
     blk, head = at_ref[0], at_ref[1]
-    queries = refs[0][:, :size]
+    queries = refs[0][:span, :size]
 
     def advance(ref, first):
-        scores = nt(ref[:, size : 2 * size], queries) * scale
+        scores = nt(ref[:span, size : 2 * size], queries) * scale
         if first:
             scores = jnp.where(own_allowed(blk, head, tok_rows, span), scores, -jnp.inf)
             top = jnp.max(scores, 0, keepdims=True)
@@ -204,7 +221,7 @@
             top = jnp.maximum(top_ref[...], jnp.max(scores, 0, keepdims=True))
         weights = jnp.exp(scores - top)
         mass = jnp.sum(weights, 0, keepdims=True)
-        term = tn(ref[:, 2 * size :], weights.astype(BF))
+        term = tn(ref[:span, 2 * size :], weights.astype(BF))
         if first:
             total_ref[...] = mass
             acc_ref[...] = term
@@ -221,11 +238,11 @@
     o_ref[...] = (acc_ref[...] / total_ref[...]).T.astype(BF)
 
 
-def attend(at, qkv, tok_rows, scale, tokens):
-    span, size = qkv[0].shape[0], qkv[0].shape[1] // 3
+def attend(at, qkv, tok_rows, span, scale, tokens):
+    size = qkv[0].shape[1] // 3
     groups = len(qkv)
     return pl.pallas_call(
-        functools.partial(attend_kernel, groups, tok_rows, scale),
+        functools.partial(attend_kernel, groups, tok_rows, span, scale),
         out_shape=(shape((span, size), BF), shape((1, span), F32)),
         in_specs=[SMEM] + [VMEM] * groups + [ANY] * len(tokens),
         out_specs=(VMEM, VMEM),
@@ -240,11 +257,10 @@
     )(at, *qkv, *tokens)
 
 
-def attend_back_kernel(groups, tok_rows, scale, at_ref, *refs):
+def attend_back_kernel(groups, tok_rows, span, scale, at_ref, *refs):
     own_refs, dout_refs = refs[:groups], refs[groups : 2 * groups]
     dq_ref, dk_ref, dv_ref, dq_acc = refs[-4:]
     size = own_refs[0].shape[1] // 3
-    span = own_refs[0].shape[0]
     blk, head = at_ref[0], at_ref[1]
     parts = span // LANES
 
@@ -256,26 +272,26 @@
         return jnp.concatenate([both[i : i + 1] for i in range(parts)], axis=1)
 
     def terms(key_ref, query_ref, dout_ref, own):
-        scores = nt(key_ref[:, size : 2 * size], query_ref[:, :size]) * scale
+        scores = nt(key_ref[:span, size : 2 * size], query_ref[:span, :size]) * scale
         if own:
             scores = jnp.where(own_allowed(blk, head, tok_rows, span), scores, -jnp.inf)
         prob = jnp.exp(scores - stat(dout_ref, 0))
-        prob_grad = nt(key_ref[:, 2 * size :], dout_ref[:span, :])
+        prob_grad = nt(key_ref[:span, 2 * size :], dout_ref[:span, :])
         score_grad = prob * (prob_grad - stat(dout_ref, 1)) * scale
         return prob.astype(BF), score_grad.astype(BF)
 
     prob, grad = terms(own_refs[0], own_refs[0], dout_refs[0], True)
-    dq_acc[...] = tn(own_refs[0][:, size : 2 * size], grad)
-    dk_ref[...] = nn(grad, own_refs[0][:, :size])
+    dq_acc[...] = tn(own_refs[0][:span, size : 2 * size], grad)
+    dk_ref[...] = nn(grad, own_refs[0][:span, :size])
     dv_ref[...] = nn(prob, dout_refs[0][:span, :])
 
     def earlier(mask):
         prob, grad = terms(own_refs[mask], own_refs[0], dout_refs[0], False)
-        dq_acc[...] += tn(own_refs[mask][:, size : 2 * size], grad)
+        dq_acc[...] += tn(own_refs[mask][:span, size : 2 * size], grad)
 
     def later(mask):
         prob, grad = terms(own_refs[0], own_refs[mask], dout_refs[mask], False)
-        dk_ref[...] += nn(grad, own_refs[mask][:, :size])
+        dk_ref[...] += nn(grad, own_refs[mask][:span, :size])
         dv_ref[...] += nn(prob, dout_refs[mask][:span, :])
 
     for mask in range(1, groups):
@@ -284,11 +300,11 @@
     dq_ref[...] = dq_acc[...].T
 
 
-def attend_back(at, qkv, douts, tok_rows, scale, tokens):
-    span, size = qkv[0].shape[0], qkv[0].shape[1] // 3
+def attend_back(at, qkv, douts, tok_rows, span, scale, tokens):
+    size = qkv[0].shape[1] // 3
     groups = len(qkv)
     return pl.pallas_call(
-        functools.partial(attend_back_kernel, groups, tok_rows, scale),
+        functools.partial(attend_back_kernel, groups, tok_rows, span, scale),
         out_shape=(shape((span, size), F32),) * 3,
         in_specs=[SMEM] + [VMEM] * (2 * groups) + [ANY] * len(tokens),
         out_specs=(VMEM,) * 3,
@@ -367,22 +383,45 @@
 SLOTS = 16
 
 
-def experts_kernel(plan, heads, experts, top, at_ref, *refs):
-    chosen, far, count, tokens = plan
-    x_refs = refs[:count]
-    g_hbm, up_hbm, down_hbm, route_ref = refs[count : count + 4]
+def sub_blocks(groups, heads, tok_rows):
+    for p in range(groups):
+        for s in range(heads):
+            sub = p * heads + s
+            rows = slice(s * tok_rows, (s + 1) * tok_rows)
+            yield p, s, sub, rows, slice(sub * SLOTS, (sub + 1) * SLOTS)
+
+
+def send_back(groups, heads, tok_rows, experts, slots, back, buf, targets, sems):
+    sends = []
+    width = buf.shape[2]
+    for p, s, sub, rows, at in sub_blocks(groups, heads, tok_rows):
+        values = slots[:experts, at, :].reshape(experts * SLOTS, width)
+        buf[p, rows, :] = nn(back[sub], values).astype(BF)
+        if s == heads - 1:
+            move = pltpu.make_async_copy(buf.at[p], targets[p], sems.at[p])
+            move.start()
+            sends.append(move)
+    return sends
+
+
+def forward_kernel(plan, heads, experts, top, at_ref, *refs):
+    chosen, count = plan
     groups = len(chosen)
-    outs = refs[count + 4 + tokens :]
-    out_refs, dx_refs = outs[:groups], outs[groups : 2 * groups]
-    xs_hbm, gs_hbm, hidden_ref, da_ref = outs[2 * groups : 2 * groups + 4]
-    xbuf, gbuf, xslot, gslot, dslot, up_ref, down_ref, back, in_sem, out_sem = outs[
-        2 * groups + 4 :
+    x_refs, id_refs = refs[:count], refs[count : count + groups]
+    up_hbm, down_hbm, route_ref = refs[count + groups : count + groups + 3]
+    outs = refs[count + groups + 3 :]
+    out_refs = outs[:groups]
+    xs_hbm, hidden_hbm, act_hbm, slope_hbm, here_hbm, back_hbm, gate_ref = outs[groups : groups + 7]
+    xbuf, idbuf, xslot, hidden_ref, act_ref, slope_ref, up_ref, down_ref, here_ref, back = outs[
+        groups + 7 : groups + 17
     ]
+    in_sem, out_sem = outs[groups + 17 :]
     oslot = xbuf
-    tok_rows = gbuf.shape[2] - top
-    span, width = heads * tok_rows, xbuf.shape[2]
-    tall = tok_rows + top
+    width = xbuf.shape[2]
+    span = sum(x_refs[i].shape[0] for i in chosen[0])
+    tok_rows = span // heads
     unit = up_ref.shape[1] // experts
+    extra = idbuf.shape[1]
     arrivals = []
     sem = 0
     for p in range(groups):
@@ -394,11 +433,9 @@
             moves.append(pltpu.make_async_copy(x_refs[index], place, in_sem.at[sem]))
             row += size
             sem += 1
-        for s in range(heads):
-            device = (at_ref[0] ^ (far + p)) * heads + (at_ref[1] ^ s)
-            source = g_hbm.at[pl.ds(pl.multiple_of(device * tall, 16), tall)]
-            moves.append(pltpu.make_async_copy(source, gbuf.at[p, s], in_sem.at[sem]))
-            sem += 1
+        source = id_refs[p].at[pl.ds(span, extra)]
+        moves.append(pltpu.make_async_copy(source, idbuf.at[p], in_sem.at[sem]))
+        sem += 1
         arrivals.append(moves)
     weights = [
         pltpu.make_async_copy(up_hbm, up_ref, in_sem.at[sem]),
@@ -412,33 +449,39 @@
     later = lax.broadcasted_iota(jnp.int32, (tok_rows, tok_rows), 1)
     before = (earlier < later).astype(BF)
     place = lax.broadcasted_iota(jnp.int32, (experts, SLOTS, tok_rows), 1).astype(F32)
-    for p in range(groups):
-        for move in arrivals[p]:
-            move.wait()
-        for s in range(heads):
-            rows = slice(s * tok_rows, (s + 1) * tok_rows)
-            ids = gbuf[p, s, tok_rows:, :tok_rows].astype(F32)
-            hots = []
-            for e in range(experts):
-                met = ids == (at_ref[2] + e).astype(F32)
-                hots.append(jnp.max(met.astype(F32), 0, keepdims=True))
-            hot = jnp.concatenate(hots)
-            rank = nn(hot.astype(BF), before)
-            rank = jnp.where(hot > 0.0, rank, -1.0)
-            here = (rank[:, None, :] == place).astype(F32).reshape(experts * SLOTS, tok_rows)
-            sub = p * heads + s
-            back[sub] = here.T.astype(BF)
-            here = here.astype(BF)
-            at = slice(sub * SLOTS, (sub + 1) * SLOTS)
-            moved = nn(here, xbuf[p, rows, :]).astype(BF)
-            xslot[:experts, at, :] = moved.reshape(experts, SLOTS, width)
-            moved = nn(here, gbuf[p, s, :tok_rows, :]).astype(BF)
-            gslot[:experts, at, :] = moved.reshape(experts, SLOTS, width)
+    for p, s, sub, rows, at in sub_blocks(groups, heads, tok_rows):
+        if s == 0:
+            for move in arrivals[p]:
+                move.wait()
+        ids = idbuf[p, s // 3 * top : (s // 3 + 1) * top, s % 3 * LANES : (s % 3 + 1) * LANES]
+        ids = ids.astype(F32)
+        hots = []
+        for e in range(experts):
+            met = ids == (at_ref[2] + e).astype(F32)
+            hots.append(jnp.max(met.astype(F32), 0, keepdims=True))
+        hot = jnp.concatenate(hots)
+        rank = nn(hot.astype(BF), before)
+        rank = jnp.where(hot > 0.0, rank, -1.0)
+        here = (rank[:, None, :] == place).astype(F32).reshape(experts * SLOTS, tok_rows)
+        back[sub] = here.T.astype(BF)
+        here = here.astype(BF)
+        here_ref[sub] = here
+        moved = nn(here, xbuf[p, rows, :]).astype(BF)
+        xslot[:experts, at, :] = moved.reshape(experts, SLOTS, width)
     saves = [
-        pltpu.make_async_copy(xslot.at[pl.ds(0, experts)], xs_hbm, out_sem.at[2 * groups]),
-        pltpu.make_async_copy(gslot.at[pl.ds(0, experts)], gs_hbm, out_sem.at[2 * groups + 1]),
+        pltpu.make_async_copy(source, target, out_sem.at[groups + i])
+        for i, (source, target) in enumerate(
+            (
+                (xslot.at[pl.ds(0, experts)], xs_hbm),
+                (here_ref, here_hbm),
+                (back, back_hbm),
+                (hidden_ref, hidden_hbm),
+                (act_ref, act_hbm),
+                (slope_ref, slope_hbm),
+            )
+        )
     ]
-    for move in [*saves]:
+    for move in saves[:3]:
         move.start()
     for move in weights:
         move.wait()
@@ -446,46 +489,105 @@
     route = route_ref[...]
     held = xslot.shape[1]
     lane = lax.broadcasted_iota(jnp.int32, (held, LANES), 1)
+    gate_slopes = jnp.zeros((held, LANES), F32)
     for e in range(experts):
         cols = slice(e * unit, (e + 1) * unit)
-        x, g = xslot[e], gslot[e]
         both = jnp.concatenate([up_ref[:, cols], route], axis=1)
-        pre_all = nn(x, both)
+        pre_all = nn(xslot[e], both)
         pre, gate = pre_all[:, :unit], jax.nn.sigmoid(pre_all[:, unit + e : unit + e + 1])
-        dh = nt(g, down_ref[cols, :])
         sig = jax.nn.sigmoid(pre)
         act = pre * sig
         hidden = (act * gate).astype(BF)
-        da = (dh * gate * (sig + act * (1.0 - sig))).astype(BF)
-        dsm = jnp.sum(dh * act, -1, keepdims=True) * gate * (1.0 - gate)
+        hidden_ref[e] = hidden
+        act_ref[e] = act
+        slope_ref[e] = gate * (sig + act * (1.0 - sig))
+        gate_slopes = jnp.where(lane == e, gate * (1.0 - gate), gate_slopes)
+        oslot[e] = nn(hidden, down_ref[cols, :]).astype(BF)
+    gate_ref[...] = gate_slopes
+    for move in saves[3:]:
+        move.start()
+    saves[0].wait()
+    sends = send_back(
+        groups, heads, tok_rows, experts, oslot, back, xslot, out_refs, out_sem
+    )
+    for move in [*saves[1:], *sends]:
+        move.wait()
+
+
+def back_kernel(far, groups, heads, experts, at_ref, *refs):
+    g_hbm, up_hbm, down_hbm, act_hbm, slope_hbm, here_hbm, back_hbm = refs[:7]
+    route_ref, gate_ref = refs[7:9]
+    dx_refs, (gs_hbm, da_ref) = refs[9 : 9 + groups], refs[9 + groups : 11 + groups]
+    gbuf, gslot, dslot, act_ref, slope_ref, up_ref, down_ref, here_ref, back = refs[
+        11 + groups : 20 + groups
+    ]
+    in_sem, out_sem = refs[20 + groups :]
+    tok_rows, width = gbuf.shape[2:]
+    unit = up_ref.shape[1] // experts
+    arrivals = [
+        [
+            pltpu.make_async_copy(source, target, in_sem.at[i])
+            for i, (source, target) in enumerate(
+                (
+                    (here_hbm, here_ref),
+                    (down_hbm, down_ref),
+                    (act_hbm, act_ref),
+                    (slope_hbm, slope_ref),
+                    (up_hbm, up_ref),
+                    (back_hbm, back),
+                )
+            )
+        ]
+    ]
+    sem = len(arrivals[0])
+    for p in range(groups):
+        moves = []
+        for s in range(heads):
+            device = (at_ref[0] ^ (far + p)) * heads + (at_ref[1] ^ s)
+            source = g_hbm.at[pl.ds(pl.multiple_of(device * tok_rows, tok_rows), tok_rows)]
+            moves.append(pltpu.make_async_copy(source, gbuf.at[p, s], in_sem.at[sem]))
+            sem += 1
+        arrivals.append(moves)
+    arrivals[0][0].start()
+    for moves in arrivals[1:]:
+        for move in moves:
+            move.start()
+    for move in arrivals[0][1:]:
+        move.start()
+    arrivals[0][0].wait()
+    for p, s, sub, rows, at in sub_blocks(groups, heads, tok_rows):
+        if s == 0:
+            for move in arrivals[1 + p]:
+                move.wait()
+        moved = nn(here_ref[sub], gbuf[p, s]).astype(BF)
+        gslot[:experts, at, :] = moved.reshape(experts, SLOTS, width)
+    save = pltpu.make_async_copy(gslot.at[pl.ds(0, experts)], gs_hbm, out_sem.at[groups])
+    save.start()
+    for move in arrivals[0][1:]:
+        move.wait()
+    route = route_ref[...]
+    held = gslot.shape[1]
+    lane = lax.broadcasted_iota(jnp.int32, (held, LANES), 1)
+    for e in range(experts):
+        cols = slice(e * unit, (e + 1) * unit)
+        both = jnp.concatenate([up_ref[:, cols], route], axis=1)
+        dh = nt(gslot[e], down_ref[cols, :])
+        da = (dh * slope_ref[e]).astype(BF)
+        dsm = jnp.sum(dh * act_ref[e], -1, keepdims=True) * gate_ref[...]
         dsm = jnp.where(lane == e, dsm, 0.0).astype(BF)
         da = jnp.concatenate([da, dsm], axis=1)
-        hidden_ref[e] = hidden
         da_ref[e] = da
         dslot[e] = nt(da, both).astype(BF)
-        oslot[e] = nn(hidden, down_ref[cols, :]).astype(BF)
-    for move in saves:
-        move.wait()
-
-    sends = []
-    for which, slots, buf, target in ((0, dslot, gslot, dx_refs), (1, oslot, xslot, out_refs)):
-        for p in range(groups):
-            for s in range(heads):
-                rows = slice(s * tok_rows, (s + 1) * tok_rows)
-                sub = p * heads + s
-                at = slice(sub * SLOTS, (sub + 1) * SLOTS)
-                values = slots[:experts, at, :].reshape(experts * SLOTS, width)
-                buf[p, rows, :] = nn(back[sub], values).astype(BF)
-            move = pltpu.make_async_copy(buf.at[p], target[p], out_sem.at[which * groups + p])
-            move.start()
-            sends.append(move)
+    save.wait()
+    sends = send_back(groups, heads, tok_rows, experts, dslot, back, gslot, dx_refs, out_sem)
     for move in sends:
         move.wait()
 
 
-def run_experts(at, far, xs, g_all, up, down, route, experts, top, heads, tokens):
+def run_experts(at, far, xs, ids, g_all, up, down, route, experts, top, heads):
     groups = len(xs)
     width, units = up.shape
+    unit = units // experts
     span = sum(x.shape[0] for x in xs[0])
     tok_rows = span // heads
     held = groups * heads * SLOTS
@@ -493,35 +595,67 @@
     for arrays in xs:
         chosen.append(tuple(range(len(flat), len(flat) + len(arrays))))
         flat += arrays
-    plan = (chosen, far, len(flat), len(tokens))
     subs = groups * heads
     slots = pltpu.VMEM((max(experts, groups), max(held, span), width), BF)
-    return pl.pallas_call(
-        functools.partial(experts_kernel, plan, heads, experts, top),
-        out_shape=(shape((span, width), BF),) * (2 * groups)
-        + (shape((experts, held, width), BF),) * 2
-        + (
-            shape((experts, held, units // experts), BF),
-            shape((experts, held, units // experts + LANES), BF),
-        ),
-        in_specs=[SMEM] + [ANY] * (len(flat) + 3) + [VMEM] + [ANY] * len(tokens),
-        out_specs=(ANY,) * (2 * groups + 2) + (VMEM, VMEM),
+    dims = {
+        "rows": ((experts, held, width), BF),
+        "hidden": ((experts, held, unit), BF),
+        "wide": ((experts, held, unit), F32),
+        "here": ((subs, experts * SLOTS, tok_rows), BF),
+        "back": ((subs, tok_rows, experts * SLOTS), BF),
+    }
+    vm = {name: pltpu.VMEM(*dim) for name, dim in dims.items()}
+    hbm = {name: shape(*dim) for name, dim in dims.items()}
+    both = [pltpu.VMEM((width, units), BF), pltpu.VMEM((units, width), BF)]
+    params = pltpu.CompilerParams(vmem_limit_bytes=58 * MIB)
+    done = pl.pallas_call(
+        functools.partial(forward_kernel, (chosen, len(flat)), heads, experts, top),
+        out_shape=(shape((span, width), BF),) * groups
+        + (hbm["rows"], hbm["hidden"], hbm["wide"], hbm["wide"], hbm["here"], hbm["back"])
+        + (shape((held, LANES), F32),),
+        in_specs=[SMEM] + [ANY] * (len(flat) + groups + 2) + [VMEM],
+        out_specs=(ANY,) * (groups + 6) + (VMEM,),
         scratch_shapes=[
             slots,
-            pltpu.VMEM((groups, heads, tok_rows + top, width), BF),
+            pltpu.VMEM((groups, ids[0].shape[0] - span, ids[0].shape[1]), BF),
             slots,
+            vm["hidden"],
+            vm["wide"],
+            vm["wide"],
+            *both,
+            vm["here"],
+            vm["back"],
+            pltpu.SemaphoreType.DMA((len(flat) + groups + 2,)),
+            pltpu.SemaphoreType.DMA((groups + 6,)),
+        ],
+        compiler_params=params,
+        cost_estimate=CHEAP,
+        name="experts_forward",
+    )(at, *flat, *ids, up, down, route)
+    outs, (rows, hidden, act, slope, here, back, gates) = done[:groups], done[groups:]
+    done = pl.pallas_call(
+        functools.partial(back_kernel, far, groups, heads, experts),
+        out_shape=(shape((span, width), BF),) * groups
+        + (hbm["rows"], shape((experts, held, unit + LANES), BF)),
+        in_specs=[SMEM] + [ANY] * 7 + [VMEM, VMEM],
+        out_specs=(ANY,) * (groups + 1) + (VMEM,),
+        scratch_shapes=[
+            pltpu.VMEM((groups, heads, tok_rows, width), BF),
             slots,
-            pltpu.VMEM((experts, held, width), BF),
-            pltpu.VMEM((width, units), BF),
-            pltpu.VMEM((units, width), BF),
-            pltpu.VMEM((subs, tok_rows, experts * SLOTS), BF),
-            pltpu.SemaphoreType.DMA((len(flat) + subs + 2,)),
-            pltpu.SemaphoreType.DMA((2 * groups + 2,)),
+            vm["rows"],
+            vm["wide"],
+            vm["wide"],
+            *both,
+            vm["here"],
+            vm["back"],
+            pltpu.SemaphoreType.DMA((6 + subs,)),
+            pltpu.SemaphoreType.DMA((groups + 1,)),
         ],
-        compiler_params=pltpu.CompilerParams(vmem_limit_bytes=60 * MIB),
-        cost_estimate=CHEAP,
-        name="experts",
-    )(at, *flat, g_all, up, down, route, *tokens)
+        compiler_params=params,
+        cost_estimate=CHEAP,
+        name="experts_back",
+    )(at, g_all, up, down, act, slope, here, back, route, gates)
+    return outs, done[:groups], (rows, done[groups], hidden, done[groups + 1])
 
 
 def expert_grads_kernel(halves, *refs):
@@ -839,15 +973,6 @@
     used = 2 * size + mixed + gain_lane + 1
     packed = 2 * size + mixed + LANES
 
-    small = jnp.concatenate(
-        [
-            route_value,
-            route_output,
-            ln_gain[:, None],
-            jnp.zeros((own_rows, LANES - 2 * head_count * att - 1), BF),
-        ],
-        axis=1,
-    )
     ids_rows = 2 * named * head_count + top
     ids = jnp.concatenate(
         [
@@ -856,16 +981,23 @@
             expert_ids.T,
         ]
     )
-    by_head = pl.pallas_call(
+    by_head, second, third = pl.pallas_call(
         functools.partial(pack_kernel, layout),
-        out_shape=shape((head_count, max(own_rows, ids_rows), packed + tok_rows), BF),
-        in_specs=[VMEM] * 5,
-        out_specs=VMEM,
+        out_shape=(
+            shape((head_count, max(own_rows, ids_rows), packed + tok_rows), BF),
+            shape(tokens.shape, BF),
+            shape(tokens.shape, BF),
+        ),
+        in_specs=[VMEM] * 8,
+        out_specs=(VMEM,) * 3,
         compiler_params=PARAMS,
         name="pack",
-    )(w_query, w_key, w_value, small, ids)
-    tok_pieces = gather_head(tokens)
+    )(w_query, w_key, w_value, route_value.T, route_output.T, ln_gain[None], ids, tokens)
+    tok_pieces = [tokens, swap(tokens, "head", 1)]
     by_head = lax.all_to_all(by_head, "head", 0, 0, tiled=True)
+    third = hold(third, by_head)
+    for mask in range(2, heads):
+        tok_pieces.append(swap(second if mask == 2 else third, "head", mask))
     ids_group = by_head[:, :ids_rows, packed:]
     w_pieces = gather_blk(by_head[:, :own_rows, :packed].reshape(heads * own_rows, packed))
 
@@ -883,7 +1015,7 @@
     qkv, expert_values, gate, weight, weights, normed = pl.pallas_call(
         functools.partial(project_kernel, layout, heads, groups, named),
         out_shape=(
-            shape((span, 3 * size), BF),
+            shape((span + -(-heads // 3) * top, 3 * size), BF),
             shape((span, mixed), F32),
             shape((span, LANES), F32),
             shape((span, LANES), F32),
@@ -897,13 +1029,10 @@
         name="project",
     )(at, cosine, sine, ids_group, *tok_pieces, *w_pieces)
 
-    ids_row = jnp.pad(expert_ids.T.astype(BF), ((0, 0), (0, width - tok_rows)))
-    g_all = lax.all_gather(
-        hold(jnp.concatenate([out_grad, ids_row]), qkv), ("blk", "head"), axis=0, tiled=True
-    )
+    g_all = lax.all_gather(hold(out_grad, qkv), ("blk", "head"), axis=0, tiled=True)
 
     qkv_pieces = gather_blk(qkv)
-    mine, log_total = attend(at, qkv_pieces, tok_rows, scale, [])
+    mine, log_total = attend(at, qkv_pieces, tok_rows, span, scale, [])
     outs = gather_head(mine)
     x1, middle, mixed_heads = mix(layout, at, outs, tok_pieces, weight, wo_full, [])
 
@@ -930,20 +1059,18 @@
         xs = []
         for mask in range(0, near, 2):
             xs += [even[mask], [swap(x, "blk", 1) for x in even[mask]]]
-        done = run_experts(
-            at, far, xs, g_all, w_up, w_down, route, experts, top, heads, []
+        outs_all, dxs_all, saved = run_experts(
+            at, far, xs, qkv_pieces[far : far + near], g_all, w_up, w_down, route,
+            experts, top, heads,
         )
-        outs_all, dxs_all = done[:near], done[near : 2 * near]
         sums = [pair_sum(dxs_all, m) for m in (2, 4, 6)]
         grad_round = [dxs_all[0], swap(dxs_all[1], "blk", 1)]
         grad_round += [swap(value, "blk", m) for m, value in zip((2, 4, 6), sums)]
-        terms = expert_grads([done[2 * near :]], sums)
+        terms = expert_grads([saved], sums)
         out_sums = [hold(pair_sum(outs_all, m), sums[-1]) for m in (2, 4, 6)]
         branch_round = [outs_all[0], swap(outs_all[1], "blk", 1)]
         out_sums = [hold(value, grad_round[-1]) for value in out_sums]
-        branch_round += [swap(value, "blk", m) for m, value in zip((2, 4), out_sums)]
-        if groups > near:
-            branch_round.append(swap(out_sums[2], "blk", 6))
+        branch_round += [swap(value, "blk", m) for m, value in zip((2, 4, 6), out_sums)]
         if groups > near:
             def whole(terms):
                 return functools.reduce(lambda a, b: a + b, [t.astype(F32) for t in terms])
@@ -959,7 +1086,7 @@
         else:
             branch_terms, grad_terms, weight_grads = branch_round, grad_round, terms
     early = [*out_sums, weight_grads[2]]
-    arrived = branch_round[2:4]
+    arrived = branch_round[2:]
     if groups > near:
         branch_terms, grad_terms = [branch_terms], [grad_terms]
     grad_up, grad_down, grad_route_expert = weight_grads
@@ -969,28 +1096,32 @@
     even, odd = output_grad(at, mixed_heads, g1_low, groups)
     got = [sends[0]] + [swap(sends[m], "head", m) for m in range(1, heads)]
     dout, dso = join(got, mine, log_total, gate, weight, att, [odd])
-    dout_pieces = gather_blk(hold(dout, *arrived))
-    dq, dk, dv = attend_back(at, qkv_pieces, dout_pieces, tok_rows, scale, [])
-
-    if groups == near:
-        branch_terms = branch_terms + [swap(hold(out_sums[2], *dout_pieces), "blk", 6)]
+    dout_pieces = gather_blk(hold(dout, *arrived[:2]))
     layer_out, *outputs = branch(x1, branch_terms, heads)
+    pair_sums = add_low(even, swap(hold(odd, *arrived), "blk", 1))
+    dq, dk, dv = attend_back(
+        at, qkv_pieces, dout_pieces, tok_rows, span, scale, [outputs[0], pair_sums]
+    )
 
     out_rows = w_output.shape[0]
-    pair_sums = add_low(even, swap(hold(odd, *dout_pieces), "blk", 1))
-    pair_sums = hold(pair_sums, outputs[0]).reshape(groups // 2, heads * out_rows, width)
+    there = []
+    pair_sums = pair_sums.reshape(groups // 2, heads * out_rows, width)
     rows_sum = pair_sums[0].astype(F32)
     for index in range(1, groups // 2):
-        rows_sum = rows_sum + swap(pair_sums[index], "blk", 2 * index).astype(F32)
+        got_rows = swap(pair_sums[index], "blk", 2 * index)
+        there.append(got_rows)
+        rows_sum = rows_sum + got_rows.astype(F32)
     rows_sum = rows_sum.reshape(heads, out_rows, width)
     grad_output = lax.dynamic_index_in_dim(rows_sum, head, 0, keepdims=False)
     for mask in range(1, heads):
         part = lax.dynamic_index_in_dim(rows_sum, head ^ mask, 0, keepdims=False).astype(BF)
         grad_output = grad_output + swap(part, "head", mask).astype(F32)
-        layer_out = layer_out + swap(outputs[mask - 1], "head", mask).astype(F32)
+        got_rows = swap(outputs[mask - 1], "head", mask)
+        there.append(got_rows)
+        layer_out = layer_out + got_rows.astype(F32)
 
     grad_input, *parts, even_rows, odd_rows = finish(
-        layout, heads, groups, at, [pair_sums], dq, dk, dv, cosine, sine, expert_values, gate, weight, dso,
+        layout, heads, groups, at, there, dq, dk, dv, cosine, sine, expert_values, gate, weight, dso,
         normed, weights, g1, *tok_pieces,
     )
     pairs = add_low(even_rows, swap(odd_rows, "blk", 1))

time: 487 us -> 465 us (0.955)
  the two profiles are of different devices: /device:TPU:8 before, /device:TPU:0 now
where the time goes in v3:
time: 465 us; the launch traced here: 457 us
  waiting for transfers between devices  207 us (45%)
  Pallas kernels  117 us (25%)
  starting transfers between devices  82.1 us (18%)
  other arithmetic  21.4 us (5%)
  between operations  15 us (3%)
  local copies, waits for them, and re-layouts  14 us (3%)
    ppermute x70, waiting for transfers between devices, swap(): return lax.ppermute(value, axis, [(i, i ^ mask) for i in range(size)])  199 us
    ppermute x70, starting transfers between devices, swap(): return lax.ppermute(value, axis, [(i, i ^ mask) for i in range(size)])  72.1 us
    pallas_call x1, Pallas kernels, run_experts(): pl.pallas_call(functools.partial(forward_kernel, (chosen, len(flat)), hea...  20.7 us
    pallas_call x1, Pallas kernels, run_experts(): pl.pallas_call(functools.partial(back_kernel, far, groups, heads, experts...  19.3 us
    pallas_call x1, Pallas kernels, expert_grads(): pl.pallas_call(functools.partial(expert_grads_kernel, halves), grid=(expe...  13.4 us
    pallas_call x1, Pallas kernels, spread(): pl.pallas_call(functools.partial(spread_kernel, layout, heads, len(terms)...  10.5 us
    convert_element_type x8, other arithmetic, add_low(): return (left.astype(F32) + right.astype(F32)).astype(BF)  10.1 us
    pallas_call x1, Pallas kernels, attend_back(): pl.pallas_call(functools.partial(attend_back_kernel, groups, tok_rows, sp...  9.96 us
  transfers between devices with their start and end apart: 74, of which 34 were waited for; matrix products, arithmetic and copies ran while one was open for 5% of the time, Pallas kernels for 24%

profile of v3, /device:TPU:0, one launch (start us, length us, event | category | flops | bytes accessed | tf_op | source)
XLA Modules:
  0.0 457.2 jit_solution(13770938665312414087)
XLA Ops:
  11.4 6.3 %all-to-all-start = ((bf16[4,32,1152]{2,1,0:T(8,128)(2,1)}), bf16[4,32,1152]{2,1,0:T(8,128)(2,1)S(1)}, u32[]{:S(2)}, u32[]{:S(2)}) async-start(bf16[4,32,1152]{2,1,0:T(8,128)(2,1)} %get-tuple-element.77), calls=%async_computation | async-start | bytes 589824 | tf_op jit(solution)/shard_map/all_to_all | solution.py:997
  19.7 2.4 collective-permute-start.1
  22.1 7.5 %all-to-all-done.refs_1_ = bf16[4,32,1152]{2,1,0:T(8,128)(2,1)S(1)} async-done(((bf16[4,32,1152]{2,1,0:T(8,128)(2,1)}), bf16[4,32,1152]{2,1,0:T(8,128)(2,1)S(1)}, u32[]{:S(2)}, u32[]{:S(2)}) %all-to-all-start) | async-done | bytes 294944 | tf_op jit(solution)/shard_map/all_to_all | solution.py:997
  29.6 2.6 collective-permute-start.8
  33.2 5.6 %collective-permute-done.refs_1_.refs_5_.refs_13_ = bf16[128,1024]{1,0:T(8,128)(2,1)S(1)} collective-permute-done((bf16[128,1024]{1,0:T(8,128)(2,1)}, bf16[128,1024]{1,0:T(8,128)(2,1)S(1)}, u32[]{:S(2)}, u32[]{:S(2)}) %collective-permute-start) | collective-permute-done | bytes 262176 | tf_op jit(solution)/shard_map/ppermute | solution.py:27
  38.8 3.2 collective-permute-done.1.refs_2_.refs_6_.refs_14_
  48.8 4.9 %collective-permute-done.2.refs_3_.refs_7_.refs_15_ = bf16[128,1024]{1,0:T(8,128)(2,1)S(1)} collective-permute-done((bf16[128,1024]{1,0:T(8,128)(2,1)}, bf16[128,1024]{1,0:T(8,128)(2,1)S(1)}, u32[]{:S(2)}, u32[]{:S(2)}) %collective-permute-start.2) | collective-permute-done | bytes 262176 | tf_op jit(solution)/shard_map/ppermute | solution.py:27
  54.4 5.8 %project.1 = (bf16[544,384]{1,0:T(8,128)(2,1)}, f32[512,640]{1,0:T(8,128)}, f32[512,128]{1,0:T(8,128)}, f32[512,128]{1,0:T(8,128)}, bf16[1024,1024]{1,0:T(8,128)(2,1)}, /*index=5*/bf16[512,1024]{1,0:T(8,128)(2,1)}) custom-call(s32[3]{0:T(128)} %pad_add_fusion.1.at_ref, f32[512,128]{1,0:T(8,128)} %get-tuple-element.206.cos_ref.refs_3_, ...), custom_call_target="tpu_custom_call" | custom-call | tf_op jit(solution)/shard_map/project/pallas_call | solution.py:1015
  60.2 2.5 collective-permute-start.15
  63.8 15.9 %collective-permute-done.15.refs_6_.refs_16_ = bf16[544,384]{1,0:T(8,128)(2,1)S(1)} collective-permute-done((bf16[544,384]{1,0:T(8,128)(2,1)}, bf16[544,384]{1,0:T(8,128)(2,1)S(1)}, u32[]{:S(2)}, u32[]{:S(2)}) %collective-permute-start.15) | collective-permute-done | bytes 417824 | tf_op jit(solution)/shard_map/ppermute | solution.py:27
  79.7 6.7 %collective-permute-done.13.refs_4_.refs_14_ = bf16[544,384]{1,0:T(8,128)(2,1)S(1)} collective-permute-done((bf16[544,384]{1,0:T(8,128)(2,1)}, bf16[544,384]{1,0:T(8,128)(2,1)S(1)}, u32[]{:S(2)}, u32[]{:S(2)}) %collective-permute-start.13) | collective-permute-done | bytes 417824 | tf_op jit(solution)/shard_map/ppermute | solution.py:27
  90.3 4.0 attend.1
  94.3 4.3 collective-permute-start.19
  98.5 6.4 %collective-permute-start.18 = (bf16[512,128]{1,0:T(8,128)(2,1)}, bf16[512,128]{1,0:T(8,128)(2,1)S(1)}, u32[]{:S(2)}, u32[]{:S(2)}) collective-permute-start(bf16[512,128]{1,0:T(8,128)(2,1)} %get-tuple-element.81.refs_0_.refs_8_.refs_4_), channel_id=1, source_target_pairs={{0,2},{1,3},{2,0},{3,1},{4,6},{5,7},{6,4},{7,5},{8,10},{9,11},{10,... | collective-permute-start | bytes 393224 | tf_op jit(solution)/shard_map/ppermute | solution.py:27
  104.9 10.2 %collective-permute-done.18.refs_2_.refs_10_ = bf16[512,128]{1,0:T(8,128)(2,1)S(1)} collective-permute-done((bf16[512,128]{1,0:T(8,128)(2,1)}, bf16[512,128]{1,0:T(8,128)(2,1)S(1)}, u32[]{:S(2)}, u32[]{:S(2)}) %collective-permute-start.18) | collective-permute-done | bytes 131104 | tf_op jit(solution)/shard_map/ppermute | solution.py:27
  115.8 8.4 %mix.1 = (f32[128,1024]{1,0:T(8,128)}, bf16[512,1024]{1,0:T(8,128)(2,1)}, bf16[512,2560]{1,0:T(8,128)(2,1)}) custom-call(s32[3]{0:T(128)} %pad_add_fusion.1.at_ref, bf16[512,128]{1,0:T(8,128)(2,1)} %get-tuple-element.81.refs_0_.refs_8_.refs_4_, bf16[512,128]{1,0:T(8,128)(2,1)} %copy-done.43, bf16[512,128]{1,0:T(8,128)(2,1)} %copy-done.42, ...), custom_call_target="tpu_custom_call" | custom-call | tf_op jit(solution)/shard_map/mix/pallas_call | solution.py:359
  124.2 6.2 %collective-permute-start.23 = (bf16[512,1024]{1,0:T(8,128)(2,1)}, bf16[512,1024]{1,0:T(8,128)(2,1)S(1)}, u32[]{:S(2)}, u32[]{:S(2)}) collective-permute-start(bf16[512,1024]{1,0:T(8,128)(2,1)} %get-tuple-element.84.refs_0_), channel_id=1, source_target_pairs={{0,16},{4,20},{8,24},{12,28},{16,0},{20,4},{24,8},{28,12},{1,17},{... | collective-permute-start | bytes 3145736 | tf_op jit(solution)/shard_map/ppermute | solution.py:27
  130.4 2.6 collective-permute-start.21
  133.0 24.5 %collective-permute-done.23.refs_4_ = bf16[512,1024]{1,0:T(8,128)(2,1)S(1)} collective-permute-done((bf16[512,1024]{1,0:T(8,128)(2,1)}, bf16[512,1024]{1,0:T(8,128)(2,1)S(1)}, u32[]{:S(2)}, u32[]{:S(2)}) %collective-permute-start.23) | collective-permute-done | bytes 1048608 | tf_op jit(solution)/shard_map/ppermute | solution.py:27
  157.5 2.7 collective-permute-start.26
  160.3 4.9 %collective-permute-done.21.refs_2_ = bf16[512,1024]{1,0:T(8,128)(2,1)S(1)} collective-permute-done((bf16[512,1024]{1,0:T(8,128)(2,1)}, bf16[512,1024]{1,0:T(8,128)(2,1)S(1)}, u32[]{:S(2)}, u32[]{:S(2)}) %collective-permute-start.21) | collective-permute-done | bytes 1048608 | tf_op jit(solution)/shard_map/ppermute | solution.py:27
  165.7 21.8 %collective-permute-done.26.refs_7_ = bf16[256,1024]{1,0:T(8,128)(2,1)} collective-permute-done((bf16[256,1024]{1,0:T(8,128)(2,1)S(1)}, bf16[256,1024]{1,0:T(8,128)(2,1)}, u32[]{:S(2)}, u32[]{:S(2)}) %collective-permute-start.26) | collective-permute-done | bytes 524320 | tf_op jit(solution)/shard_map/ppermute | solution.py:27
  191.0 20.7 %experts_forward.1 = (bf16[512,1024]{1,0:T(8,128)(2,1)}, bf16[512,1024]{1,0:T(8,128)(2,1)}, bf16[512,1024]{1,0:T(8,128)(2,1)}, bf16[512,1024]{1,0:T(8,128)(2,1)}...) custom-call(s32[3]{0:T(128)} %pad_add_fusion.1.at_ref, ...), custom_call_target="tpu_custom_call" | custom-call | tf_op jit(solution)/shard_map/experts_forward/pallas_call | solution.py:611
  211.8 19.3 %experts_back.1 = (bf16[512,1024]{1,0:T(8,128)(2,1)}, bf16[512,1024]{1,0:T(8,128)(2,1)}, bf16[512,1024]{1,0:T(8,128)(2,1)}, bf16[512,1024]{1,0:T(8,128)(2,1)}, b...) custom-call(s32[3]{0:T(128)} %pad_add_fusion.1.at_ref, ...), custom_call_target="tpu_custom_call" | custom-call | tf_op jit(solution)/shard_map/experts_back/pallas_call | solution.py:636
  245.6 18.2 %collective-permute-done.32.refs_1_.refs_4_ = bf16[512,1024]{1,0:T(8,128)(2,1)S(1)} collective-permute-done((bf16[512,1024]{1,0:T(8,128)(2,1)S(1)}, bf16[512,1024]{1,0:T(8,128)(2,1)S(1)}, u32[]{:S(2)}, u32[]{:S(2)}) %collective-permute-start.32) | collective-permute-done | bytes 1048608 | tf_op jit(solution)/shard_map/ppermute | solution.py:27
  268.3 13.4 %expert_grads.1 = (f32[1024,1024]{1,0:T(8,128)}, f32[1024,1024]{1,0:T(8,128)}, f32[1024,128]{1,0:T(8,128)}) custom-call(bf16[8,512,1024]{2,1,0:T(8,128)(2,1)} %get-tuple-element.110.refs_0_, bf16[8,512,1024]{2,1,0:T(8,128)(2,1)} %get-tuple-element.111.refs_1_, bf16[8,512,128]{2,1,0:T(8,128)(2,1)} %get-tuple-element.112.refs_2_, ...), custom_call_target="tpu_custom_call" | custom-call | tf_op jit(solution)/shard_map/expert_grads/pallas_call | solution.py:694
  281.7 3.5 collective-permute-done.43.refs_2_
  285.6 10.5 %spread.1 = (f32[512,1024]{1,0:T(8,128)}, bf16[512,1024]{1,0:T(8,128)(2,1)}, bf16[576,128]{1,0:T(8,128)(2,1)}, bf16[576,128]{1,0:T(8,128)(2,1)}, bf16[576,128]{1,0:T(8,128)(2,1)}, /*index=5*/bf16[576,128]{1,0:T(8,128)(2,1)}) custom-call(s32[3]{0:T(128)} %pad_add_fusion.1.at_ref, bf16[512,1024]{1,0:T(8,128)(2,1)} %get-tuple-element.104.refs_0_, ...), custom_call_target="tpu_custom_call" | custom-call | tf_op jit(solution)/shard_map/spread/pallas_call | solution.py:756
  296.1 3.6 collective-permute-start.47
  299.8 5.2 %collective-permute-done.46.refs_1_ = bf16[576,128]{1,0:T(8,128)(2,1)S(1)} collective-permute-done((bf16[576,128]{1,0:T(8,128)(2,1)}, bf16[576,128]{1,0:T(8,128)(2,1)S(1)}, u32[]{:S(2)}, u32[]{:S(2)}) %collective-permute-start.46) | collective-permute-done | bytes 147488 | tf_op jit(solution)/shard_map/ppermute | solution.py:27
  306.4 7.4 %output_grad.1 = (bf16[1280,1024]{1,0:T(8,128)(2,1)}, bf16[1280,1024]{1,0:T(8,128)(2,1)}) custom-call(s32[3]{0:T(128)} %pad_add_fusion.1.at_ref, bf16[512,2560]{1,0:T(8,128)(2,1)} %get-tuple-element.121.u_ref, bf16[512,1024]{1,0:T(8,128)(2,1)} %get-tuple-element.122.g_ref), custom_call_target="tpu_custom_call" | custom-call | tf_op jit(solution)/shard_map/output_grad/pallas_call | solution.py:824
  314.5 2.4 join.1
  316.9 13.6 %collective-permute-done.37.refs_5_.refs_3_ = bf16[512,1024]{1,0:T(8,128)(2,1)} collective-permute-done((bf16[512,1024]{1,0:T(8,128)(2,1)}, bf16[512,1024]{1,0:T(8,128)(2,1)}, u32[]{:S(2)}, u32[]{:S(2)}) %collective-permute-start.37) | collective-permute-done | bytes 1048608 | tf_op jit(solution)/shard_map/ppermute | solution.py:27
  334.5 2.2 collective-permute-done.29.refs_2_
  337.7 4.2 branch.1
  343.7 3.0 add_convert_fusion.refs_17_
  346.9 2.2 collective-permute-start.59
  350.9 6.3 %collective-permute-done.39.refs_20_ = bf16[128,1024]{1,0:T(8,128)(2,1)S(1)} collective-permute-done((bf16[128,1024]{1,0:T(8,128)(2,1)}, bf16[128,1024]{1,0:T(8,128)(2,1)S(1)}, u32[]{:S(2)}, u32[]{:S(2)}) %collective-permute-start.39) | collective-permute-done | bytes 262176 | tf_op jit(solution)/shard_map/ppermute | solution.py:27
  358.6 2.7 collective-permute-start.40
  362.0 10.0 %attend_back.1 = (f32[512,128]{1,0:T(8,128)}, f32[512,128]{1,0:T(8,128)}, f32[512,128]{1,0:T(8,128)}) custom-call(s32[3]{0:T(128)} %pad_add_fusion.1.at_ref, bf16[544,384]{1,0:T(8,128)(2,1)} %get-tuple-element.80.refs_0_.refs_10_.refs_1_, bf16[544,384]{1,0:T(8,128)(2,1)} %copy-done.9, bf16[544,384]{1,0:T(8,128)(2,1)} %copy-done.8, ...), custom_call_target="tpu_custom_call" | custom-call | tf_op jit(solution)/shard_map/attend_back/pallas_call | solution.py:306
  372.0 2.7 collective-permute-done.38.refs_19_
  374.7 4.0 collective-permute-done.58.refs_17_
  379.8 9.1 %finish.1 = (f32[128,1024]{1,0:T(8,128)}, bf16[128,1024]{1,0:T(8,128)(2,1)}, bf16[128,1024]{1,0:T(8,128)(2,1)}, bf16[128,1024]{1,0:T(8,128)(2,1)}, bf16[512,1024]{1,0:T(8,128)(2,1)}, /*index=5*/bf16[512,1024]{1,0:T(8,128)(2,1)}) custom-call(s32[3]{0:T(128)} %pad_add_fusion.1.at_ref, f32[512,128]{1,0:T(8,128)} %get-tuple-element.126.refs_0_, ...), custom_call_target="tpu_custom_call" | custom-call | tf_op jit(solution)/shard_map/finish/pallas_call | solution.py:926
  400.2 3.4 collective-permute-done.64
  404.4 4.4 collective-permute-done.66
  411.7 3.6 all-to-all-start.1
  415.3 7.7 %collective-permute-done.69 = bf16[80,1024]{1,0:T(8,128)(2,1)S(1)} collective-permute-done((bf16[80,1024]{1,0:T(8,128)(2,1)S(1)}, bf16[80,1024]{1,0:T(8,128)(2,1)S(1)}, u32[]{:S(2)}, u32[]{:S(2)}) %collective-permute-start.69) | collective-permute-done | bytes 163872 | tf_op jit(solution)/shard_map/ppermute | solution.py:27
  423.0 20.2 %collective-permute-done.68 = bf16[80,1024]{1,0:T(8,128)(2,1)} collective-permute-done((bf16[80,1024]{1,0:T(8,128)(2,1)S(1)}, bf16[80,1024]{1,0:T(8,128)(2,1)}, u32[]{:S(2)}, u32[]{:S(2)}) %collective-permute-start.68) | collective-permute-done | bytes 163872 | tf_op jit(solution)/shard_map/ppermute | solution.py:27
  (293 shorter events, 79.3 us)
Async XLA Ops:
  7.2 107.9 %all-gather.3.cloned.1.call-start = ((), (), s32[]{:S(2)}) async-start(), calls=%async_computation.2 | async-start | bytes 5406720 | tf_op jit(solution)/shard_map/all_gather | solution.py:1004
  11.4 18.2 %all-to-all-start = ((bf16[4,32,1152]{2,1,0:T(8,128)(2,1)}), bf16[4,32,1152]{2,1,0:T(8,128)(2,1)S(1)}, u32[]{:S(2)}, u32[]{:S(2)}) async-start(bf16[4,32,1152]{2,1,0:T(8,128)(2,1)} %get-tuple-element.77), calls=%async_computation | async-start | bytes 589824 | tf_op jit(solution)/shard_map/all_to_all | solution.py:997
  17.7 194.1 %all-gather.5.cloned.1.call-start = ((), (), s32[]{:S(2)}) async-start(), calls=%async_computation.3 | async-start | bytes 8650752 | tf_op jit(solution)/shard_map/all_gather | solution.py:1032
  17.7 21.1 %collective-permute-start = (bf16[128,1024]{1,0:T(8,128)(2,1)}, bf16[128,1024]{1,0:T(8,128)(2,1)S(1)}, u32[]{:S(2)}, u32[]{:S(2)}) collective-permute-start(bf16[128,1024]{1,0:T(8,128)(2,1)} %refs_12_.1), channel_id=1, source_target_pairs={{0,1},{1,0},{2,3},{3,2},{4,5},{5,4},{6,7},{7,6},{8,9},{9,8},{10,11... | collective-permute-start | bytes 786440 | tf_op jit(solution)/shard_map/ppermute | solution.py:27
  19.7 22.3 %collective-permute-start.1 = (bf16[128,1024]{1,0:T(8,128)(2,1)}, bf16[128,1024]{1,0:T(8,128)(2,1)S(1)}, u32[]{:S(2)}, u32[]{:S(2)}) collective-permute-start(bf16[128,1024]{1,0:T(8,128)(2,1)} %get-tuple-element.78), channel_id=1, source_target_pairs={{0,2},{1,3},{2,0},{3,1},{4,6},{5,7},{6,4},{7,5},{8,10},{9,11},{10,... | collective-permute-start | bytes 786440 | tf_op jit(solution)/shard_map/ppermute | solution.py:27
  29.6 13.9 %collective-permute-start.8 = (bf16[128,1024]{1,0:T(8,128)(2,1)S(1)}, bf16[128,1024]{1,0:T(8,128)(2,1)S(1)}, u32[]{:S(2)}, u32[]{:S(2)}) collective-permute-start(bf16[128,1024]{1,0:T(8,128)(2,1)S(1)} %bitcast.56), channel_id=1, source_target_pairs={{0,24},{4,28},{8,16},{12,20},{16,8},{20,12},{24,0},{28,4},{1,25},{... | collective-permute-start | bytes 786440 | tf_op jit(solution)/shard_map/ppermute | solution.py:27
  42.0 11.7 %collective-permute-start.2 = (bf16[128,1024]{1,0:T(8,128)(2,1)}, bf16[128,1024]{1,0:T(8,128)(2,1)S(1)}, u32[]{:S(2)}, u32[]{:S(2)}) collective-permute-start(bf16[128,1024]{1,0:T(8,128)(2,1)} %hold.10), channel_id=1, source_target_pairs={{0,3},{1,2},{2,1},{3,0},{4,7},{5,6},{6,5},{7,4},{8,11},{9,10},{10,... | collective-permute-start | bytes 786440 | tf_op jit(solution)/shard_map/ppermute | solution.py:27
  60.2 19.5 %collective-permute-start.15 = (bf16[544,384]{1,0:T(8,128)(2,1)}, bf16[544,384]{1,0:T(8,128)(2,1)S(1)}, u32[]{:S(2)}, u32[]{:S(2)}) collective-permute-start(bf16[544,384]{1,0:T(8,128)(2,1)} %get-tuple-element.80.refs_0_.refs_10_.refs_1_), channel_id=1, source_target_pairs={{0,24},{4,28},{8,16},{12,20},{16,8},{20,12},{24,0},{28,4},{1,25},{... | collective-permute-start | bytes 1253384 | tf_op jit(solution)/shard_map/ppermute | solution.py:27
  62.7 23.7 %collective-permute-start.13 = (bf16[544,384]{1,0:T(8,128)(2,1)}, bf16[544,384]{1,0:T(8,128)(2,1)S(1)}, u32[]{:S(2)}, u32[]{:S(2)}) collective-permute-start(bf16[544,384]{1,0:T(8,128)(2,1)} %get-tuple-element.80.refs_0_.refs_10_.refs_1_), channel_id=1, source_target_pairs={{0,16},{4,20},{8,24},{12,28},{16,0},{20,4},{24,8},{28,12},{1,17},{... | collective-permute-start | bytes 1253384 | tf_op jit(solution)/shard_map/ppermute | solution.py:27
  63.2 24.5 %collective-permute-start.11 = (bf16[544,384]{1,0:T(8,128)(2,1)}, bf16[544,384]{1,0:T(8,128)(2,1)S(1)}, u32[]{:S(2)}, u32[]{:S(2)}) collective-permute-start(bf16[544,384]{1,0:T(8,128)(2,1)} %get-tuple-element.80.refs_0_.refs_10_.refs_1_), channel_id=1, source_target_pairs={{0,8},{4,12},{8,0},{12,4},{16,24},{20,28},{24,16},{28,20},{1,9},{5... | collective-permute-start | bytes 1253384 | tf_op jit(solution)/shard_map/ppermute | solution.py:27
  63.8 24.0 %collective-permute-start.10 = (bf16[544,384]{1,0:T(8,128)(2,1)}, bf16[544,384]{1,0:T(8,128)(2,1)S(1)}, u32[]{:S(2)}, u32[]{:S(2)}) collective-permute-start(bf16[544,384]{1,0:T(8,128)(2,1)} %get-tuple-element.80.refs_0_.refs_10_.refs_1_), channel_id=1, source_target_pairs={{0,4},{4,0},{8,12},{12,8},{16,20},{20,16},{24,28},{28,24},{1,5},{5... | collective-permute-start | bytes 1253384 | tf_op jit(solution)/shard_map/ppermute | solution.py:27
  98.5 16.5 %collective-permute-start.18 = (bf16[512,128]{1,0:T(8,128)(2,1)}, bf16[512,128]{1,0:T(8,128)(2,1)S(1)}, u32[]{:S(2)}, u32[]{:S(2)}) collective-permute-start(bf16[512,128]{1,0:T(8,128)(2,1)} %get-tuple-element.81.refs_0_.refs_8_.refs_4_), channel_id=1, source_target_pairs={{0,2},{1,3},{2,0},{3,1},{4,6},{5,7},{6,4},{7,5},{8,10},{9,11},{10,... | collective-permute-start | bytes 393224 | tf_op jit(solution)/shard_map/ppermute | solution.py:27
  124.2 33.3 %collective-permute-start.23 = (bf16[512,1024]{1,0:T(8,128)(2,1)}, bf16[512,1024]{1,0:T(8,128)(2,1)S(1)}, u32[]{:S(2)}, u32[]{:S(2)}) collective-permute-start(bf16[512,1024]{1,0:T(8,128)(2,1)} %get-tuple-element.84.refs_0_), channel_id=1, source_target_pairs={{0,16},{4,20},{8,24},{12,28},{16,0},{20,4},{24,8},{28,12},{1,17},{... | collective-permute-start | bytes 3145736 | tf_op jit(solution)/shard_map/ppermute | solution.py:27
  130.4 34.8 %collective-permute-start.21 = (bf16[512,1024]{1,0:T(8,128)(2,1)}, bf16[512,1024]{1,0:T(8,128)(2,1)S(1)}, u32[]{:S(2)}, u32[]{:S(2)}) collective-permute-start(bf16[512,1024]{1,0:T(8,128)(2,1)} %get-tuple-element.84.refs_0_), channel_id=1, source_target_pairs={{0,8},{4,12},{8,0},{12,4},{16,24},{20,28},{24,16},{28,20},{1,9},{5... | collective-permute-start | bytes 3145736 | tf_op jit(solution)/shard_map/ppermute | solution.py:27
  133.0 56.6 %collective-permute-start.20 = (bf16[512,1024]{1,0:T(8,128)(2,1)}, bf16[512,1024]{1,0:T(8,128)(2,1)S(1)}, u32[]{:S(2)}, u32[]{:S(2)}) collective-permute-start(bf16[512,1024]{1,0:T(8,128)(2,1)} %get-tuple-element.84.refs_0_), channel_id=1, source_target_pairs={{0,4},{4,0},{8,12},{12,8},{16,20},{20,16},{24,28},{28,24},{1,5},{5... | collective-permute-start | bytes 3145736 | tf_op jit(solution)/shard_map/ppermute | solution.py:27
  157.5 30.0 %collective-permute-start.26 = (bf16[256,1024]{1,0:T(8,128)(2,1)S(1)}, bf16[256,1024]{1,0:T(8,128)(2,1)}, u32[]{:S(2)}, u32[]{:S(2)}) collective-permute-start(bf16[256,1024]{1,0:T(8,128)(2,1)S(1)} %slice.83), channel_id=1, source_target_pairs={{0,8},{4,12},{8,0},{12,4},{16,24},{20,28},{24,16},{28,20},{1,9},{5... | collective-permute-start | bytes 1572872 | tf_op jit(solution)/shard_map/ppermute | solution.py:27
  160.3 29.4 %collective-permute-start.24 = (bf16[512,1024]{1,0:T(8,128)(2,1)S(1)}, bf16[512,1024]{1,0:T(8,128)(2,1)}, u32[]{:S(2)}, u32[]{:S(2)}) collective-permute-start(bf16[512,1024]{1,0:T(8,128)(2,1)S(1)} %collective-permute-done.23.refs_4_), channel_id=1, source_target_pairs={{0,4},{4,0},{8,12},{12,8},{16,20},{20,16},{24,28},{28,24},{1,5},{5... | collective-permute-start | bytes 3145736 | tf_op jit(solution)/shard_map/ppermute | solution.py:27
  165.2 24.4 %collective-permute-start.22 = (bf16[512,1024]{1,0:T(8,128)(2,1)S(1)}, bf16[512,1024]{1,0:T(8,128)(2,1)}, u32[]{:S(2)}, u32[]{:S(2)}) collective-permute-start(bf16[512,1024]{1,0:T(8,128)(2,1)S(1)} %collective-permute-done.21.refs_2_), channel_id=1, source_target_pairs={{0,4},{4,0},{8,12},{12,8},{16,20},{20,16},{24,28},{28,24},{1,5},{5... | collective-permute-start | bytes 3145736 | tf_op jit(solution)/shard_map/ppermute | solution.py:27
  165.3 23.4 %collective-permute-start.25 = (bf16[256,1024]{1,0:T(8,128)(2,1)S(1)}, bf16[256,1024]{1,0:T(8,128)(2,1)}, u32[]{:S(2)}, u32[]{:S(2)}) collective-permute-start(bf16[256,1024]{1,0:T(8,128)(2,1)S(1)} %slice.82), channel_id=1, source_target_pairs={{0,16},{4,20},{8,24},{12,28},{16,0},{20,4},{24,8},{28,12},{1,17},{... | collective-permute-start | bytes 1572872 | tf_op jit(solution)/shard_map/ppermute | solution.py:27
  211.6 20.6 %collective-permute-start.30 = (bf16[512,1024]{1,0:T(8,128)(2,1)}, bf16[512,1024]{1,0:T(8,128)(2,1)S(1)}, u32[]{:S(2)}, u32[]{:S(2)}) collective-permute-start(bf16[512,1024]{1,0:T(8,128)(2,1)} %get-tuple-element.88), channel_id=1, source_target_pairs={{0,4},{4,0},{8,12},{12,8},{16,20},{20,16},{24,28},{28,24},{1,5},{5... | collective-permute-start | bytes 3145736 | tf_op jit(solution)/shard_map/ppermute | solution.py:27
  232.1 12.1 %collective-permute-start.36 = (bf16[512,1024]{1,0:T(8,128)(2,1)}, bf16[512,1024]{1,0:T(8,128)(2,1)S(1)}, u32[]{:S(2)}, u32[]{:S(2)}) collective-permute-start(bf16[512,1024]{1,0:T(8,128)(2,1)} %get-tuple-element.99), channel_id=1, source_target_pairs={{0,4},{4,0},{8,12},{12,8},{16,20},{20,16},{24,28},{28,24},{1,5},{5... | collective-permute-start | bytes 3145736 | tf_op jit(solution)/shard_map/ppermute | solution.py:27
  234.7 32.1 %collective-permute-start.41 = (bf16[512,1024]{1,0:T(8,128)(2,1)}, bf16[512,1024]{1,0:T(8,128)(2,1)}, u32[]{:S(2)}, u32[]{:S(2)}) collective-permute-start(bf16[512,1024]{1,0:T(8,128)(2,1)} %get-tuple-element.105), channel_id=1, source_target_pairs={{0,4},{4,0},{8,12},{12,8},{16,20},{20,16},{24,28},{28,24},{1,5},{5... | collective-permute-start | bytes 3145736 | tf_op jit(solution)/shard_map/ppermute | solution.py:27
  236.9 26.9 %collective-permute-start.32 = (bf16[512,1024]{1,0:T(8,128)(2,1)S(1)}, bf16[512,1024]{1,0:T(8,128)(2,1)S(1)}, u32[]{:S(2)}, u32[]{:S(2)}) collective-permute-start(bf16[512,1024]{1,0:T(8,128)(2,1)S(1)} %add_convert_fusion.6.refs_1_.refs_6_), channel_id=1, source_target_pairs={{0,24},{4,28},{8,16},{12,20},{16,8},{20,12},{24,0},{28,4},{1,25},{... | collective-permute-start | bytes 3145736 | tf_op jit(solution)/shard_map/ppermute | solution.py:27
  240.1 45.1 %collective-permute-start.43 = (bf16[512,1024]{1,0:T(8,128)(2,1)S(1)}, bf16[512,1024]{1,0:T(8,128)(2,1)}, u32[]{:S(2)}, u32[]{:S(2)}) collective-permute-start(bf16[512,1024]{1,0:T(8,128)(2,1)S(1)} %add_convert_fusion.3.refs_4_), channel_id=1, source_target_pairs={{0,8},{4,12},{8,0},{12,4},{16,24},{20,28},{24,16},{28,20},{1,9},{5... | collective-permute-start | bytes 3145736 | tf_op jit(solution)/shard_map/ppermute | solution.py:27
  243.1 42.5 %collective-permute-start.45 = (bf16[512,1024]{1,0:T(8,128)(2,1)}, bf16[512,1024]{1,0:T(8,128)(2,1)}, u32[]{:S(2)}, u32[]{:S(2)}) collective-permute-start(bf16[512,1024]{1,0:T(8,128)(2,1)} %add_convert_fusion.2.refs_5_), channel_id=1, source_target_pairs={{0,16},{4,20},{8,24},{12,28},{16,0},{20,4},{24,8},{28,12},{1,17},{... | collective-permute-start | bytes 3145736 | tf_op jit(solution)/shard_map/ppermute | solution.py:27
  264.8 52.1 %collective-permute-start.33 = (bf16[512,1024]{1,0:T(8,128)(2,1)}, bf16[512,1024]{1,0:T(8,128)(2,1)S(1)}, u32[]{:S(2)}, u32[]{:S(2)}) collective-permute-start(bf16[512,1024]{1,0:T(8,128)(2,1)} %hold.13.refs_12_), channel_id=1, source_target_pairs={{0,8},{4,12},{8,0},{12,4},{16,24},{20,28},{24,16},{28,20},{1,9},{5... | collective-permute-start | bytes 3145736 | tf_op jit(solution)/shard_map/ppermute | solution.py:27
  266.6 50.3 %collective-permute-start.35 = (bf16[512,1024]{1,0:T(8,128)(2,1)}, bf16[512,1024]{1,0:T(8,128)(2,1)S(1)}, u32[]{:S(2)}, u32[]{:S(2)}) collective-permute-start(bf16[512,1024]{1,0:T(8,128)(2,1)} %hold.15.refs_13_), channel_id=1, source_target_pairs={{0,16},{4,20},{8,24},{12,28},{16,0},{20,4},{24,8},{28,12},{1,17},{... | collective-permute-start | bytes 3145736 | tf_op jit(solution)/shard_map/ppermute | solution.py:27
  266.8 63.8 %collective-permute-start.37 = (bf16[512,1024]{1,0:T(8,128)(2,1)}, bf16[512,1024]{1,0:T(8,128)(2,1)}, u32[]{:S(2)}, u32[]{:S(2)}) collective-permute-start(bf16[512,1024]{1,0:T(8,128)(2,1)} %hold.17.refs_14_), channel_id=1, source_target_pairs={{0,24},{4,28},{8,16},{12,20},{16,8},{20,12},{24,0},{28,4},{1,25},{... | collective-permute-start | bytes 3145736 | tf_op jit(solution)/shard_map/ppermute | solution.py:27
  296.1 17.7 %collective-permute-start.47 = (bf16[576,128]{1,0:T(8,128)(2,1)}, bf16[576,128]{1,0:T(8,128)(2,1)S(1)}, u32[]{:S(2)}, u32[]{:S(2)}) collective-permute-start(bf16[576,128]{1,0:T(8,128)(2,1)} %get-tuple-element.117), channel_id=1, source_target_pairs={{0,2},{1,3},{2,0},{3,1},{4,6},{5,7},{6,4},{7,5},{8,10},{9,11},{10,... | collective-permute-start | bytes 442376 | tf_op jit(solution)/shard_map/ppermute | solution.py:27
  330.5 11.4 %collective-permute-start.56 = (bf16[1280,1024]{1,0:T(8,128)(2,1)}, bf16[1280,1024]{1,0:T(8,128)(2,1)}, u32[]{:S(2)}, u32[]{:S(2)}) collective-permute-start(bf16[1280,1024]{1,0:T(8,128)(2,1)} %hold.19), channel_id=1, source_target_pairs={{0,4},{4,0},{8,12},{12,8},{16,20},{20,16},{24,28},{28,24},{1,5},{5... | collective-permute-start | bytes 7864328 | tf_op jit(solution)/shard_map/ppermute | solution.py:27
  331.0 15.9 %collective-permute-start.54 = (bf16[528,128]{1,0:T(8,128)(2,1)}, bf16[528,128]{1,0:T(8,128)(2,1)S(1)}, u32[]{:S(2)}, u32[]{:S(2)}) collective-permute-start(bf16[528,128]{1,0:T(8,128)(2,1)} %hold.18.refs_8_), channel_id=1, source_target_pairs={{0,24},{4,28},{8,16},{12,20},{16,8},{20,12},{24,0},{28,4},{1,25},{... | collective-permute-start | bytes 405512 | tf_op jit(solution)/shard_map/ppermute | solution.py:27
  332.4 16.7 %collective-permute-start.52 = (bf16[528,128]{1,0:T(8,128)(2,1)}, bf16[528,128]{1,0:T(8,128)(2,1)S(1)}, u32[]{:S(2)}, u32[]{:S(2)}) collective-permute-start(bf16[528,128]{1,0:T(8,128)(2,1)} %hold.18.refs_8_), channel_id=1, source_target_pairs={{0,16},{4,20},{8,24},{12,28},{16,0},{20,4},{24,8},{28,12},{1,17},{... | collective-permute-start | bytes 405512 | tf_op jit(solution)/shard_map/ppermute | solution.py:27
  334.5 16.3 %collective-permute-start.50 = (bf16[528,128]{1,0:T(8,128)(2,1)}, bf16[528,128]{1,0:T(8,128)(2,1)S(1)}, u32[]{:S(2)}, u32[]{:S(2)}) collective-permute-start(bf16[528,128]{1,0:T(8,128)(2,1)} %hold.18.refs_8_), channel_id=1, source_target_pairs={{0,8},{4,12},{8,0},{12,4},{16,24},{20,28},{24,16},{28,20},{1,9},{5... | collective-permute-start | bytes 405512 | tf_op jit(solution)/shard_map/ppermute | solution.py:27
  336.8 14.0 %collective-permute-start.49 = (bf16[528,128]{1,0:T(8,128)(2,1)}, bf16[528,128]{1,0:T(8,128)(2,1)S(1)}, u32[]{:S(2)}, u32[]{:S(2)}) collective-permute-start(bf16[528,128]{1,0:T(8,128)(2,1)} %hold.18.refs_8_), channel_id=1, source_target_pairs={{0,4},{4,0},{8,12},{12,8},{16,20},{20,16},{24,28},{28,24},{1,5},{5... | collective-permute-start | bytes 405512 | tf_op jit(solution)/shard_map/ppermute | solution.py:27
  341.9 15.3 %collective-permute-start.39 = (bf16[128,1024]{1,0:T(8,128)(2,1)}, bf16[128,1024]{1,0:T(8,128)(2,1)S(1)}, u32[]{:S(2)}, u32[]{:S(2)}) collective-permute-start(bf16[128,1024]{1,0:T(8,128)(2,1)} %get-tuple-element.102), channel_id=1, source_target_pairs={{0,2},{1,3},{2,0},{3,1},{4,6},{5,7},{6,4},{7,5},{8,10},{9,11},{10,... | collective-permute-start | bytes 786440 | tf_op jit(solution)/shard_map/ppermute | solution.py:27
  346.9 27.7 %collective-permute-start.59 = (bf16[320,1024]{1,0:T(8,128)(2,1)S(1)}, bf16[320,1024]{1,0:T(8,128)(2,1)S(1)}, u32[]{:S(2)}, u32[]{:S(2)}) collective-permute-start(bf16[320,1024]{1,0:T(8,128)(2,1)S(1)} %get-tuple-element.190), channel_id=1, source_target_pairs={{0,24},{4,28},{8,16},{12,20},{16,8},{20,12},{24,0},{28,4},{1,25},{... | collective-permute-start | bytes 1966088 | tf_op jit(solution)/shard_map/ppermute | solution.py:27
  349.2 29.5 %collective-permute-start.58 = (bf16[320,1024]{1,0:T(8,128)(2,1)S(1)}, bf16[320,1024]{1,0:T(8,128)(2,1)S(1)}, u32[]{:S(2)}, u32[]{:S(2)}) collective-permute-start(bf16[320,1024]{1,0:T(8,128)(2,1)S(1)} %get-tuple-element.191), channel_id=1, source_target_pairs={{0,16},{4,20},{8,24},{12,28},{16,0},{20,4},{24,8},{28,12},{1,17},{... | collective-permute-start | bytes 1966088 | tf_op jit(solution)/shard_map/ppermute | solution.py:27
  350.8 27.9 %collective-permute-start.57 = (bf16[320,1024]{1,0:T(8,128)(2,1)S(1)}, bf16[320,1024]{1,0:T(8,128)(2,1)S(1)}, u32[]{:S(2)}, u32[]{:S(2)}) collective-permute-start(bf16[320,1024]{1,0:T(8,128)(2,1)S(1)} %get-tuple-element.192), channel_id=1, source_target_pairs={{0,8},{4,12},{8,0},{12,4},{16,24},{20,28},{24,16},{28,20},{1,9},{5... | collective-permute-start | bytes 1966088 | tf_op jit(solution)/shard_map/ppermute | solution.py:27
  358.6 13.4 %collective-permute-start.40 = (bf16[128,1024]{1,0:T(8,128)(2,1)}, bf16[128,1024]{1,0:T(8,128)(2,1)S(1)}, u32[]{:S(2)}, u32[]{:S(2)}) collective-permute-start(bf16[128,1024]{1,0:T(8,128)(2,1)} %get-tuple-element.103), channel_id=1, source_target_pairs={{0,3},{1,2},{2,1},{3,0},{4,7},{5,6},{6,5},{7,4},{8,11},{9,10},{10,... | collective-permute-start | bytes 786440 | tf_op jit(solution)/shard_map/ppermute | solution.py:27
  362.0 12.7 %collective-permute-start.38 = (bf16[128,1024]{1,0:T(8,128)(2,1)S(1)}, bf16[128,1024]{1,0:T(8,128)(2,1)S(1)}, u32[]{:S(2)}, u32[]{:S(2)}) collective-permute-start(bf16[128,1024]{1,0:T(8,128)(2,1)S(1)} %copy-done.50), channel_id=1, source_target_pairs={{0,1},{1,0},{2,3},{3,2},{4,5},{5,4},{6,7},{7,6},{8,9},{9,8},{10,11... | collective-permute-start | bytes 786440 | tf_op jit(solution)/shard_map/ppermute | solution.py:27
  395.6 13.2 %collective-permute-start.66 = (bf16[128,1024]{1,0:T(8,128)(2,1)S(1)}, bf16[128,1024]{1,0:T(8,128)(2,1)S(1)}, u32[]{:S(2)}, u32[]{:S(2)}) collective-permute-start(bf16[128,1024]{1,0:T(8,128)(2,1)S(1)} %get-tuple-element.197), channel_id=1, source_target_pairs={{0,24},{4,28},{8,16},{12,20},{16,8},{20,12},{24,0},{28,4},{1,25},{... | collective-permute-start | bytes 786440 | tf_op jit(solution)/shard_map/ppermute | solution.py:27
  396.7 13.5 %collective-permute-start.65 = (bf16[128,1024]{1,0:T(8,128)(2,1)S(1)}, bf16[128,1024]{1,0:T(8,128)(2,1)S(1)}, u32[]{:S(2)}, u32[]{:S(2)}) collective-permute-start(bf16[128,1024]{1,0:T(8,128)(2,1)S(1)} %get-tuple-element.198), channel_id=1, source_target_pairs={{0,16},{4,20},{8,24},{12,28},{16,0},{20,4},{24,8},{28,12},{1,17},{... | collective-permute-start | bytes 786440 | tf_op jit(solution)/shard_map/ppermute | solution.py:27
  398.9 46.0 %collective-permute-start.60 = (bf16[128,1024]{1,0:T(8,128)(2,1)}, bf16[128,1024]{1,0:T(8,128)(2,1)S(1)}, u32[]{:S(2)}, u32[]{:S(2)}) collective-permute-start(bf16[128,1024]{1,0:T(8,128)(2,1)} %get-tuple-element.135), channel_id=1, source_target_pairs={{0,1},{1,0},{2,3},{3,2},{4,5},{5,4},{6,7},{7,6},{8,9},{9,8},{10,11... | collective-permute-start | bytes 786440 | tf_op jit(solution)/shard_map/ppermute | solution.py:27
  399.1 45.8 %collective-permute-start.61 = (bf16[128,1024]{1,0:T(8,128)(2,1)}, bf16[128,1024]{1,0:T(8,128)(2,1)S(1)}, u32[]{:S(2)}, u32[]{:S(2)}) collective-permute-start(bf16[128,1024]{1,0:T(8,128)(2,1)} %get-tuple-element.136), channel_id=1, source_target_pairs={{0,2},{1,3},{2,0},{3,1},{4,6},{5,7},{6,4},{7,5},{8,10},{9,11},{10,... | collective-permute-start | bytes 786440 | tf_op jit(solution)/shard_map/ppermute | solution.py:27
  403.6 41.3 %collective-permute-start.62 = (bf16[128,1024]{1,0:T(8,128)(2,1)}, bf16[128,1024]{1,0:T(8,128)(2,1)S(1)}, u32[]{:S(2)}, u32[]{:S(2)}) collective-permute-start(bf16[128,1024]{1,0:T(8,128)(2,1)} %get-tuple-element.137), channel_id=1, source_target_pairs={{0,3},{1,2},{2,1},{3,0},{4,7},{5,6},{6,5},{7,4},{8,11},{9,10},{10,... | collective-permute-start | bytes 786440 | tf_op jit(solution)/shard_map/ppermute | solution.py:27
  408.8 14.2 %collective-permute-start.69 = (bf16[80,1024]{1,0:T(8,128)(2,1)S(1)}, bf16[80,1024]{1,0:T(8,128)(2,1)S(1)}, u32[]{:S(2)}, u32[]{:S(2)}) collective-permute-start(bf16[80,1024]{1,0:T(8,128)(2,1)S(1)} %get-tuple-element.194), channel_id=1, source_target_pairs={{0,3},{1,2},{2,1},{3,0},{4,7},{5,6},{6,5},{7,4},{8,11},{9,10},{10,... | collective-permute-start | bytes 491528 | tf_op jit(solution)/shard_map/ppermute | solution.py:27
  410.1 33.0 %collective-permute-start.68 = (bf16[80,1024]{1,0:T(8,128)(2,1)S(1)}, bf16[80,1024]{1,0:T(8,128)(2,1)}, u32[]{:S(2)}, u32[]{:S(2)}) collective-permute-start(bf16[80,1024]{1,0:T(8,128)(2,1)S(1)} %get-tuple-element.195), channel_id=1, source_target_pairs={{0,2},{1,3},{2,0},{3,1},{4,6},{5,7},{6,4},{7,5},{8,10},{9,11},{10,... | collective-permute-start | bytes 491528 | tf_op jit(solution)/shard_map/ppermute | solution.py:27
  411.7 34.1 %all-to-all-start.1 = ((bf16[4,32,1024]{2,1,0:T(8,128)(2,1)}), bf16[4,32,1024]{2,1,0:T(8,128)(2,1)S(1)}, u32[]{:S(2)}, u32[]{:S(2)}) async-start(bf16[4,32,1024]{2,1,0:T(8,128)(2,1)} %bitcast.12), calls=%async_computation.1 | async-start | bytes 524288 | tf_op jit(solution)/shard_map/all_to_all | solution.py:1135
  (89 other events, 775.8 us)
Sparse Core Ops, SparseCore 0:
  10.9 94.6 all-gather.2
  108.5 92.7 all-gather.4

commit v4 on v3

--- a/solution.py
+++ b/solution.py
@@ -318,7 +318,7 @@
 def mix_kernel(layout, heads, at_ref, *refs):
     o_refs, tok_refs = refs[:heads], refs[heads : 2 * heads]
     weight_ref, wo_ref = refs[2 * heads : 2 * heads + 2]
-    x1_ref, low_ref, u_ref = refs[-3:]
+    x1_ref, low_ref, high_ref, u_ref = refs[-4:]
     size, mixed, att, _, _ = layout
     head = at_ref[1]
     span = weight_ref.shape[0]
@@ -341,7 +341,9 @@
     own = jnp.concatenate([ref[...] for ref in tok_refs]).astype(F32)
     x1 = own + nn(u_ref[...], wo_ref[...])
     x1_ref[...] = x1[:tok_rows]
-    low_ref[...] = x1.astype(BF)
+    low = x1.astype(BF)
+    low_ref[...] = low[: span // 2]
+    high_ref[...] = low[span // 2 :]
 
 
 def mix(layout, at, outs, tok_pieces, weight, w_output, tokens):
@@ -361,7 +363,8 @@
         grid=(width // step,),
         out_shape=(
             shape((span // heads, width), F32),
-            shape((span, width), BF),
+            shape((span // 2, width), BF),
+            shape((span // 2, width), BF),
             shape((span, depth), BF),
         ),
         in_specs=[SMEM]
@@ -371,7 +374,8 @@
         + [ANY] * len(tokens),
         out_specs=(
             columns(span // heads),
-            columns(span),
+            columns(span // 2),
+            columns(span // 2),
             pl.BlockSpec((span, depth), lambda i: (0, 0)),
         ),
         compiler_params=PARAMS,
@@ -833,6 +837,52 @@
     )(at, u, g)
 
 
+def pair_kernel(mine_ref, got_ref, *refs):
+    rows = refs[0].shape[0]
+    for i, ref in enumerate(refs):
+        at = slice(i * rows, (i + 1) * rows)
+        total = mine_ref[at, :].astype(F32) + got_ref[at, :].astype(F32)
+        ref[...] = total.astype(ref.dtype)
+
+
+def pair_rows(mine, got, parts):
+    rows = (mine.shape[0] // parts, mine.shape[1])
+    return pl.pallas_call(
+        pair_kernel,
+        out_shape=(shape(rows, F32),) + (shape(rows, BF),) * (parts - 1),
+        in_specs=[VMEM, VMEM],
+        out_specs=(VMEM,) * parts,
+        compiler_params=PARAMS,
+        cost_estimate=CHEAP,
+        name="pair_rows",
+    )(mine, got)
+
+
+def unpack_kernel(layout, all_ref, q_ref, k_ref, v_ref, rv_ref, ro_ref, gain_ref):
+    size, mixed, att, head_count, gain_lane = layout
+    row = lax.broadcasted_iota(jnp.int32, (LANES, LANES), 0)
+    lane = lax.broadcasted_iota(jnp.int32, (LANES, LANES), 1)
+    few = att * head_count
+    values = outputs = gains = None
+    for h in range(head_count):
+        q_ref[:, h * size : (h + 1) * size] = all_ref[h, :, :size].astype(F32)
+        k_ref[:, h * size : (h + 1) * size] = all_ref[h, :, size : 2 * size].astype(F32)
+        v_ref[:, h * mixed : (h + 1) * mixed] = all_ref[h, :, 2 * size : 2 * size + mixed].astype(
+            F32
+        )
+        tail = all_ref[h, :, 2 * size + mixed :]
+        here = (row >= att * h) & (row < att * (h + 1))
+        value = nt(select(row - att * h, here, lane), tail)
+        output = nt(select(row - att * h + att, here, lane), tail)
+        gain = nt((lane == gain_lane).astype(BF), tail)
+        values = value if h == 0 else values + value
+        outputs = output if h == 0 else outputs + output
+        gains = gain if h == 0 else gains + gain
+    rv_ref[...] = values[:few]
+    ro_ref[...] = outputs[:few]
+    gain_ref[...] = gains[:1]
+
+
 def branch_kernel(heads, *refs):
     x1_ref, own_ref, send_refs = refs[0], refs[-heads], refs[1 - heads :]
     rows = x1_ref.shape[0]
@@ -1034,7 +1084,7 @@
     qkv_pieces = gather_blk(qkv)
     mine, log_total = attend(at, qkv_pieces, tok_rows, span, scale, [])
     outs = gather_head(mine)
-    x1, middle, mixed_heads = mix(layout, at, outs, tok_pieces, weight, wo_full, [])
+    x1, *middle, mixed_heads = mix(layout, at, outs, tok_pieces, weight, wo_full, [])
 
     route = jnp.pad(route_expert, ((0, 0), (0, LANES - experts)))
     near = 8
@@ -1050,12 +1100,11 @@
                 (base, branch_terms, grad_terms, *weight_grads)
             )
             branch_terms, grad_terms, *weight_grads = old
-            base = swap(base, "blk", far)
-        even = {0: [base], 2: [swap(base, "blk", 2)], 4: [swap(base, "blk", 4)]}
-        even[6] = [
-            swap(even[2][0][: span // 2], "blk", 4),
-            swap(even[4][0][span // 2 :], "blk", 2),
-        ]
+            base = [swap(rows, "blk", far) for rows in base]
+        even = {0: base}
+        for mask in (2, 4):
+            even[mask] = [swap(rows, "blk", mask) for rows in base]
+        even[6] = [swap(even[2][0], "blk", 4), swap(even[4][1], "blk", 2)]
         xs = []
         for mask in range(0, near, 2):
             xs += [even[mask], [swap(x, "blk", 1) for x in even[mask]]]
@@ -1098,15 +1147,15 @@
     dout, dso = join(got, mine, log_total, gate, weight, att, [odd])
     dout_pieces = gather_blk(hold(dout, *arrived[:2]))
     layer_out, *outputs = branch(x1, branch_terms, heads)
-    pair_sums = add_low(even, swap(hold(odd, *arrived), "blk", 1))
+    pair_sums = pair_rows(even, swap(hold(odd, *arrived), "blk", 1), groups // 2)
+    pair_sums = [hold(rows, *dout_pieces) for rows in pair_sums]
     dq, dk, dv = attend_back(
-        at, qkv_pieces, dout_pieces, tok_rows, span, scale, [outputs[0], pair_sums]
+        at, qkv_pieces, dout_pieces, tok_rows, span, scale, [outputs[0], pair_sums[0]]
     )
 
     out_rows = w_output.shape[0]
-    there = []
-    pair_sums = pair_sums.reshape(groups // 2, heads * out_rows, width)
-    rows_sum = pair_sums[0].astype(F32)
+    there, last_rows = [], []
+    rows_sum = pair_sums[0]
     for index in range(1, groups // 2):
         got_rows = swap(pair_sums[index], "blk", 2 * index)
         there.append(got_rows)
@@ -1114,8 +1163,10 @@
     rows_sum = rows_sum.reshape(heads, out_rows, width)
     grad_output = lax.dynamic_index_in_dim(rows_sum, head, 0, keepdims=False)
     for mask in range(1, heads):
-        part = lax.dynamic_index_in_dim(rows_sum, head ^ mask, 0, keepdims=False).astype(BF)
-        grad_output = grad_output + swap(part, "head", mask).astype(F32)
+        sent = lax.dynamic_index_in_dim(rows_sum, head ^ mask, 0, keepdims=False).astype(BF)
+        there.append(sent)
+        last_rows.append(swap(sent, "head", mask))
+        grad_output = grad_output + last_rows[-1].astype(F32)
         got_rows = swap(outputs[mask - 1], "head", mask)
         there.append(got_rows)
         layer_out = layer_out + got_rows.astype(F32)
@@ -1124,27 +1175,29 @@
         layout, heads, groups, at, there, dq, dk, dv, cosine, sine, expert_values, gate, weight, dso,
         normed, weights, g1, *tok_pieces,
     )
-    pairs = add_low(even_rows, swap(odd_rows, "blk", 1))
-    own = width // groups
-    summed = pairs[:own].astype(F32)
-    for index in range(1, groups // 2):
-        piece = pairs[index * own : (index + 1) * own]
-        summed = summed + swap(piece, "blk", 2 * index).astype(F32)
+    parts = [hold(rows, *last_rows) for rows in parts]
+    summed, *pairs = pair_rows(even_rows, swap(odd_rows, "blk", 1), groups // 2)
+    for index, piece in enumerate(pairs):
+        summed = summed + swap(piece, "blk", 2 * index + 2).astype(F32)
     for mask in range(1, heads):
         grad_input = grad_input + swap(parts[mask - 1], "head", mask).astype(F32)
     summed = lax.all_to_all(
         summed.astype(BF).reshape(heads, own_rows, packed), "head", 0, 0, tiled=True
-    ).astype(F32)
-
-    def columns(first, count):
-        return summed[:, :, first : first + count].transpose(1, 0, 2).reshape(own_rows, -1)
-
-    grad_query = columns(0, size)
-    grad_key = columns(size, size)
-    grad_value = columns(2 * size, mixed)
-    grad_value_router = columns(2 * size + mixed, att)
-    grad_output_router = columns(2 * size + mixed + att, att)
-    grad_gain = jnp.sum(summed[:, :, used - 1], 0)
+    )
+    few = head_count * att
+    full = [(own_rows, head_count * columns) for columns in (size, size, mixed)]
+    flat = [(few, own_rows), (few, own_rows), (1, own_rows)]
+    grad_query, grad_key, grad_value, *routers, grad_gain = pl.pallas_call(
+        functools.partial(unpack_kernel, layout),
+        out_shape=tuple(shape(dims, F32) for dims in full + flat),
+        in_specs=[VMEM],
+        out_specs=(VMEM,) * 6,
+        compiler_params=PARAMS,
+        cost_estimate=CHEAP,
+        name="unpack",
+    )(summed)
+    grad_value_router, grad_output_router = (rows.T for rows in routers)
+    grad_gain = grad_gain[0]
 
     return (
         layer_out,

time: 465 us -> 455 us (0.978)
  waiting for transfers between devices: 207 us -> 193 us
  Pallas kernels: 117 us -> 127 us
    ppermute x70 -> x75, waiting for transfers between devices: 199 us -> 180 us  [swap(): return lax.ppermute(value, axis, [(i, i ^ mask) for i in range(size)])]
    pallas_call x0 -> x3, Pallas kernels: none -> 8.88 us  [the longest x2 7 us: pair_rows(): pl.pallas_call(pair_kernel, out_shape=(shape(rows, F32),) + (shape(rows,...]
    convert_element_type x8 -> x6, other arithmetic: 10.1 us -> 6.4 us  [add_low(): return (left.astype(F32) + right.astype(F32)).astype(BF)]
    ppermute x70 -> x75, starting transfers between devices: 72.1 us -> 73.8 us  [swap(): return lax.ppermute(value, axis, [(i, i ^ mask) for i in range(size)])]
  transfers between devices with their start and end apart: 74 -> 79, of which waited for: 34 -> 32; matrix products, arithmetic and copies ran while one was open for 5% -> 5% of each run, Pallas kernels for 24% -> 26%
where the time goes in v4:
time: 455 us; the launch traced here: 448 us
  waiting for transfers between devices  193 us (42%)
  Pallas kernels  127 us (28%)
  starting transfers between devices  83.6 us (18%)
  other arithmetic  17.3 us (4%)
  between operations  15 us (3%)
  local copies, waits for them, and re-layouts  12 us (3%)
    ppermute x75, waiting for transfers between devices, swap(): return lax.ppermute(value, axis, [(i, i ^ mask) for i in range(size)])  180 us
    ppermute x75, starting transfers between devices, swap(): return lax.ppermute(value, axis, [(i, i ^ mask) for i in range(size)])  73.8 us
    pallas_call x1, Pallas kernels, run_experts(): pl.pallas_call(functools.partial(forward_kernel, (chosen, len(flat)), hea...  20.7 us
    pallas_call x1, Pallas kernels, run_experts(): pl.pallas_call(functools.partial(back_kernel, far, groups, heads, experts...  19.2 us
    pallas_call x1, Pallas kernels, expert_grads(): pl.pallas_call(functools.partial(expert_grads_kernel, halves), grid=(expe...  13.7 us
    pallas_call x1, Pallas kernels, spread(): pl.pallas_call(functools.partial(spread_kernel, layout, heads, len(terms)...  10.4 us
    pallas_call x1, Pallas kernels, attend_back(): pl.pallas_call(functools.partial(attend_back_kernel, groups, tok_rows, sp...  10.2 us
    pallas_call x1, Pallas kernels, finish(): pl.pallas_call(functools.partial(finish_kernel, layout, heads, groups), o...  9.2 us
  transfers between devices with their start and end apart: 79, of which 32 were waited for; matrix products, arithmetic and copies ran while one was open for 5% of the time, Pallas kernels for 26%

profile of v4, /device:TPU:0, one launch (start us, length us, event | category | flops | bytes accessed | tf_op | source)
XLA Modules:
  0.0 447.6 jit_solution(8516778730311057314)
XLA Ops:
  11.4 6.3 %all-to-all-start = ((bf16[4,32,1152]{2,1,0:T(8,128)(2,1)}), bf16[4,32,1152]{2,1,0:T(8,128)(2,1)S(1)}, u32[]{:S(2)}, u32[]{:S(2)}) async-start(bf16[4,32,1152]{2,1,0:T(8,128)(2,1)} %get-tuple-element.92), calls=%async_computation | async-start | bytes 589824 | tf_op jit(solution)/shard_map/all_to_all | solution.py:1047
  19.7 2.4 collective-permute-start.1
  22.1 7.5 %all-to-all-done.refs_1_ = bf16[4,32,1152]{2,1,0:T(8,128)(2,1)S(1)} async-done(((bf16[4,32,1152]{2,1,0:T(8,128)(2,1)}), bf16[4,32,1152]{2,1,0:T(8,128)(2,1)S(1)}, u32[]{:S(2)}, u32[]{:S(2)}) %all-to-all-start) | async-done | bytes 294944 | tf_op jit(solution)/shard_map/all_to_all | solution.py:1047
  29.6 2.6 collective-permute-start.8
  33.2 5.6 %collective-permute-done.refs_1_.refs_5_.refs_13_ = bf16[128,1024]{1,0:T(8,128)(2,1)S(1)} collective-permute-done((bf16[128,1024]{1,0:T(8,128)(2,1)}, bf16[128,1024]{1,0:T(8,128)(2,1)S(1)}, u32[]{:S(2)}, u32[]{:S(2)}) %collective-permute-start) | collective-permute-done | bytes 262176 | tf_op jit(solution)/shard_map/ppermute | solution.py:27
  38.8 3.2 collective-permute-done.1.refs_2_.refs_6_.refs_14_
  48.7 4.9 %collective-permute-done.2.refs_3_.refs_7_.refs_15_ = bf16[128,1024]{1,0:T(8,128)(2,1)S(1)} collective-permute-done((bf16[128,1024]{1,0:T(8,128)(2,1)}, bf16[128,1024]{1,0:T(8,128)(2,1)S(1)}, u32[]{:S(2)}, u32[]{:S(2)}) %collective-permute-start.2) | collective-permute-done | bytes 262176 | tf_op jit(solution)/shard_map/ppermute | solution.py:27
  54.5 5.8 %project.1 = (bf16[544,384]{1,0:T(8,128)(2,1)}, f32[512,640]{1,0:T(8,128)}, f32[512,128]{1,0:T(8,128)}, f32[512,128]{1,0:T(8,128)}, bf16[1024,1024]{1,0:T(8,128)(2,1)}, /*index=5*/bf16[512,1024]{1,0:T(8,128)(2,1)}) custom-call(s32[3]{0:T(128)} %pad_add_fusion.1.at_ref, f32[512,128]{1,0:T(8,128)} %get-tuple-element.190.cos_ref.refs_3_, ...), custom_call_target="tpu_custom_call" | custom-call | tf_op jit(solution)/shard_map/project/pallas_call | solution.py:1065
  60.3 2.5 collective-permute-start.15
  63.8 16.0 %collective-permute-done.15.refs_6_.refs_22_ = bf16[544,384]{1,0:T(8,128)(2,1)S(1)} collective-permute-done((bf16[544,384]{1,0:T(8,128)(2,1)}, bf16[544,384]{1,0:T(8,128)(2,1)S(1)}, u32[]{:S(2)}, u32[]{:S(2)}) %collective-permute-start.15) | collective-permute-done | bytes 417824 | tf_op jit(solution)/shard_map/ppermute | solution.py:27
  79.8 6.7 %collective-permute-done.13.refs_4_.refs_20_ = bf16[544,384]{1,0:T(8,128)(2,1)S(1)} collective-permute-done((bf16[544,384]{1,0:T(8,128)(2,1)}, bf16[544,384]{1,0:T(8,128)(2,1)S(1)}, u32[]{:S(2)}, u32[]{:S(2)}) %collective-permute-start.13) | collective-permute-done | bytes 417824 | tf_op jit(solution)/shard_map/ppermute | solution.py:27
  90.4 4.0 attend.1
  94.3 4.3 collective-permute-start.19
  98.7 6.3 %collective-permute-start.18 = (bf16[512,128]{1,0:T(8,128)(2,1)}, bf16[512,128]{1,0:T(8,128)(2,1)S(1)}, u32[]{:S(2)}, u32[]{:S(2)}) collective-permute-start(bf16[512,128]{1,0:T(8,128)(2,1)} %get-tuple-element.96.refs_0_.refs_8_.refs_4_), channel_id=1, source_target_pairs={{0,2},{1,3},{2,0},{3,1},{4,6},{5,7},{6,4},{7,5},{8,10},{9,11},{10,... | collective-permute-start | bytes 393224 | tf_op jit(solution)/shard_map/ppermute | solution.py:27
  105.0 10.1 %collective-permute-done.18.refs_2_.refs_10_ = bf16[512,128]{1,0:T(8,128)(2,1)S(1)} collective-permute-done((bf16[512,128]{1,0:T(8,128)(2,1)}, bf16[512,128]{1,0:T(8,128)(2,1)S(1)}, u32[]{:S(2)}, u32[]{:S(2)}) %collective-permute-start.18) | collective-permute-done | bytes 131104 | tf_op jit(solution)/shard_map/ppermute | solution.py:27
  115.8 9.1 %mix.1 = (f32[128,1024]{1,0:T(8,128)}, bf16[256,1024]{1,0:T(8,128)(2,1)}, bf16[256,1024]{1,0:T(8,128)(2,1)}, bf16[512,2560]{1,0:T(8,128)(2,1)}) custom-call(s32[3]{0:T(128)} %pad_add_fusion.1.at_ref, bf16[512,128]{1,0:T(8,128)(2,1)} %get-tuple-element.96.refs_0_.refs_8_.refs_4_, bf16[512,128]{1,0:T(8,128)(2,1)} %copy-done.52, bf16[512,128]{1,0:T(8,128)(2,1)} %copy-done.51, ...), custom_call_target="tpu_custom_call" | custom-call | tf_op jit(solution)/shard_map/mix/pallas_call | solution.py:361
  124.9 6.3 %collective-permute-start.26 = (bf16[256,1024]{1,0:T(8,128)(2,1)}, bf16[256,1024]{1,0:T(8,128)(2,1)S(1)}, u32[]{:S(2)}, u32[]{:S(2)}) collective-permute-start(bf16[256,1024]{1,0:T(8,128)(2,1)} %get-tuple-element.99.refs_0_), channel_id=1, source_target_pairs={{0,16},{4,20},{8,24},{12,28},{16,0},{20,4},{24,8},{28,12},{1,17},{... | collective-permute-start | bytes 1572872 | tf_op jit(solution)/shard_map/ppermute | solution.py:27
  131.2 2.6 collective-permute-start.22
  134.0 13.9 %collective-permute-done.26.refs_8_ = bf16[256,1024]{1,0:T(8,128)(2,1)S(1)} collective-permute-done((bf16[256,1024]{1,0:T(8,128)(2,1)}, bf16[256,1024]{1,0:T(8,128)(2,1)S(1)}, u32[]{:S(2)}, u32[]{:S(2)}) %collective-permute-start.26) | collective-permute-done | bytes 524320 | tf_op jit(solution)/shard_map/ppermute | solution.py:27
  147.9 4.9 %collective-permute-done.22.refs_4_ = bf16[256,1024]{1,0:T(8,128)(2,1)S(1)} collective-permute-done((bf16[256,1024]{1,0:T(8,128)(2,1)}, bf16[256,1024]{1,0:T(8,128)(2,1)S(1)}, u32[]{:S(2)}, u32[]{:S(2)}) %collective-permute-start.22) | collective-permute-done | bytes 524320 | tf_op jit(solution)/shard_map/ppermute | solution.py:27
  154.0 5.2 %collective-permute-done.27.refs_9_ = bf16[256,1024]{1,0:T(8,128)(2,1)S(1)} collective-permute-done((bf16[256,1024]{1,0:T(8,128)(2,1)}, bf16[256,1024]{1,0:T(8,128)(2,1)S(1)}, u32[]{:S(2)}, u32[]{:S(2)}) %collective-permute-start.27) | collective-permute-done | bytes 524320 | tf_op jit(solution)/shard_map/ppermute | solution.py:27
  159.2 2.2 collective-permute-start.31
  161.4 4.3 collective-permute-done.23.refs_5_
  166.3 11.2 %collective-permute-done.30.refs_12_ = bf16[256,1024]{1,0:T(8,128)(2,1)} collective-permute-done((bf16[256,1024]{1,0:T(8,128)(2,1)S(1)}, bf16[256,1024]{1,0:T(8,128)(2,1)}, u32[]{:S(2)}, u32[]{:S(2)}) %collective-permute-start.30) | collective-permute-done | bytes 524320 | tf_op jit(solution)/shard_map/ppermute | solution.py:27
  177.5 10.3 %collective-permute-done.31.refs_13_ = bf16[256,1024]{1,0:T(8,128)(2,1)} collective-permute-done((bf16[256,1024]{1,0:T(8,128)(2,1)S(1)}, bf16[256,1024]{1,0:T(8,128)(2,1)}, u32[]{:S(2)}, u32[]{:S(2)}) %collective-permute-start.31) | collective-permute-done | bytes 524320 | tf_op jit(solution)/shard_map/ppermute | solution.py:27
  190.1 20.7 %experts_forward.1 = (bf16[512,1024]{1,0:T(8,128)(2,1)}, bf16[512,1024]{1,0:T(8,128)(2,1)}, bf16[512,1024]{1,0:T(8,128)(2,1)}, bf16[512,1024]{1,0:T(8,128)(2,1)}...) custom-call(s32[3]{0:T(128)} %pad_add_fusion.1.at_ref, ...), custom_call_target="tpu_custom_call" | custom-call | tf_op jit(solution)/shard_map/experts_forward/pallas_call | solution.py:615
  211.0 19.2 %experts_back.1 = (bf16[512,1024]{1,0:T(8,128)(2,1)}, bf16[512,1024]{1,0:T(8,128)(2,1)}, bf16[512,1024]{1,0:T(8,128)(2,1)}, bf16[512,1024]{1,0:T(8,128)(2,1)}, b...) custom-call(s32[3]{0:T(128)} %pad_add_fusion.1.at_ref, ...), custom_call_target="tpu_custom_call" | custom-call | tf_op jit(solution)/shard_map/experts_back/pallas_call | solution.py:640
  244.2 18.7 %collective-permute-done.37.refs_1_.refs_4_ = bf16[512,1024]{1,0:T(8,128)(2,1)S(1)} collective-permute-done((bf16[512,1024]{1,0:T(8,128)(2,1)S(1)}, bf16[512,1024]{1,0:T(8,128)(2,1)S(1)}, u32[]{:S(2)}, u32[]{:S(2)}) %collective-permute-start.37) | collective-permute-done | bytes 1048608 | tf_op jit(solution)/shard_map/ppermute | solution.py:27
  267.4 13.7 %expert_grads.1 = (f32[1024,1024]{1,0:T(8,128)}, f32[1024,1024]{1,0:T(8,128)}, f32[1024,128]{1,0:T(8,128)}) custom-call(bf16[8,512,1024]{2,1,0:T(8,128)(2,1)} %get-tuple-element.126.refs_0_, bf16[8,512,1024]{2,1,0:T(8,128)(2,1)} %get-tuple-element.127.refs_1_, bf16[8,512,128]{2,1,0:T(8,128)(2,1)} %get-tuple-element.128.refs_2_, ...), custom_call_target="tpu_custom_call" | custom-call | tf_op jit(solution)/shard_map/expert_grads/pallas_call | solution.py:698
  281.1 3.6 collective-permute-done.48.refs_2_
  284.7 10.4 %spread.1 = (f32[512,1024]{1,0:T(8,128)}, bf16[512,1024]{1,0:T(8,128)(2,1)}, bf16[576,128]{1,0:T(8,128)(2,1)}, bf16[576,128]{1,0:T(8,128)(2,1)}, bf16[576,128]{1,0:T(8,128)(2,1)}, /*index=5*/bf16[576,128]{1,0:T(8,128)(2,1)}) custom-call(s32[3]{0:T(128)} %pad_add_fusion.1.at_ref, bf16[512,1024]{1,0:T(8,128)(2,1)} %get-tuple-element.120.refs_0_, ...), custom_call_target="tpu_custom_call" | custom-call | tf_op jit(solution)/shard_map/spread/pallas_call | solution.py:760
  296.4 5.8 %collective-permute-done.51.refs_1_ = bf16[576,128]{1,0:T(8,128)(2,1)S(1)} collective-permute-done((bf16[576,128]{1,0:T(8,128)(2,1)}, bf16[576,128]{1,0:T(8,128)(2,1)S(1)}, u32[]{:S(2)}, u32[]{:S(2)}) %collective-permute-start.51) | collective-permute-done | bytes 147488 | tf_op jit(solution)/shard_map/ppermute | solution.py:27
  304.3 7.4 %output_grad.1 = (bf16[1280,1024]{1,0:T(8,128)(2,1)}, bf16[1280,1024]{1,0:T(8,128)(2,1)}) custom-call(s32[3]{0:T(128)} %pad_add_fusion.1.at_ref, bf16[512,2560]{1,0:T(8,128)(2,1)} %get-tuple-element.137.u_ref, bf16[512,1024]{1,0:T(8,128)(2,1)} %get-tuple-element.138.g_ref), custom_call_target="tpu_custom_call" | custom-call | tf_op jit(solution)/shard_map/output_grad/pallas_call | solution.py:828
  312.4 2.4 join.1
  314.8 14.8 %collective-permute-done.42.refs_5_.refs_3_ = bf16[512,1024]{1,0:T(8,128)(2,1)} collective-permute-done((bf16[512,1024]{1,0:T(8,128)(2,1)}, bf16[512,1024]{1,0:T(8,128)(2,1)}, u32[]{:S(2)}, u32[]{:S(2)}) %collective-permute-start.42) | collective-permute-done | bytes 1048608 | tf_op jit(solution)/shard_map/ppermute | solution.py:27
  333.6 4.1 collective-permute-done.59.refs_7_.refs_14_
  340.3 4.4 pair_rows.2
  349.0 4.0 branch.1
  353.9 10.2 %attend_back.1 = (f32[512,128]{1,0:T(8,128)}, f32[512,128]{1,0:T(8,128)}, f32[512,128]{1,0:T(8,128)}) custom-call(s32[3]{0:T(128)} %pad_add_fusion.1.at_ref, bf16[544,384]{1,0:T(8,128)(2,1)} %get-tuple-element.95.refs_0_.refs_16_.refs_1_, bf16[544,384]{1,0:T(8,128)(2,1)} %copy-done.9, bf16[544,384]{1,0:T(8,128)(2,1)} %copy-done.8, ...), custom_call_target="tpu_custom_call" | custom-call | tf_op jit(solution)/shard_map/attend_back/pallas_call | solution.py:306
  364.1 3.6 collective-permute-start.45
  367.6 9.2 %collective-permute-done.64.refs_18_ = bf16[320,1024]{1,0:T(8,128)(2,1)S(1)} collective-permute-done((bf16[320,1024]{1,0:T(8,128)(2,1)}, bf16[320,1024]{1,0:T(8,128)(2,1)S(1)}, u32[]{:S(2)}, u32[]{:S(2)}) %collective-permute-start.64) | collective-permute-done | bytes 655392 | tf_op jit(solution)/shard_map/ppermute | solution.py:27
  379.4 9.2 %finish.1 = (f32[128,1024]{1,0:T(8,128)}, bf16[128,1024]{1,0:T(8,128)(2,1)}, bf16[128,1024]{1,0:T(8,128)(2,1)}, bf16[128,1024]{1,0:T(8,128)(2,1)}, bf16[512,1024]{1,0:T(8,128)(2,1)}, /*index=5*/bf16[512,1024]{1,0:T(8,128)(2,1)}) custom-call(s32[3]{0:T(128)} %pad_add_fusion.1.at_ref, f32[512,128]{1,0:T(8,128)} %get-tuple-element.143.refs_0_, ...), custom_call_target="tpu_custom_call" | custom-call | tf_op jit(solution)/shard_map/finish/pallas_call | solution.py:976
  391.4 2.5 collective-permute-start.65
  393.9 2.6 pair_rows.3
  402.0 3.7 collective-permute-done.66.refs_2_
  413.9 3.4 all-to-all-start.1
  419.5 12.2 %collective-permute-done.69 = bf16[128,1024]{1,0:T(8,128)(2,1)} collective-permute-done((bf16[128,1024]{1,0:T(8,128)(2,1)}, bf16[128,1024]{1,0:T(8,128)(2,1)}, u32[]{:S(2)}, u32[]{:S(2)}) %collective-permute-start.69) | collective-permute-done | bytes 262176 | tf_op jit(solution)/shard_map/ppermute | solution.py:27
  433.7 4.3 all-to-all-done.1.all_ref
  (317 shorter events, 84.3 us)
Async XLA Ops:
  7.2 107.9 %all-gather.3.cloned.1.call-start = ((), (), s32[]{:S(2)}) async-start(), calls=%async_computation.2 | async-start | bytes 5406720 | tf_op jit(solution)/shard_map/all_gather | solution.py:1054
  11.4 18.2 %all-to-all-start = ((bf16[4,32,1152]{2,1,0:T(8,128)(2,1)}), bf16[4,32,1152]{2,1,0:T(8,128)(2,1)S(1)}, u32[]{:S(2)}, u32[]{:S(2)}) async-start(bf16[4,32,1152]{2,1,0:T(8,128)(2,1)} %get-tuple-element.92), calls=%async_computation | async-start | bytes 589824 | tf_op jit(solution)/shard_map/all_to_all | solution.py:1047
  17.7 193.3 %all-gather.5.cloned.1.call-start = ((), (), s32[]{:S(2)}) async-start(), calls=%async_computation.3 | async-start | bytes 8650752 | tf_op jit(solution)/shard_map/all_gather | solution.py:1082
  17.7 21.1 %collective-permute-start = (bf16[128,1024]{1,0:T(8,128)(2,1)}, bf16[128,1024]{1,0:T(8,128)(2,1)S(1)}, u32[]{:S(2)}, u32[]{:S(2)}) collective-permute-start(bf16[128,1024]{1,0:T(8,128)(2,1)} %refs_12_.1), channel_id=1, source_target_pairs={{0,1},{1,0},{2,3},{3,2},{4,5},{5,4},{6,7},{7,6},{8,9},{9,8},{10,11... | collective-permute-start | bytes 786440 | tf_op jit(solution)/shard_map/ppermute | solution.py:27
  19.7 22.3 %collective-permute-start.1 = (bf16[128,1024]{1,0:T(8,128)(2,1)}, bf16[128,1024]{1,0:T(8,128)(2,1)S(1)}, u32[]{:S(2)}, u32[]{:S(2)}) collective-permute-start(bf16[128,1024]{1,0:T(8,128)(2,1)} %get-tuple-element.93), channel_id=1, source_target_pairs={{0,2},{1,3},{2,0},{3,1},{4,6},{5,7},{6,4},{7,5},{8,10},{9,11},{10,... | collective-permute-start | bytes 786440 | tf_op jit(solution)/shard_map/ppermute | solution.py:27
  29.6 13.9 %collective-permute-start.8 = (bf16[128,1024]{1,0:T(8,128)(2,1)S(1)}, bf16[128,1024]{1,0:T(8,128)(2,1)S(1)}, u32[]{:S(2)}, u32[]{:S(2)}) collective-permute-start(bf16[128,1024]{1,0:T(8,128)(2,1)S(1)} %bitcast.35), channel_id=1, source_target_pairs={{0,24},{4,28},{8,16},{12,20},{16,8},{20,12},{24,0},{28,4},{1,25},{... | collective-permute-start | bytes 786440 | tf_op jit(solution)/shard_map/ppermute | solution.py:27
  60.3 19.6 %collective-permute-start.15 = (bf16[544,384]{1,0:T(8,128)(2,1)}, bf16[544,384]{1,0:T(8,128)(2,1)S(1)}, u32[]{:S(2)}, u32[]{:S(2)}) collective-permute-start(bf16[544,384]{1,0:T(8,128)(2,1)} %get-tuple-element.95.refs_0_.refs_16_.refs_1_), channel_id=1, source_target_pairs={{0,24},{4,28},{8,16},{12,20},{16,8},{20,12},{24,0},{28,4},{1,25},{... | collective-permute-start | bytes 1253384 | tf_op jit(solution)/shard_map/ppermute | solution.py:27
  62.7 23.8 %collective-permute-start.13 = (bf16[544,384]{1,0:T(8,128)(2,1)}, bf16[544,384]{1,0:T(8,128)(2,1)S(1)}, u32[]{:S(2)}, u32[]{:S(2)}) collective-permute-start(bf16[544,384]{1,0:T(8,128)(2,1)} %get-tuple-element.95.refs_0_.refs_16_.refs_1_), channel_id=1, source_target_pairs={{0,16},{4,20},{8,24},{12,28},{16,0},{20,4},{24,8},{28,12},{1,17},{... | collective-permute-start | bytes 1253384 | tf_op jit(solution)/shard_map/ppermute | solution.py:27
  63.3 24.5 %collective-permute-start.11 = (bf16[544,384]{1,0:T(8,128)(2,1)}, bf16[544,384]{1,0:T(8,128)(2,1)S(1)}, u32[]{:S(2)}, u32[]{:S(2)}) collective-permute-start(bf16[544,384]{1,0:T(8,128)(2,1)} %get-tuple-element.95.refs_0_.refs_16_.refs_1_), channel_id=1, source_target_pairs={{0,8},{4,12},{8,0},{12,4},{16,24},{20,28},{24,16},{28,20},{1,9},{5... | collective-permute-start | bytes 1253384 | tf_op jit(solution)/shard_map/ppermute | solution.py:27
  63.8 24.0 %collective-permute-start.10 = (bf16[544,384]{1,0:T(8,128)(2,1)}, bf16[544,384]{1,0:T(8,128)(2,1)S(1)}, u32[]{:S(2)}, u32[]{:S(2)}) collective-permute-start(bf16[544,384]{1,0:T(8,128)(2,1)} %get-tuple-element.95.refs_0_.refs_16_.refs_1_), channel_id=1, source_target_pairs={{0,4},{4,0},{8,12},{12,8},{16,20},{20,16},{24,28},{28,24},{1,5},{5... | collective-permute-start | bytes 1253384 | tf_op jit(solution)/shard_map/ppermute | solution.py:27
  98.7 16.4 %collective-permute-start.18 = (bf16[512,128]{1,0:T(8,128)(2,1)}, bf16[512,128]{1,0:T(8,128)(2,1)S(1)}, u32[]{:S(2)}, u32[]{:S(2)}) collective-permute-start(bf16[512,128]{1,0:T(8,128)(2,1)} %get-tuple-element.96.refs_0_.refs_8_.refs_4_), channel_id=1, source_target_pairs={{0,2},{1,3},{2,0},{3,1},{4,6},{5,7},{6,4},{7,5},{8,10},{9,11},{10,... | collective-permute-start | bytes 393224 | tf_op jit(solution)/shard_map/ppermute | solution.py:27
  124.9 23.0 %collective-permute-start.26 = (bf16[256,1024]{1,0:T(8,128)(2,1)}, bf16[256,1024]{1,0:T(8,128)(2,1)S(1)}, u32[]{:S(2)}, u32[]{:S(2)}) collective-permute-start(bf16[256,1024]{1,0:T(8,128)(2,1)} %get-tuple-element.99.refs_0_), channel_id=1, source_target_pairs={{0,16},{4,20},{8,24},{12,28},{16,0},{20,4},{24,8},{28,12},{1,17},{... | collective-permute-start | bytes 1572872 | tf_op jit(solution)/shard_map/ppermute | solution.py:27
  131.2 21.7 %collective-permute-start.22 = (bf16[256,1024]{1,0:T(8,128)(2,1)}, bf16[256,1024]{1,0:T(8,128)(2,1)S(1)}, u32[]{:S(2)}, u32[]{:S(2)}) collective-permute-start(bf16[256,1024]{1,0:T(8,128)(2,1)} %get-tuple-element.99.refs_0_), channel_id=1, source_target_pairs={{0,8},{4,12},{8,0},{12,4},{16,24},{20,28},{24,16},{28,20},{1,9},{5... | collective-permute-start | bytes 1572872 | tf_op jit(solution)/shard_map/ppermute | solution.py:27
  133.8 19.1 %collective-permute-start.20 = (bf16[256,1024]{1,0:T(8,128)(2,1)}, bf16[256,1024]{1,0:T(8,128)(2,1)S(1)}, u32[]{:S(2)}, u32[]{:S(2)}) collective-permute-start(bf16[256,1024]{1,0:T(8,128)(2,1)} %get-tuple-element.99.refs_0_), channel_id=1, source_target_pairs={{0,4},{4,0},{8,12},{12,8},{16,20},{20,16},{24,28},{28,24},{1,5},{5... | collective-permute-start | bytes 1572872 | tf_op jit(solution)/shard_map/ppermute | solution.py:27
  133.8 25.4 %collective-permute-start.27 = (bf16[256,1024]{1,0:T(8,128)(2,1)}, bf16[256,1024]{1,0:T(8,128)(2,1)S(1)}, u32[]{:S(2)}, u32[]{:S(2)}) collective-permute-start(bf16[256,1024]{1,0:T(8,128)(2,1)} %get-tuple-element.100.refs_1_), channel_id=1, source_target_pairs={{0,16},{4,20},{8,24},{12,28},{16,0},{20,4},{24,8},{28,12},{1,17},{... | collective-permute-start | bytes 1572872 | tf_op jit(solution)/shard_map/ppermute | solution.py:27
  133.9 31.8 %collective-permute-start.23 = (bf16[256,1024]{1,0:T(8,128)(2,1)}, bf16[256,1024]{1,0:T(8,128)(2,1)S(1)}, u32[]{:S(2)}, u32[]{:S(2)}) collective-permute-start(bf16[256,1024]{1,0:T(8,128)(2,1)} %get-tuple-element.100.refs_1_), channel_id=1, source_target_pairs={{0,8},{4,12},{8,0},{12,4},{16,24},{20,28},{24,16},{28,20},{1,9},{5... | collective-permute-start | bytes 1572872 | tf_op jit(solution)/shard_map/ppermute | solution.py:27
  147.9 17.7 %collective-permute-start.21 = (bf16[256,1024]{1,0:T(8,128)(2,1)}, bf16[256,1024]{1,0:T(8,128)(2,1)S(1)}, u32[]{:S(2)}, u32[]{:S(2)}) collective-permute-start(bf16[256,1024]{1,0:T(8,128)(2,1)} %get-tuple-element.100.refs_1_), channel_id=1, source_target_pairs={{0,4},{4,0},{8,12},{12,8},{16,20},{20,16},{24,28},{28,24},{1,5},{5... | collective-permute-start | bytes 1572872 | tf_op jit(solution)/shard_map/ppermute | solution.py:27
  152.9 13.3 %collective-permute-start.28 = (bf16[256,1024]{1,0:T(8,128)(2,1)S(1)}, bf16[256,1024]{1,0:T(8,128)(2,1)S(1)}, u32[]{:S(2)}, u32[]{:S(2)}) collective-permute-start(bf16[256,1024]{1,0:T(8,128)(2,1)S(1)} %collective-permute-done.26.refs_8_), channel_id=1, source_target_pairs={{0,4},{4,0},{8,12},{12,8},{16,20},{20,16},{24,28},{28,24},{1,5},{5... | collective-permute-start | bytes 1572872 | tf_op jit(solution)/shard_map/ppermute | solution.py:27
  152.9 24.6 %collective-permute-start.30 = (bf16[256,1024]{1,0:T(8,128)(2,1)S(1)}, bf16[256,1024]{1,0:T(8,128)(2,1)}, u32[]{:S(2)}, u32[]{:S(2)}) collective-permute-start(bf16[256,1024]{1,0:T(8,128)(2,1)S(1)} %collective-permute-done.22.refs_4_), channel_id=1, source_target_pairs={{0,16},{4,20},{8,24},{12,28},{16,0},{20,4},{24,8},{28,12},{1,17},{... | collective-permute-start | bytes 1572872 | tf_op jit(solution)/shard_map/ppermute | solution.py:27
  159.2 28.6 %collective-permute-start.31 = (bf16[256,1024]{1,0:T(8,128)(2,1)S(1)}, bf16[256,1024]{1,0:T(8,128)(2,1)}, u32[]{:S(2)}, u32[]{:S(2)}) collective-permute-start(bf16[256,1024]{1,0:T(8,128)(2,1)S(1)} %collective-permute-done.27.refs_9_), channel_id=1, source_target_pairs={{0,8},{4,12},{8,0},{12,4},{16,24},{20,28},{24,16},{28,20},{1,9},{5... | collective-permute-start | bytes 1572872 | tf_op jit(solution)/shard_map/ppermute | solution.py:27
  165.6 23.1 %collective-permute-start.24 = (bf16[256,1024]{1,0:T(8,128)(2,1)S(1)}, bf16[256,1024]{1,0:T(8,128)(2,1)}, u32[]{:S(2)}, u32[]{:S(2)}) collective-permute-start(bf16[256,1024]{1,0:T(8,128)(2,1)S(1)} %collective-permute-done.22.refs_4_), channel_id=1, source_target_pairs={{0,4},{4,0},{8,12},{12,8},{16,20},{20,16},{24,28},{28,24},{1,5},{5... | collective-permute-start | bytes 1572872 | tf_op jit(solution)/shard_map/ppermute | solution.py:27
  165.7 23.0 %collective-permute-start.29 = (bf16[256,1024]{1,0:T(8,128)(2,1)S(1)}, bf16[256,1024]{1,0:T(8,128)(2,1)}, u32[]{:S(2)}, u32[]{:S(2)}) collective-permute-start(bf16[256,1024]{1,0:T(8,128)(2,1)S(1)} %collective-permute-done.27.refs_9_), channel_id=1, source_target_pairs={{0,4},{4,0},{8,12},{12,8},{16,20},{20,16},{24,28},{28,24},{1,5},{5... | collective-permute-start | bytes 1572872 | tf_op jit(solution)/shard_map/ppermute | solution.py:27
  166.2 22.5 %collective-permute-start.25 = (bf16[256,1024]{1,0:T(8,128)(2,1)S(1)}, bf16[256,1024]{1,0:T(8,128)(2,1)}, u32[]{:S(2)}, u32[]{:S(2)}) collective-permute-start(bf16[256,1024]{1,0:T(8,128)(2,1)S(1)} %collective-permute-done.23.refs_5_), channel_id=1, source_target_pairs={{0,4},{4,0},{8,12},{12,8},{16,20},{20,16},{24,28},{28,24},{1,5},{5... | collective-permute-start | bytes 1572872 | tf_op jit(solution)/shard_map/ppermute | solution.py:27
  210.8 20.5 %collective-permute-start.35 = (bf16[512,1024]{1,0:T(8,128)(2,1)}, bf16[512,1024]{1,0:T(8,128)(2,1)S(1)}, u32[]{:S(2)}, u32[]{:S(2)}) collective-permute-start(bf16[512,1024]{1,0:T(8,128)(2,1)} %get-tuple-element.104), channel_id=1, source_target_pairs={{0,4},{4,0},{8,12},{12,8},{16,20},{20,16},{24,28},{28,24},{1,5},{5... | collective-permute-start | bytes 3145736 | tf_op jit(solution)/shard_map/ppermute | solution.py:27
  233.8 32.1 %collective-permute-start.46 = (bf16[512,1024]{1,0:T(8,128)(2,1)}, bf16[512,1024]{1,0:T(8,128)(2,1)}, u32[]{:S(2)}, u32[]{:S(2)}) collective-permute-start(bf16[512,1024]{1,0:T(8,128)(2,1)} %get-tuple-element.121), channel_id=1, source_target_pairs={{0,4},{4,0},{8,12},{12,8},{16,20},{20,16},{24,28},{28,24},{1,5},{5... | collective-permute-start | bytes 3145736 | tf_op jit(solution)/shard_map/ppermute | solution.py:27
  235.9 26.9 %collective-permute-start.37 = (bf16[512,1024]{1,0:T(8,128)(2,1)S(1)}, bf16[512,1024]{1,0:T(8,128)(2,1)S(1)}, u32[]{:S(2)}, u32[]{:S(2)}) collective-permute-start(bf16[512,1024]{1,0:T(8,128)(2,1)S(1)} %add_convert_fusion.4.refs_1_.refs_6_), channel_id=1, source_target_pairs={{0,24},{4,28},{8,16},{12,20},{16,8},{20,12},{24,0},{28,4},{1,25},{... | collective-permute-start | bytes 3145736 | tf_op jit(solution)/shard_map/ppermute | solution.py:27
  239.2 45.4 %collective-permute-start.48 = (bf16[512,1024]{1,0:T(8,128)(2,1)S(1)}, bf16[512,1024]{1,0:T(8,128)(2,1)}, u32[]{:S(2)}, u32[]{:S(2)}) collective-permute-start(bf16[512,1024]{1,0:T(8,128)(2,1)S(1)} %add_convert_fusion.1.refs_4_), channel_id=1, source_target_pairs={{0,8},{4,12},{8,0},{12,4},{16,24},{20,28},{24,16},{28,20},{1,9},{5... | collective-permute-start | bytes 3145736 | tf_op jit(solution)/shard_map/ppermute | solution.py:27
  242.1 42.5 %collective-permute-start.50 = (bf16[512,1024]{1,0:T(8,128)(2,1)}, bf16[512,1024]{1,0:T(8,128)(2,1)}, u32[]{:S(2)}, u32[]{:S(2)}) collective-permute-start(bf16[512,1024]{1,0:T(8,128)(2,1)} %add_convert_fusion.refs_5_), channel_id=1, source_target_pairs={{0,16},{4,20},{8,24},{12,28},{16,0},{20,4},{24,8},{28,12},{1,17},{... | collective-permute-start | bytes 3145736 | tf_op jit(solution)/shard_map/ppermute | solution.py:27
  263.9 50.9 %collective-permute-start.38 = (bf16[512,1024]{1,0:T(8,128)(2,1)}, bf16[512,1024]{1,0:T(8,128)(2,1)S(1)}, u32[]{:S(2)}, u32[]{:S(2)}) collective-permute-start(bf16[512,1024]{1,0:T(8,128)(2,1)} %hold.20.refs_12_), channel_id=1, source_target_pairs={{0,8},{4,12},{8,0},{12,4},{16,24},{20,28},{24,16},{28,20},{1,9},{5... | collective-permute-start | bytes 3145736 | tf_op jit(solution)/shard_map/ppermute | solution.py:27
  264.2 50.6 %collective-permute-start.40 = (bf16[512,1024]{1,0:T(8,128)(2,1)}, bf16[512,1024]{1,0:T(8,128)(2,1)S(1)}, u32[]{:S(2)}, u32[]{:S(2)}) collective-permute-start(bf16[512,1024]{1,0:T(8,128)(2,1)} %hold.22.refs_13_), channel_id=1, source_target_pairs={{0,16},{4,20},{8,24},{12,28},{16,0},{20,4},{24,8},{28,12},{1,17},{... | collective-permute-start | bytes 3145736 | tf_op jit(solution)/shard_map/ppermute | solution.py:27
  265.9 63.7 %collective-permute-start.42 = (bf16[512,1024]{1,0:T(8,128)(2,1)}, bf16[512,1024]{1,0:T(8,128)(2,1)}, u32[]{:S(2)}, u32[]{:S(2)}) collective-permute-start(bf16[512,1024]{1,0:T(8,128)(2,1)} %hold.24.refs_14_), channel_id=1, source_target_pairs={{0,24},{4,28},{8,16},{12,20},{16,8},{20,12},{24,0},{28,4},{1,25},{... | collective-permute-start | bytes 3145736 | tf_op jit(solution)/shard_map/ppermute | solution.py:27
  295.1 16.6 %collective-permute-start.52 = (bf16[576,128]{1,0:T(8,128)(2,1)}, bf16[576,128]{1,0:T(8,128)(2,1)S(1)}, u32[]{:S(2)}, u32[]{:S(2)}) collective-permute-start(bf16[576,128]{1,0:T(8,128)(2,1)} %get-tuple-element.133), channel_id=1, source_target_pairs={{0,2},{1,3},{2,0},{3,1},{4,6},{5,7},{6,4},{7,5},{8,10},{9,11},{10,... | collective-permute-start | bytes 442376 | tf_op jit(solution)/shard_map/ppermute | solution.py:27
  329.6 19.4 %collective-permute-start.34 = (bf16[512,1024]{1,0:T(8,128)(2,1)}, bf16[512,1024]{1,0:T(8,128)(2,1)}, u32[]{:S(2)}, u32[]{:S(2)}) collective-permute-start(bf16[512,1024]{1,0:T(8,128)(2,1)} %get-tuple-element.102), channel_id=1, source_target_pairs={{0,4},{4,0},{8,12},{12,8},{16,20},{20,16},{24,28},{28,24},{1,5},{5... | collective-permute-start | bytes 3145736 | tf_op jit(solution)/shard_map/ppermute | solution.py:27
  345.5 18.6 %collective-permute-start.62 = (bf16[320,1024]{1,0:T(8,128)(2,1)}, bf16[320,1024]{1,0:T(8,128)(2,1)S(1)}, u32[]{:S(2)}, u32[]{:S(2)}) collective-permute-start(bf16[320,1024]{1,0:T(8,128)(2,1)} %hold.28), channel_id=1, source_target_pairs={{0,8},{4,12},{8,0},{12,4},{16,24},{20,28},{24,16},{28,20},{1,9},{5... | collective-permute-start | bytes 1966088 | tf_op jit(solution)/shard_map/ppermute | solution.py:27
  346.0 21.7 %collective-permute-start.63 = (bf16[320,1024]{1,0:T(8,128)(2,1)}, bf16[320,1024]{1,0:T(8,128)(2,1)S(1)}, u32[]{:S(2)}, u32[]{:S(2)}) collective-permute-start(bf16[320,1024]{1,0:T(8,128)(2,1)} %hold.29), channel_id=1, source_target_pairs={{0,16},{4,20},{8,24},{12,28},{16,0},{20,4},{24,8},{28,12},{1,17},{... | collective-permute-start | bytes 1966088 | tf_op jit(solution)/shard_map/ppermute | solution.py:27
  347.5 29.4 %collective-permute-start.64 = (bf16[320,1024]{1,0:T(8,128)(2,1)}, bf16[320,1024]{1,0:T(8,128)(2,1)S(1)}, u32[]{:S(2)}, u32[]{:S(2)}) collective-permute-start(bf16[320,1024]{1,0:T(8,128)(2,1)} %hold.30), channel_id=1, source_target_pairs={{0,24},{4,28},{8,16},{12,20},{16,8},{20,12},{24,0},{28,4},{1,25},{... | collective-permute-start | bytes 1966088 | tf_op jit(solution)/shard_map/ppermute | solution.py:27
  353.0 25.6 %collective-permute-start.44 = (bf16[128,1024]{1,0:T(8,128)(2,1)}, bf16[128,1024]{1,0:T(8,128)(2,1)S(1)}, u32[]{:S(2)}, u32[]{:S(2)}) collective-permute-start(bf16[128,1024]{1,0:T(8,128)(2,1)} %get-tuple-element.118), channel_id=1, source_target_pairs={{0,2},{1,3},{2,0},{3,1},{4,6},{5,7},{6,4},{7,5},{8,10},{9,11},{10,... | collective-permute-start | bytes 786440 | tf_op jit(solution)/shard_map/ppermute | solution.py:27
  353.0 25.6 %collective-permute-start.43 = (bf16[128,1024]{1,0:T(8,128)(2,1)}, bf16[128,1024]{1,0:T(8,128)(2,1)}, u32[]{:S(2)}, u32[]{:S(2)}) collective-permute-start(bf16[128,1024]{1,0:T(8,128)(2,1)} %get-tuple-element.117.refs_16_), channel_id=1, source_target_pairs={{0,1},{1,0},{2,3},{3,2},{4,5},{5,4},{6,7},{7,6},{8,9},{9,8},{10,11... | collective-permute-start | bytes 786440 | tf_op jit(solution)/shard_map/ppermute | solution.py:27
  364.1 14.5 %collective-permute-start.45 = (bf16[128,1024]{1,0:T(8,128)(2,1)S(1)}, bf16[128,1024]{1,0:T(8,128)(2,1)S(1)}, u32[]{:S(2)}, u32[]{:S(2)}) collective-permute-start(bf16[128,1024]{1,0:T(8,128)(2,1)S(1)} %copy-done.73), channel_id=1, source_target_pairs={{0,3},{1,2},{2,1},{3,0},{4,7},{5,6},{6,5},{7,4},{8,11},{9,10},{10,... | collective-permute-start | bytes 786440 | tf_op jit(solution)/shard_map/ppermute | solution.py:27
  391.4 14.2 %collective-permute-start.66 = (bf16[80,1024]{1,0:T(8,128)(2,1)S(1)}, bf16[80,1024]{1,0:T(8,128)(2,1)S(1)}, u32[]{:S(2)}, u32[]{:S(2)}) collective-permute-start(bf16[80,1024]{1,0:T(8,128)(2,1)S(1)} %copy-done.48), channel_id=1, source_target_pairs={{0,2},{1,3},{2,0},{3,1},{4,6},{5,7},{6,4},{7,5},{8,10},{9,11},{10,... | collective-permute-start | bytes 491528 | tf_op jit(solution)/shard_map/ppermute | solution.py:27
  391.4 14.2 %collective-permute-start.65 = (bf16[80,1024]{1,0:T(8,128)(2,1)S(1)}, bf16[80,1024]{1,0:T(8,128)(2,1)S(1)}, u32[]{:S(2)}, u32[]{:S(2)}) collective-permute-start(bf16[80,1024]{1,0:T(8,128)(2,1)S(1)} %copy-done.47), channel_id=1, source_target_pairs={{0,1},{1,0},{2,3},{3,2},{4,5},{5,4},{6,7},{7,6},{8,9},{9,8},{10,11... | collective-permute-start | bytes 491528 | tf_op jit(solution)/shard_map/ppermute | solution.py:27
  396.6 12.8 %collective-permute-start.72 = (bf16[128,1024]{1,0:T(8,128)(2,1)}, bf16[128,1024]{1,0:T(8,128)(2,1)}, u32[]{:S(2)}, u32[]{:S(2)}) collective-permute-start(bf16[128,1024]{1,0:T(8,128)(2,1)} %get-tuple-element.161), channel_id=1, source_target_pairs={{0,8},{4,12},{8,0},{12,4},{16,24},{20,28},{24,16},{28,20},{1,9},{5... | collective-permute-start | bytes 786440 | tf_op jit(solution)/shard_map/ppermute | solution.py:27
  398.5 13.5 %collective-permute-start.73 = (bf16[128,1024]{1,0:T(8,128)(2,1)}, bf16[128,1024]{1,0:T(8,128)(2,1)}, u32[]{:S(2)}, u32[]{:S(2)}) collective-permute-start(bf16[128,1024]{1,0:T(8,128)(2,1)} %get-tuple-element.162), channel_id=1, source_target_pairs={{0,16},{4,20},{8,24},{12,28},{16,0},{20,4},{24,8},{28,12},{1,17},{... | collective-permute-start | bytes 786440 | tf_op jit(solution)/shard_map/ppermute | solution.py:27
  399.1 12.9 %collective-permute-start.74 = (bf16[128,1024]{1,0:T(8,128)(2,1)}, bf16[128,1024]{1,0:T(8,128)(2,1)}, u32[]{:S(2)}, u32[]{:S(2)}) collective-permute-start(bf16[128,1024]{1,0:T(8,128)(2,1)} %get-tuple-element.163), channel_id=1, source_target_pairs={{0,24},{4,28},{8,16},{12,20},{16,8},{20,12},{24,0},{28,4},{1,25},{... | collective-permute-start | bytes 786440 | tf_op jit(solution)/shard_map/ppermute | solution.py:27
  406.4 13.2 %collective-permute-start.68 = (bf16[128,1024]{1,0:T(8,128)(2,1)}, bf16[128,1024]{1,0:T(8,128)(2,1)S(1)}, u32[]{:S(2)}, u32[]{:S(2)}) collective-permute-start(bf16[128,1024]{1,0:T(8,128)(2,1)} %hold.31), channel_id=1, source_target_pairs={{0,1},{1,0},{2,3},{3,2},{4,5},{5,4},{6,7},{7,6},{8,9},{9,8},{10,11... | collective-permute-start | bytes 786440 | tf_op jit(solution)/shard_map/ppermute | solution.py:27
  407.3 24.5 %collective-permute-start.69 = (bf16[128,1024]{1,0:T(8,128)(2,1)}, bf16[128,1024]{1,0:T(8,128)(2,1)}, u32[]{:S(2)}, u32[]{:S(2)}) collective-permute-start(bf16[128,1024]{1,0:T(8,128)(2,1)} %hold.32), channel_id=1, source_target_pairs={{0,2},{1,3},{2,0},{3,1},{4,6},{5,7},{6,4},{7,5},{8,10},{9,11},{10,... | collective-permute-start | bytes 786440 | tf_op jit(solution)/shard_map/ppermute | solution.py:27
  409.4 22.4 %collective-permute-start.70 = (bf16[128,1024]{1,0:T(8,128)(2,1)}, bf16[128,1024]{1,0:T(8,128)(2,1)}, u32[]{:S(2)}, u32[]{:S(2)}) collective-permute-start(bf16[128,1024]{1,0:T(8,128)(2,1)} %hold.33), channel_id=1, source_target_pairs={{0,3},{1,2},{2,1},{3,0},{4,7},{5,6},{6,5},{7,4},{8,11},{9,10},{10,... | collective-permute-start | bytes 786440 | tf_op jit(solution)/shard_map/ppermute | solution.py:27
  413.9 24.1 %all-to-all-start.1 = ((bf16[4,32,1024]{2,1,0:T(8,128)(2,1)}), bf16[4,32,1024]{2,1,0:T(8,128)(2,1)S(1)}, u32[]{:S(2)}, u32[]{:S(2)}) async-start(bf16[4,32,1024]{2,1,0:T(8,128)(2,1)} %bitcast.16), calls=%async_computation.1 | async-start | bytes 524288 | tf_op jit(solution)/shard_map/all_to_all | solution.py:1184
  (105 other events, 1037.1 us)
Sparse Core Ops, SparseCore 0:
  10.9 94.7 all-gather.2
  108.6 91.3 all-gather.4
